TPU v7x, 512 devices: a whole 4x4x16 slice. The times are simulated.
512 devices in a mesh: row: 64 (over z, x_lo, core), col: 8 (over y, x_hi).
Axes of the slice: x: 4 (x_hi: 2, x_lo: 2; x = x_hi * 2 + x_lo), y: 4, z: 16, core: 2. Of those that a mesh axis runs over, the one named last changes fastest.
Arguments:
- features: bfloat16 [49152, 512], P(('row', 'col')), may hold values from -6 to 6
- degree: int32 [49152], P(('row', 'col')), may hold values from 1 to 32
- w_self: bfloat16 [512, 512], replicated, may hold values from -0.25 to 0.25
- w_neigh: bfloat16 [512, 512], replicated, may hold values from -0.25 to 0.25
- bias_term: float32 [512], replicated, may hold values from -4 to 4
- tile_index: int32 [64, 8, 72, 3], P('row', 'col'), may hold values from 0 to 64, as said below
- tile_edges: int32 [64, 8, 72, 64], P('row', 'col'), may hold values from 0 to 16383, as said below
- old_grad: bfloat16 [49152, 512], P(('row', 'col')), may hold values from -6 to 6
- old_degree: int32 [49152], P(('row', 'col')), may hold values from 1 to 32
- old_index: int32 [64, 8, 72, 3], P('row', 'col'), may hold values from 0 to 64, as said below
- old_edges: int32 [64, 8, 72, 64], P('row', 'col'), may hold values from 0 to 16383, as said below
Outputs:
- output: bfloat16 [49152, 512], P(('row', 'col'))
- grad_input: bfloat16 [49152, 512], P(('row', 'col'))
Inputs may be any that keep to these rules, and one draw needn't show every extreme that they name: `tile_index`: each slot holds a row block under 6, a column block under 48 and an edge count of 0 to 64; on each device slots with a positive count come first; one device has all 72 slots live; every device has a slot with 64 edges. Row and column blocks may repeat. `tile_edges`: each entry is target * 128 + source inside its tile. `old_index`: as for tile_index. `old_edges`: as for tile_edges.
All inputs are finite; a program needn't handle non-finite values.
Results may differ from a plain program's by a relative error of at most 0.01.
Values may be sent and summed in bfloat16 or wider, within the bound.
No kernel may reach another device: no remote copies, remote signals or barrier semaphores. Data moves between devices by JAX's collectives and lax.ppermute only.
A program may use at most 128 MiB of HBM per device.

v0:
```python
import jax
import jax.numpy as jnp
from jax import lax
from jax.sharding import PartitionSpec as P

TILE = 128


def block_sums(slot_info, slot_edges, sources, rows_total):
    slot_info = slot_info.reshape(-1, 3)
    slot_count = slot_info.shape[0]
    slot_edges = slot_edges.reshape(slot_count, -1)
    feat_width = sources.shape[1]
    col_blocks = sources.reshape(-1, TILE, feat_width)
    row_count = rows_total // TILE
    lane_ids = lax.iota(jnp.int32, TILE)
    row_ids = lax.iota(jnp.int32, row_count)
    edge_ids = lax.iota(jnp.int32, slot_edges.shape[1])

    def add_group(group_idx, running):
        part_tiles = lax.dynamic_slice_in_dim(slot_info, group_idx * 8, 8, 0)
        part_edges = lax.dynamic_slice_in_dim(slot_edges, group_idx * 8, 8, 0)
        is_live = edge_ids[None, :] < part_tiles[:, 2:3]
        dst_hot = ((part_edges // TILE)[:, :, None] == lane_ids) & is_live[:, :, None]
        src_hot = (part_edges % TILE)[:, :, None] == lane_ids
        dense_tile = jnp.einsum(
            "set,seu->stu",
            dst_hot.astype(jnp.bfloat16),
            src_hot.astype(jnp.bfloat16),
            preferred_element_type=jnp.float32,
        ).astype(jnp.bfloat16)
        picked = jnp.take(col_blocks, part_tiles[:, 1], axis=0)
        product = jnp.einsum("stu,suf->stf", dense_tile, picked, preferred_element_type=jnp.float32)
        row_hot = (part_tiles[:, 0][None, :] == row_ids[:, None]).astype(jnp.float32)
        return running + jnp.einsum(
            "rs,stf->rtf", row_hot, product, precision=lax.Precision.HIGHEST
        )

    zero_sum = jnp.zeros((row_count, TILE, feat_width), jnp.float32)
    running = lax.fori_loop(0, slot_count // 8, add_group, zero_sum)
    return running.reshape(rows_total, feat_width)


def shards(
    features,
    degree,
    w_self,
    w_neigh,
    bias_term,
    tile_index,
    tile_edges,
    old_grad,
    old_degree,
    old_index,
    old_edges,
):
    node_count = features.shape[0]
    rows_total = lax.axis_size("col") * node_count
    mean_grad = lax.dot_general(
        old_grad, w_neigh, (((1,), (1,)), ((), ())), preferred_element_type=jnp.float32
    )
    mean_grad = (mean_grad / old_degree[:, None].astype(jnp.float32)).astype(jnp.bfloat16)
    source_feats = lax.all_gather(features, "row", axis=0, tiled=True)
    source_grads = lax.all_gather(mean_grad, "row", axis=0, tiled=True)
    forward_terms = block_sums(tile_index, tile_edges, source_feats, rows_total)
    summed = lax.psum_scatter(
        forward_terms.astype(jnp.bfloat16), "col", scatter_dimension=0, tiled=True
    ).astype(jnp.float32)
    backward_terms = block_sums(old_index, old_edges, source_grads, rows_total)
    old_summed = lax.psum_scatter(
        backward_terms.astype(jnp.bfloat16), "col", scatter_dimension=0, tiled=True
    ).astype(jnp.float32)
    neighbour_mean = (summed / degree[:, None].astype(jnp.float32)).astype(jnp.bfloat16)
    preact = jnp.dot(features, w_self, preferred_element_type=jnp.float32)
    preact = (
        preact + jnp.dot(neighbour_mean, w_neigh, preferred_element_type=jnp.float32) + bias_term
    )
    output = jax.nn.relu(preact).astype(jnp.bfloat16)
    self_grad = lax.dot_general(
        old_grad, w_self, (((1,), (1,)), ((), ())), preferred_element_type=jnp.float32
    )
    grad_input = (self_grad + old_summed).astype(jnp.bfloat16)
    return (output, grad_input)


def solution(mesh):
    in_specs = (
        P(("row", "col"), None),
        P(("row", "col")),
        P(),
        P(),
        P(),
        P("row", "col", None, None),
        P("row", "col", None, None),
        P(("row", "col"), None),
        P(("row", "col")),
        P("row", "col", None, None),
        P("row", "col", None, None),
    )
    out_specs = (P(("row", "col"), None), P(("row", "col"), None))
    return jax.shard_map(shards, mesh=mesh, in_specs=in_specs, out_specs=out_specs, check_vma=False)
```

profile of v0, /device:TPU:6, one launch (start us, length us, event | category | flops | bytes accessed | tf_op | source)
XLA Modules:
  0.0 467.5 jit_solution(996540250998319813)
XLA Ops:
  7.9 2.0 fusion.62
  13.9 128.2 %all-gather.5.cloned.1.call-done = bf16[6144,512]{1,0:T(8,128)(2,1)} async-done(((bf16[96,512]{1,0:T(8,128)(2,1)}), bf16[6144,512]{1,0:T(8,128)(2,1)}) %all-gather.5.cloned.1.call-update) | async-done | bytes 6291472 | tf_op jit(solution)/shard_map/all_gather | solution.py:64
  142.1 106.0 %while.35 = (s32[]{:T(128)}, f32[6,128,512]{2,0,1:T(8,128)}, s32[72,3]{0,1:T(4,128)S(1)}, s32[72,64]{1,0:T(8,128)S(1)}, bf16[48,128,512]{2,1,0:T(8,128)(2,1)}, /*index=5*/s32[]{:T(128)}, s32[]{:T(128)}, s32[]{:T(128)}, s32[]{:T(128)}) while((s32[]{:T(128)}, f32[6,128,512]{2,0,1:T(8,128)}, s32[72,3]{0,1:T(4,128)S(1)}, ...), condition=%wide.region_4.6_spmd.clone.clone, body=%wide.region_3.5_spmd.clone.clone.sunk | while | flops 190396512 | bytes 10504881 | solution.py:40
  142.2 4.4 gather_fusion.1
  146.7 2.1 fusion.93
  148.8 3.6 select_add_fusion.5
  152.5 4.4 gather_fusion.1
  157.0 2.1 fusion.93
  159.1 5.2 %select_add_fusion.5 = f32[6,128,512]{2,0,1:T(8,128)} fusion(f32[6,128,512]{2,0,1:T(8,128)} %get-tuple-element.656, f32[8,128,512]{2,1,0:T(8,128)S(1)} %fusion.93, pred[]{:T(512)S(6)} %compare.29, s32[8]{0:T(128)S(1)} %get-tuple-element.618), kind=kOutput, calls=%fused_computation.43.clone.1 | convolution fusion | flops 38535216 | bytes 5242913 | tf_op jit(solution)/shard_map/while/body/eval_jaxpr/rs,stf->rtf/dot_general | solution.py:35
  164.5 4.4 gather_fusion.1
  169.0 2.1 fusion.93
  171.1 5.2 %select_add_fusion.5 = f32[6,128,512]{2,0,1:T(8,128)} fusion(f32[6,128,512]{2,0,1:T(8,128)} %get-tuple-element.656, f32[8,128,512]{2,1,0:T(8,128)S(1)} %fusion.93, pred[]{:T(512)S(6)} %compare.29, s32[8]{0:T(128)S(1)} %get-tuple-element.618), kind=kOutput, calls=%fused_computation.43.clone.1 | convolution fusion | flops 38535216 | bytes 5242913 | tf_op jit(solution)/shard_map/while/body/eval_jaxpr/rs,stf->rtf/dot_general | solution.py:35
  176.4 4.4 gather_fusion.1
  180.9 2.1 fusion.93
  183.0 5.2 %select_add_fusion.5 = f32[6,128,512]{2,0,1:T(8,128)} fusion(f32[6,128,512]{2,0,1:T(8,128)} %get-tuple-element.656, f32[8,128,512]{2,1,0:T(8,128)S(1)} %fusion.93, pred[]{:T(512)S(6)} %compare.29, s32[8]{0:T(128)S(1)} %get-tuple-element.618), kind=kOutput, calls=%fused_computation.43.clone.1 | convolution fusion | flops 38535216 | bytes 5242913 | tf_op jit(solution)/shard_map/while/body/eval_jaxpr/rs,stf->rtf/dot_general | solution.py:35
  188.4 4.4 gather_fusion.1
  192.9 2.1 fusion.93
  195.0 5.2 %select_add_fusion.5 = f32[6,128,512]{2,0,1:T(8,128)} fusion(f32[6,128,512]{2,0,1:T(8,128)} %get-tuple-element.656, f32[8,128,512]{2,1,0:T(8,128)S(1)} %fusion.93, pred[]{:T(512)S(6)} %compare.29, s32[8]{0:T(128)S(1)} %get-tuple-element.618), kind=kOutput, calls=%fused_computation.43.clone.1 | convolution fusion | flops 38535216 | bytes 5242913 | tf_op jit(solution)/shard_map/while/body/eval_jaxpr/rs,stf->rtf/dot_general | solution.py:35
  200.3 4.4 gather_fusion.1
  204.8 2.1 fusion.93
  206.9 5.2 %select_add_fusion.5 = f32[6,128,512]{2,0,1:T(8,128)} fusion(f32[6,128,512]{2,0,1:T(8,128)} %get-tuple-element.656, f32[8,128,512]{2,1,0:T(8,128)S(1)} %fusion.93, pred[]{:T(512)S(6)} %compare.29, s32[8]{0:T(128)S(1)} %get-tuple-element.618), kind=kOutput, calls=%fused_computation.43.clone.1 | convolution fusion | flops 38535216 | bytes 5242913 | tf_op jit(solution)/shard_map/while/body/eval_jaxpr/rs,stf->rtf/dot_general | solution.py:35
  212.3 4.4 gather_fusion.1
  216.8 2.1 fusion.93
  218.9 5.2 %select_add_fusion.5 = f32[6,128,512]{2,0,1:T(8,128)} fusion(f32[6,128,512]{2,0,1:T(8,128)} %get-tuple-element.656, f32[8,128,512]{2,1,0:T(8,128)S(1)} %fusion.93, pred[]{:T(512)S(6)} %compare.29, s32[8]{0:T(128)S(1)} %get-tuple-element.618), kind=kOutput, calls=%fused_computation.43.clone.1 | convolution fusion | flops 38535216 | bytes 5242913 | tf_op jit(solution)/shard_map/while/body/eval_jaxpr/rs,stf->rtf/dot_general | solution.py:35
  224.2 4.4 gather_fusion.1
  228.7 2.1 fusion.93
  230.8 5.2 %select_add_fusion.5 = f32[6,128,512]{2,0,1:T(8,128)} fusion(f32[6,128,512]{2,0,1:T(8,128)} %get-tuple-element.656, f32[8,128,512]{2,1,0:T(8,128)S(1)} %fusion.93, pred[]{:T(512)S(6)} %compare.29, s32[8]{0:T(128)S(1)} %get-tuple-element.618), kind=kOutput, calls=%fused_computation.43.clone.1 | convolution fusion | flops 38535216 | bytes 5242913 | tf_op jit(solution)/shard_map/while/body/eval_jaxpr/rs,stf->rtf/dot_general | solution.py:35
  236.2 4.4 gather_fusion.1
  240.7 2.1 fusion.93
  242.8 5.2 %select_add_fusion.5 = f32[6,128,512]{2,0,1:T(8,128)} fusion(f32[6,128,512]{2,0,1:T(8,128)} %get-tuple-element.656, f32[8,128,512]{2,1,0:T(8,128)S(1)} %fusion.93, pred[]{:T(512)S(6)} %compare.29, s32[8]{0:T(128)S(1)} %get-tuple-element.618), kind=kOutput, calls=%fused_computation.43.clone.1 | convolution fusion | flops 38535216 | bytes 5242913 | tf_op jit(solution)/shard_map/while/body/eval_jaxpr/rs,stf->rtf/dot_general | solution.py:35
  248.0 1.8 convert_element_type.84
  251.0 16.5 %all-gather.3.cloned.1.call-done = bf16[6144,512]{1,0:T(8,128)(2,1)} async-done(((bf16[96,512]{1,0:T(8,128)(2,1)}), bf16[6144,512]{1,0:T(8,128)(2,1)}) %all-gather.3.cloned.1.call-update) | async-done | bytes 6291472 | tf_op jit(solution)/shard_map/all_gather | solution.py:63
  267.6 106.0 %while.34 = (s32[]{:T(128)}, f32[6,128,512]{2,0,1:T(8,128)}, s32[72,3]{0,1:T(4,128)S(1)}, s32[72,64]{1,0:T(8,128)S(1)}, bf16[48,128,512]{2,1,0:T(8,128)(2,1)}, /*index=5*/s32[]{:T(128)}, s32[]{:T(128)}, s32[]{:T(128)}, s32[]{:T(128)}) while((s32[]{:T(128)}, f32[6,128,512]{2,0,1:T(8,128)}, s32[72,3]{0,1:T(4,128)S(1)}, ...), condition=%wide.region_1.3_spmd.clone.clone, body=%wide.region_0.2_spmd.clone.clone.sunk | while | flops 190396512 | bytes 10504881 | solution.py:40
  267.7 4.4 gather_fusion
  272.2 2.1 fusion.88
  274.2 3.7 select_add_fusion.4
  278.0 4.4 gather_fusion
  282.5 2.1 fusion.88
  284.6 5.3 %select_add_fusion.4 = f32[6,128,512]{2,0,1:T(8,128)} fusion(f32[6,128,512]{2,0,1:T(8,128)} %get-tuple-element.629, f32[8,128,512]{2,1,0:T(8,128)S(1)} %fusion.88, pred[]{:T(512)S(6)} %compare.28, s32[8]{0:T(128)S(1)} %get-tuple-element.607), kind=kOutput, calls=%fused_computation.10.clone.1 | convolution fusion | flops 38535216 | bytes 5242913 | tf_op jit(solution)/shard_map/while/body/eval_jaxpr/rs,stf->rtf/dot_general | solution.py:35
  290.0 4.4 gather_fusion
  294.5 2.1 fusion.88
  296.6 5.3 %select_add_fusion.4 = f32[6,128,512]{2,0,1:T(8,128)} fusion(f32[6,128,512]{2,0,1:T(8,128)} %get-tuple-element.629, f32[8,128,512]{2,1,0:T(8,128)S(1)} %fusion.88, pred[]{:T(512)S(6)} %compare.28, s32[8]{0:T(128)S(1)} %get-tuple-element.607), kind=kOutput, calls=%fused_computation.10.clone.1 | convolution fusion | flops 38535216 | bytes 5242913 | tf_op jit(solution)/shard_map/while/body/eval_jaxpr/rs,stf->rtf/dot_general | solution.py:35
  302.0 4.4 gather_fusion
  306.5 2.1 fusion.88
  308.6 5.3 %select_add_fusion.4 = f32[6,128,512]{2,0,1:T(8,128)} fusion(f32[6,128,512]{2,0,1:T(8,128)} %get-tuple-element.629, f32[8,128,512]{2,1,0:T(8,128)S(1)} %fusion.88, pred[]{:T(512)S(6)} %compare.28, s32[8]{0:T(128)S(1)} %get-tuple-element.607), kind=kOutput, calls=%fused_computation.10.clone.1 | convolution fusion | flops 38535216 | bytes 5242913 | tf_op jit(solution)/shard_map/while/body/eval_jaxpr/rs,stf->rtf/dot_general | solution.py:35
  314.0 4.4 gather_fusion
  318.5 2.1 fusion.88
  320.6 5.3 %select_add_fusion.4 = f32[6,128,512]{2,0,1:T(8,128)} fusion(f32[6,128,512]{2,0,1:T(8,128)} %get-tuple-element.629, f32[8,128,512]{2,1,0:T(8,128)S(1)} %fusion.88, pred[]{:T(512)S(6)} %compare.28, s32[8]{0:T(128)S(1)} %get-tuple-element.607), kind=kOutput, calls=%fused_computation.10.clone.1 | convolution fusion | flops 38535216 | bytes 5242913 | tf_op jit(solution)/shard_map/while/body/eval_jaxpr/rs,stf->rtf/dot_general | solution.py:35
  325.9 4.4 gather_fusion
  330.4 2.1 fusion.88
  332.5 5.3 %select_add_fusion.4 = f32[6,128,512]{2,0,1:T(8,128)} fusion(f32[6,128,512]{2,0,1:T(8,128)} %get-tuple-element.629, f32[8,128,512]{2,1,0:T(8,128)S(1)} %fusion.88, pred[]{:T(512)S(6)} %compare.28, s32[8]{0:T(128)S(1)} %get-tuple-element.607), kind=kOutput, calls=%fused_computation.10.clone.1 | convolution fusion | flops 38535216 | bytes 5242913 | tf_op jit(solution)/shard_map/while/body/eval_jaxpr/rs,stf->rtf/dot_general | solution.py:35
  337.9 4.4 gather_fusion
  342.3 2.1 fusion.88
  344.4 5.3 %select_add_fusion.4 = f32[6,128,512]{2,0,1:T(8,128)} fusion(f32[6,128,512]{2,0,1:T(8,128)} %get-tuple-element.629, f32[8,128,512]{2,1,0:T(8,128)S(1)} %fusion.88, pred[]{:T(512)S(6)} %compare.28, s32[8]{0:T(128)S(1)} %get-tuple-element.607), kind=kOutput, calls=%fused_computation.10.clone.1 | convolution fusion | flops 38535216 | bytes 5242913 | tf_op jit(solution)/shard_map/while/body/eval_jaxpr/rs,stf->rtf/dot_general | solution.py:35
  349.8 4.4 gather_fusion
  354.3 2.1 fusion.88
  356.4 5.3 %select_add_fusion.4 = f32[6,128,512]{2,0,1:T(8,128)} fusion(f32[6,128,512]{2,0,1:T(8,128)} %get-tuple-element.629, f32[8,128,512]{2,1,0:T(8,128)S(1)} %fusion.88, pred[]{:T(512)S(6)} %compare.28, s32[8]{0:T(128)S(1)} %get-tuple-element.607), kind=kOutput, calls=%fused_computation.10.clone.1 | convolution fusion | flops 38535216 | bytes 5242913 | tf_op jit(solution)/shard_map/while/body/eval_jaxpr/rs,stf->rtf/dot_general | solution.py:35
  361.7 4.4 gather_fusion
  366.2 2.1 fusion.88
  368.3 5.3 %select_add_fusion.4 = f32[6,128,512]{2,0,1:T(8,128)} fusion(f32[6,128,512]{2,0,1:T(8,128)} %get-tuple-element.629, f32[8,128,512]{2,1,0:T(8,128)S(1)} %fusion.88, pred[]{:T(512)S(6)} %compare.28, s32[8]{0:T(128)S(1)} %get-tuple-element.607), kind=kOutput, calls=%fused_computation.10.clone.1 | convolution fusion | flops 38535216 | bytes 5242913 | tf_op jit(solution)/shard_map/while/body/eval_jaxpr/rs,stf->rtf/dot_general | solution.py:35
  373.6 3.4 copy.35
  377.3 1.8 fusion.61
  379.2 80.0 %reduce-scatter.3.cloned.1.call-done = bf16[96,512]{1,0:T(8,128)(2,1)} async-done(((bf16[768,512]{1,0:T(8,128)(2,1)}), bf16[96,512]{1,0:T(8,128)(2,1)}) %reduce-scatter.3.cloned.1.call-update) | async-done | bytes 98320 | tf_op jit(solution)/shard_map/reduce_scatter | solution.py:66
  459.2 1.8 fusion.60
  (157 shorter events, 9.7 us)
Async XLA Ops:
  7.2 369.9 %copy-start = (bf16[512,512]{1,0:T(8,128)(2,1)S(1)}, bf16[512,512]{1,0:T(8,128)(2,1)}, u32[]{:S(2)}) copy-start(bf16[512,512]{1,0:T(8,128)(2,1)} %param.19) | copy-start | bytes 1572868
  7.2 134.9 %all-gather.5.cloned.1.call-start = ((), (), s32[]{:S(2)}) async-start(), calls=%async_computation.4 | async-start | bytes 6389760 | tf_op jit(solution)/shard_map/all_gather | solution.py:64
  10.0 257.6 %all-gather.3.cloned.1.call-start = ((), (), s32[]{:S(2)}) async-start(), calls=%async_computation.2 | async-start | bytes 6389760 | tf_op jit(solution)/shard_map/all_gather | solution.py:63
  10.7 366.6 %reduce-scatter.5.cloned.1.call-start = ((), (), s32[]{:S(2)}) async-start(), calls=%async_computation.5 | async-start | bytes 884736 | tf_op jit(solution)/shard_map/reduce_scatter | solution.py:70
  251.0 208.2 %reduce-scatter.3.cloned.1.call-start = ((), (), s32[]{:S(2)}) async-start(), calls=%async_computation.3 | async-start | bytes 884736 | tf_op jit(solution)/shard_map/reduce_scatter | solution.py:66
  373.5 3.5 copy-start.5
  373.5 3.5 copy-start.1
  373.5 3.8 copy-start.2
  373.6 85.6 %copy-start.3 = (bf16[512,512]{1,0:T(8,128)(2,1)S(1)}, bf16[512,512]{1,0:T(8,128)(2,1)}, u32[]{:S(2)}) copy-start(bf16[512,512]{1,0:T(8,128)(2,1)} %param.20) | copy-start | bytes 1572868
  373.6 85.6 %copy-start.4 = (f32[512]{0:T(512)S(1)}, f32[512]{0:T(512)}, u32[]{:S(2)}) copy-start(f32[512]{0:T(512)} %param.21) | copy-start | bytes 6148
Sparse Core Ops, SparseCore 0:
  10.7 131.2 all-gather.4
  144.2 123.2 all-gather.2
  272.0 82.0 reduce-scatter.4
  377.1 81.9 reduce-scatter.2
where the time goes:
time: 470 us; the launch traced here: 468 us
  waiting for transfers between devices  226 us (48%)
  matrix products  135 us (29%)
  local copies, waits for them, and re-layouts  88.3 us (19%)
  between operations  13.9 us (3%)
    all_gather x1, waiting for transfers between devices, shards(): source_grads = lax.all_gather(mean_grad, 'row', axis=0, tiled=True)  128 us
    dot_general x18, matrix products, add_group(): jnp.einsum('rs,stf->rtf', row_hot, product, precision=lax.Precision.HIGHEST)  91.2 us
    reduce_scatter x1, waiting for transfers between devices, shards(): lax.psum_scatter(forward_terms.astype(jnp.bfloat16), 'col', scatter_dimen...  80 us
    gather x18, local copies, waits for them, and re-layouts, add_group(): picked = jnp.take(col_blocks, part_tiles[:, 1], axis=0)  79.2 us
    dot_general x18, matrix products, add_group(): jnp.einsum('stu,suf->stf', dense_tile, picked, preferred_element_type=jnp...  37.5 us
    all_gather x1, waiting for transfers between devices, shards(): source_feats = lax.all_gather(features, 'row', axis=0, tiled=True)  16.5 us
  transfers between devices with their start and end apart: 4, of which 3 were waited for; matrix products, arithmetic and copies ran while one was open for 48% of the time, Pallas kernels for 0%

commit v1 on v0

v1 whole, which is shorter than its diff:
```python
import jax
import jax.numpy as jnp
from jax import lax
from jax.experimental import pallas as pl
from jax.experimental.pallas import tpu as pltpu
from jax.sharding import Mesh
from jax.sharding import PartitionSpec as P

TILE = 128
GROUP = 4
MIB = 1024 * 1024
PARTS = ("z", "xl", "core", "y", "xh")
PLANE = ("xl", "y", "xh")
SHIFTS = (64, 32, 16, 8, 4, 2)


def count_kernel(live_ref, place_ref, dst_ref, src_ref, out_ref, total):
    half = pl.program_id(0)
    total[...] = jnp.zeros_like(total)
    lane_ids = lax.broadcasted_iota(jnp.int32, (TILE, dst_ref.shape[2]), 0)

    def add_group(step, carry):
        slots = [step * GROUP + offset for offset in range(GROUP)]
        counts = []
        for slot in slots:
            dst_hot = (lane_ids == dst_ref[0, pl.ds(slot, 1), :]).astype(jnp.bfloat16)
            src_hot = (lane_ids == src_ref[0, pl.ds(slot, 1), :]).astype(jnp.bfloat16)
            counts.append(
                lax.dot_general(
                    dst_hot, src_hot, (((1,), (1,)), ((), ())), preferred_element_type=jnp.float32
                )
            )
        for slot, count in zip(slots, counts):
            rows = pl.ds(pl.multiple_of(place_ref[half, 0, slot] * TILE, TILE), TILE)
            total[place_ref[half, 1, slot], rows, :] += count
        return carry

    lax.fori_loop(0, pl.cdiv(live_ref[half], GROUP), add_group, 0)
    for block in range(total.shape[0]):
        out_ref[:, block * TILE : (block + 1) * TILE] = total[block].astype(jnp.bfloat16)


def edge_counts(live, place, dst, src, rows, depth):
    halves, slots, width = dst.shape
    blocks = depth // TILE
    return pl.pallas_call(
        count_kernel,
        out_shape=jax.ShapeDtypeStruct((halves * rows, depth), jnp.bfloat16),
        grid_spec=pltpu.PrefetchScalarGridSpec(
            num_scalar_prefetch=2,
            grid=(halves,),
            in_specs=[pl.BlockSpec((1, slots, width), lambda h, *_: (h, 0, 0))] * 2,
            out_specs=pl.BlockSpec((rows, depth), lambda h, *_: (h, 0)),
            scratch_shapes=[pltpu.VMEM((blocks, rows, TILE), jnp.float32)],
        ),
        compiler_params=pltpu.CompilerParams(vmem_limit_bytes=40 * MIB),
        cost_estimate=pl.CostEstimate(
            flops=2 * 10**9, bytes_accessed=40 * 10**6, transcendentals=0
        ),
    )(live, place, dst, src)


def product_kernel(place_ref, counts_ref, sources_ref, out_ref, held):
    @pl.when(pl.program_id(0) == 0)
    def _():
        planes = sources_ref.shape[0]
        wide = pl.ds(pl.multiple_of(place_ref[0], TILE // 2), TILE)
        narrow = pl.ds(pl.multiple_of(place_ref[1], TILE // 2), TILE // 2)
        for z in range(planes):
            held[z * TILE : (z + 1) * TILE] = sources_ref[z, wide]
            begin = planes * TILE + z * TILE // 2
            held[begin : begin + TILE // 2] = sources_ref[z, narrow]

    out_ref[...] = jnp.dot(
        counts_ref[...], held[...], preferred_element_type=jnp.float32
    ).astype(jnp.bfloat16)


def edge_products(place, counts, sources, chunk=512):
    rows, depth = counts.shape
    planes, height, width = sources.shape
    return pl.pallas_call(
        product_kernel,
        out_shape=jax.ShapeDtypeStruct((rows, width), jnp.bfloat16),
        grid_spec=pltpu.PrefetchScalarGridSpec(
            num_scalar_prefetch=1,
            grid=(rows // chunk,),
            in_specs=[
                pl.BlockSpec((chunk, depth), lambda m, *_: (m, 0)),
                pl.BlockSpec((planes, height, width), lambda m, *_: (0, 0, 0)),
            ],
            out_specs=pl.BlockSpec((chunk, width), lambda m, *_: (m, 0)),
            scratch_shapes=[pltpu.VMEM((depth, width), jnp.bfloat16)],
        ),
        compiler_params=pltpu.CompilerParams(vmem_limit_bytes=40 * MIB),
        cost_estimate=pl.CostEstimate(
            flops=2 * rows * depth * width, bytes_accessed=30 * 10**6, transcendentals=0
        ),
    )(place, counts, sources)


def slot_plan(index, edges, lane, planes):
    plane, part = index[..., 1] // 3, index[..., 1] % 3
    whole = part == 2 * lane
    source = edges % TILE
    own = whole[..., None] | ((part == 1)[..., None] & (source // (TILE // 2) == lane))
    own &= lax.iota(jnp.int32, edges.shape[-1]) < index[..., 2:3]
    in_half = source % (TILE // 2) + (plane % 2)[..., None] * (TILE // 2)
    src = jnp.where(own, jnp.where(whole[..., None], source, in_half), -1)
    block = jnp.where(whole, plane, planes + plane // 2)
    live = jnp.sum((index[..., 2] > 0).astype(jnp.int32), axis=-1)
    place = jnp.stack([index[..., 0], block], axis=-2)
    return live, place, edges // TILE, src


def gather_scaled(values):
    top = jnp.max(jnp.abs(values)).astype(jnp.float32)
    scale = jnp.float32(1)
    flags = []
    for shift in SHIFTS:
        fits = top * 2.0**shift <= 2.0**15
        top = jnp.where(fits, top * 2.0**shift, top)
        scale = jnp.where(fits, scale * 2.0**shift, scale)
        flags.append(fits.astype(jnp.float16))
    nodes, width = values.shape
    lane_ids = lax.broadcasted_iota(jnp.int32, (8, width), 1)
    tail = jnp.zeros((8, width), jnp.float16)
    for place, flag in enumerate(flags):
        tail = jnp.where(lane_ids == place, flag, tail)
    sent = (values.astype(jnp.float32) * scale).astype(jnp.float16)
    sent = jnp.concatenate([sent, tail], axis=0)
    got = lax.all_gather(sent, ("z", "core"), axis=0, tiled=False)
    undo = jnp.ones((got.shape[0], 1, 1), jnp.float32)
    for place, shift in enumerate(SHIFTS):
        undo = undo * jnp.where(got[:, nodes : nodes + 1, place : place + 1] > 0, 2.0**-shift, 1.0)
    got = (got[:, :nodes].astype(jnp.float32) * undo).astype(jnp.bfloat16)
    return got.reshape(-1, 2 * nodes, width)


def shards(
    features,
    degree,
    w_self,
    w_neigh,
    bias_term,
    tile_index,
    tile_edges,
    old_grad,
    old_degree,
    old_index,
    old_edges,
):
    nodes, width = features.shape
    planes = lax.axis_size("z")
    depth = 2 * planes * nodes
    rows = lax.axis_size("y") * lax.axis_size("xh") * nodes
    lane = lax.axis_index("xl")

    all_features = lax.all_gather(features, ("z", "core"), axis=0, tiled=True)
    all_features = all_features.reshape(planes, 2 * nodes, width)

    mean_grad = lax.dot_general(
        old_grad, w_neigh, (((1,), (1,)), ((), ())), preferred_element_type=jnp.float32
    )
    mean_grad = (mean_grad / old_degree[:, None].astype(jnp.float32)).astype(jnp.bfloat16)

    own_slots = jnp.stack(
        [
            jnp.concatenate([tile_index[0, 0], tile_edges[0, 0]], axis=1),
            jnp.concatenate([old_index[0, 0], old_edges[0, 0]], axis=1),
        ]
    )
    other_slots = lax.ppermute(own_slots, "xl", [(0, 1), (1, 0)])
    pair = jnp.stack(
        [
            jnp.where(lane == 0, own_slots, other_slots),
            jnp.where(lane == 0, other_slots, own_slots),
        ],
        axis=1,
    )
    place = jnp.stack([lane * (TILE // 2), (1 - lane) * TILE])
    new_plan = slot_plan(pair[0, :, :, :3], pair[0, :, :, 3:], lane, planes)
    old_plan = slot_plan(pair[1, :, :, :3], pair[1, :, :, 3:], lane, planes)

    all_grads = gather_scaled(mean_grad)

    def partial_sums(plan, sources):
        counts = edge_counts(*plan, rows, depth)
        partial = edge_products(place, counts, sources)
        return lax.all_to_all(partial.reshape(-1, nodes, width), PLANE, 0, 0)

    old_parts = partial_sums(old_plan, all_grads)
    new_parts = partial_sums(new_plan, all_features)

    old_summed = jnp.sum(old_parts.astype(jnp.float32), axis=0)
    self_grad = lax.dot_general(
        old_grad, w_self, (((1,), (1,)), ((), ())), preferred_element_type=jnp.float32
    )
    grad_input = (self_grad + old_summed).astype(jnp.bfloat16)

    summed = jnp.sum(new_parts.astype(jnp.float32), axis=0)
    neighbour_mean = (summed / degree[:, None].astype(jnp.float32)).astype(jnp.bfloat16)
    preact = jnp.dot(features, w_self, preferred_element_type=jnp.float32) + bias_term
    preact = preact + jnp.dot(neighbour_mean, w_neigh, preferred_element_type=jnp.float32)
    output = jax.nn.relu(preact).astype(jnp.bfloat16)
    return (output, grad_input)


def solution(mesh):
    devices = mesh.devices.reshape(16, 2, 2, 4, 2)
    parts = Mesh(devices, PARTS)
    block = ("z", "xl", "core")
    side = ("y", "xh")
    in_specs = (
        P(PARTS, None),
        P(PARTS),
        P(),
        P(),
        P(),
        P(block, side, None, None),
        P(block, side, None, None),
        P(PARTS, None),
        P(PARTS),
        P(block, side, None, None),
        P(block, side, None, None),
    )
    out_specs = (P(PARTS, None), P(PARTS, None))
    return jax.shard_map(
        shards, mesh=parts, in_specs=in_specs, out_specs=out_specs, check_vma=False
    )
```

time: 470 us -> 182 us (0.39)
  the two profiles are of different devices: /device:TPU:6 before, /device:TPU:33 now
where the time goes in v1:
time: 182 us; the launch traced here: 181 us
  blocking collectives  52 us (29%)
  Pallas kernels  26.6 us (15%)
  starting transfers between devices  25.4 us (14%)
  waiting for transfers between devices  25.3 us (14%)
  local copies, waits for them, and re-layouts  22.3 us (12%)
  between operations  15.7 us (9%)
  other arithmetic  9.8 us (5%)
  matrix products  3.89 us (2%)
    all_gather x1, blocking collectives, gather_scaled(): got = lax.all_gather(sent, ('z', 'core'), axis=0, tiled=False)  52 us
    all_to_all x2, waiting for transfers between devices, partial_sums(): return lax.all_to_all(partial.reshape(-1, nodes, width), PLANE, 0, 0)  25.3 us
    all_to_all x2, starting transfers between devices, partial_sums(): return lax.all_to_all(partial.reshape(-1, nodes, width), PLANE, 0, 0)  22.2 us
    unnamed x36, local copies, waits for them, and re-layouts  22.1 us
    pallas_call x2, Pallas kernels, edge_products(): pl.pallas_call(product_kernel, out_shape=jax.ShapeDtypeStruct((rows, widt...  13.9 us
    pallas_call x2, Pallas kernels, edge_counts(): pl.pallas_call(count_kernel, out_shape=jax.ShapeDtypeStruct((halves * row...  12.7 us
    convert_element_type x1, other arithmetic, gather_scaled(): got = (got[:, :nodes].astype(jnp.float32) * undo).astype(jnp.bfloat16)  4.91 us
  transfers between devices with their start and end apart: 4, of which 1 were waited for; matrix products, arithmetic and copies ran while one was open for 7% of the time, Pallas kernels for 15%

profile of v1, /device:TPU:33, one launch (start us, length us, event | category | flops | bytes accessed | tf_op | source)
XLA Modules:
  0.0 181.1 jit_solution(18399238858518311371)
XLA Ops:
  7.2 0.0 copy-start
  7.2 0.0 all-gather.4.cloned.1.call-start
  7.2 0.8 copy.122
  8.0 0.8 copy.123
  8.9 0.8 copy.124
  9.7 0.8 copy.125
  10.5 0.1 add_bitcast_fusion
  10.6 3.1 %collective-permute-start = (s32[2,72,67]{2,1,0:T(8,128)S(1)}, s32[2,72,67]{2,1,0:T(8,128)S(1)}, u32[]{:S(2)}, u32[]{:S(2)}) collective-permute-start(s32[2,72,67]{2,1,0:T(8,128)S(1)} %pad_add_fusion.1), channel_id=1, source_target_pairs={{0,16},{16,0},{1,17},{17,1},{2,18},{18,2},{3,19},{19,3},{4,20},{20... | collective-permute-start | bytes 115784 | tf_op jit(solution)/shard_map/ppermute | solution.py:173
  13.7 0.0 all-gather.4.cloned.1.call-update
  13.8 0.7 convert_element_type.71
  14.4 0.0 copy-done
  14.4 1.8 abs_reduce_fusion
  17.8 52.0 %all-gather.5 = f16[3328,512]{1,0:T(8,128)(2,1)S(1)} all-gather(f16[104,512]{1,0:T(8,128)(2,1)S(1)} %pad_maximum_fusion), channel_id=2, replica_groups=mesh['z'=16,'xl'=2,'core'=2,'y'=4,'xh'=2] {'z','core'}, dimensions={0}, use_global_device_ids=true | all-gather | bytes 3514368 | tf_op jit(solution)/shard_map/all_gather | solution.py:132
  69.8 0.0 copy-start.7
  69.8 1.7 copy-done.7
  71.5 0.2 fusion.55
  71.8 0.1 copy.149
  71.9 0.1 copy.150
  72.0 0.1 copy.151
  72.1 0.1 copy.152
  72.2 0.1 copy.153
  72.3 0.1 copy.154
  72.4 4.9 %multiply_convert_fusion = bf16[32,96,512]{2,1,0:T(8,128)(2,1)} fusion(f16[32,104,512]{2,1,0:T(8,128)(2,1)} %bitcast.75, f32[32]{0:T(128)S(1)} %fusion.50), kind=kLoop, calls=%fused_computation | loop fusion | flops 4718592 | bytes 6291584 | tf_op jit(solution)/shard_map/convert_element_type | solution.py:136
  77.3 0.1 pad_add_fusion.4.place_ref
  77.4 0.0 collective-permute-done
  77.4 0.3 compare_reduce_fusion.1
  77.7 0.4 fusion.18
  78.1 0.1 fusion.44.live_ref
  78.2 0.3 compare_reduce_fusion.3
  78.5 0.4 fusion.11
  78.9 0.4 fusion.15
  79.3 0.0 copy-start.5
  79.3 6.6 %shard_map.124.counts_ref = bf16[1536,3072]{1,0:T(8,128)(2,1)S(1)} custom-call(s32[2]{0:T(128)S(1)} %fusion.44.live_ref, s32[2,2,72]{2,1,0:T(2,128)S(1)} %pad_add_fusion.3.place_ref, s32[2,72,64]{2,1,0:T(8,128)S(1)} %get-tuple-element.30.dst_ref, s32[2,72,64]{2,1,0:T(8,128)S(1)} %get-tuple-element.28.src_ref), custom_call_target="tpu_custom_call" | custom-call | flops 2000000000 | bytes 40000000 | tf_op jit(solution)/shard_map/pallas_call | solution.py:46
  85.9 0.0 copy-start.3
  85.9 3.6 %copy-done.3 = bf16[1536,3072]{1,0:T(8,128)(2,1)} copy-done((bf16[1536,3072]{1,0:T(8,128)(2,1)}, bf16[1536,3072]{1,0:T(8,128)(2,1)S(1)}, u32[]{:S(2)}) %copy-start.3) | copy-done | bytes 9437208
  89.5 0.0 copy-done.5
  89.5 0.0 copy-start.4
  89.5 3.7 %copy-done.4 = bf16[1536,3072]{1,0:T(8,128)(2,1)S(1)} copy-done((bf16[1536,3072]{1,0:T(8,128)(2,1)S(1)}, bf16[1536,3072]{1,0:T(8,128)(2,1)}, u32[]{:S(2)}) %copy-start.4) | copy-done | bytes 9437208
  93.2 6.9 %shard_map.125 = bf16[1536,512]{1,0:T(8,128)(2,1)} custom-call(s32[2]{0:T(128)S(1)} %pad_add_fusion.4.place_ref, bf16[1536,3072]{1,0:T(8,128)(2,1)S(1)} %copy-done.4, bf16[16,192,512]{2,1,0:T(8,128)(2,1)S(1)} %bitcast.72), custom_call_target="tpu_custom_call" | custom-call | flops 4831838208 | bytes 30000000 | tf_op jit(solution)/shard_map/pallas_call | solution.py:82
  100.2 11.3 %all-to-all-start.1 = ((bf16[16,96,512]{2,1,0:T(8,128)(2,1)}), bf16[16,96,512]{2,1,0:T(8,128)(2,1)S(1)}, u32[]{:S(2)}, u32[]{:S(2)}) async-start(bf16[16,96,512]{2,1,0:T(8,128)(2,1)} %bitcast.34), calls=%async_computation.1 | async-start | bytes 3145728 | tf_op jit(solution)/shard_map/all_to_all | solution.py:190
  111.5 0.1 fusion.43.live_ref
  111.6 6.1 %shard_map.122.counts_ref = bf16[1536,3072]{1,0:T(8,128)(2,1)S(1)} custom-call(s32[2]{0:T(128)S(1)} %fusion.43.live_ref, s32[2,2,72]{2,1,0:T(2,128)S(1)} %pad_add_fusion.2.place_ref, s32[2,72,64]{2,1,0:T(8,128)S(1)} %get-tuple-element.29.dst_ref, s32[2,72,64]{2,1,0:T(8,128)S(1)} %get-tuple-element.31.src_ref), custom_call_target="tpu_custom_call" | custom-call | flops 2000000000 | bytes 40000000 | tf_op jit(solution)/shard_map/pallas_call | solution.py:46
  117.7 0.0 copy-start.1
  117.7 3.6 %copy-done.1 = bf16[1536,3072]{1,0:T(8,128)(2,1)} copy-done((bf16[1536,3072]{1,0:T(8,128)(2,1)}, bf16[1536,3072]{1,0:T(8,128)(2,1)S(1)}, u32[]{:S(2)}) %copy-start.1) | copy-done | bytes 9437208
  121.4 0.0 all-gather.4.cloned.1.call-done
  121.4 0.0 copy-start.2
  121.4 3.7 %copy-done.2 = bf16[1536,3072]{1,0:T(8,128)(2,1)S(1)} copy-done((bf16[1536,3072]{1,0:T(8,128)(2,1)S(1)}, bf16[1536,3072]{1,0:T(8,128)(2,1)}, u32[]{:S(2)}) %copy-start.2) | copy-done | bytes 9437208
  125.0 0.0 copy-start.6
  125.1 1.9 %copy-done.6 = bf16[3072,512]{1,0:T(8,128)(2,1)S(1)} copy-done((bf16[3072,512]{1,0:T(8,128)(2,1)S(1)}, bf16[3072,512]{1,0:T(8,128)(2,1)}, u32[]{:S(2)}) %copy-start.6) | copy-done | bytes 3145752
  126.9 7.0 %shard_map.123 = bf16[1536,512]{1,0:T(8,128)(2,1)} custom-call(s32[2]{0:T(128)S(1)} %pad_add_fusion.4.place_ref, bf16[1536,3072]{1,0:T(8,128)(2,1)S(1)} %copy-done.2, bf16[16,192,512]{2,1,0:T(8,128)(2,1)S(1)} %bitcast.73), custom_call_target="tpu_custom_call" | custom-call | flops 4831838208 | bytes 30000000 | tf_op jit(solution)/shard_map/pallas_call | solution.py:82
  133.9 0.0 copy-start.10
  133.9 0.0 all-to-all-done.1
  133.9 11.0 %all-to-all-start = ((bf16[16,96,512]{2,1,0:T(8,128)(2,1)}), bf16[16,96,512]{2,1,0:T(8,128)(2,1)}, u32[]{:S(2)}, u32[]{:S(2)}) async-start(bf16[16,96,512]{2,1,0:T(8,128)(2,1)} %bitcast.21), calls=%async_computation | async-start | bytes 3145728 | tf_op jit(solution)/shard_map/all_to_all | solution.py:190
  144.9 0.0 copy-done.12
  144.9 0.0 copy-done.8
  145.0 0.0 copy-done.9
  145.0 0.0 copy-done.11
  145.0 0.2 convolution_add_fusion.2
  145.2 0.2 convert_reduce_fusion
  145.4 0.0 copy-done.10
  145.4 0.9 fusion.2
  146.4 25.3 %all-to-all-done = bf16[16,96,512]{2,1,0:T(8,128)(2,1)} async-done(((bf16[16,96,512]{2,1,0:T(8,128)(2,1)}), bf16[16,96,512]{2,1,0:T(8,128)(2,1)}, u32[]{:S(2)}, u32[]{:S(2)}) %all-to-all-start) | async-done | bytes 1572896 | tf_op jit(solution)/shard_map/all_to_all | solution.py:190
  171.6 1.6 convert_reduce_fusion.1
  173.3 0.9 fusion.1
  (20 shorter events, 0.2 us)
Async XLA Ops:
  7.2 7.3 %copy-start = (bf16[512,512]{1,0:T(8,128)(2,1)S(1)}, bf16[512,512]{1,0:T(8,128)(2,1)}, u32[]{:S(2)}) copy-start(bf16[512,512]{1,0:T(8,128)(2,1)} %param.14) | copy-start | bytes 1572868
  7.2 114.2 %all-gather.4.cloned.1.call-start = ((), (), s32[]{:S(2)}) async-start(), calls=%async_computation.2 | async-start | bytes 3244032 | tf_op jit(solution)/shard_map/all_gather | solution.py:159
  10.6 66.8 %collective-permute-start = (s32[2,72,67]{2,1,0:T(8,128)S(1)}, s32[2,72,67]{2,1,0:T(8,128)S(1)}, u32[]{:S(2)}, u32[]{:S(2)}) collective-permute-start(s32[2,72,67]{2,1,0:T(8,128)S(1)} %pad_add_fusion.1), channel_id=1, source_target_pairs={{0,16},{16,0},{1,17},{17,1},{2,18},{18,2},{3,19},{19,3},{4,20},{20... | collective-permute-start | bytes 115784 | tf_op jit(solution)/shard_map/ppermute | solution.py:173
  69.8 1.7 copy-start.7
  79.3 10.2 %copy-start.5 = (bf16[32,96,512]{2,1,0:T(8,128)(2,1)S(1)}, bf16[32,96,512]{2,1,0:T(8,128)(2,1)}, u32[]{:S(2)}) copy-start(bf16[32,96,512]{2,1,0:T(8,128)(2,1)} %multiply_convert_fusion) | copy-start | bytes 9437188
  85.9 3.6 %copy-start.3 = (bf16[1536,3072]{1,0:T(8,128)(2,1)}, bf16[1536,3072]{1,0:T(8,128)(2,1)S(1)}, u32[]{:S(2)}) copy-start(bf16[1536,3072]{1,0:T(8,128)(2,1)S(1)} %shard_map.124.counts_ref) | copy-start | bytes 28311556
  89.5 3.7 %copy-start.4 = (bf16[1536,3072]{1,0:T(8,128)(2,1)S(1)}, bf16[1536,3072]{1,0:T(8,128)(2,1)}, u32[]{:S(2)}) copy-start(bf16[1536,3072]{1,0:T(8,128)(2,1)} %copy-done.3) | copy-start | bytes 28311556
  100.2 33.8 %all-to-all-start.1 = ((bf16[16,96,512]{2,1,0:T(8,128)(2,1)}), bf16[16,96,512]{2,1,0:T(8,128)(2,1)S(1)}, u32[]{:S(2)}, u32[]{:S(2)}) async-start(bf16[16,96,512]{2,1,0:T(8,128)(2,1)} %bitcast.34), calls=%async_computation.1 | async-start | bytes 3145728 | tf_op jit(solution)/shard_map/all_to_all | solution.py:190
  117.7 3.6 %copy-start.1 = (bf16[1536,3072]{1,0:T(8,128)(2,1)}, bf16[1536,3072]{1,0:T(8,128)(2,1)S(1)}, u32[]{:S(2)}) copy-start(bf16[1536,3072]{1,0:T(8,128)(2,1)S(1)} %shard_map.122.counts_ref) | copy-start | bytes 28311556
  121.4 3.7 %copy-start.2 = (bf16[1536,3072]{1,0:T(8,128)(2,1)S(1)}, bf16[1536,3072]{1,0:T(8,128)(2,1)}, u32[]{:S(2)}) copy-start(bf16[1536,3072]{1,0:T(8,128)(2,1)} %copy-done.1) | copy-start | bytes 28311556
  125.0 1.9 %copy-start.6 = (bf16[3072,512]{1,0:T(8,128)(2,1)S(1)}, bf16[3072,512]{1,0:T(8,128)(2,1)}, u32[]{:S(2)}) copy-start(bf16[3072,512]{1,0:T(8,128)(2,1)} %all-gather.4.cloned.1.call-done) | copy-start | bytes 9437188
  133.9 11.0 %copy-start.12 = (s32[96]{0:T(128)S(1)}, s32[96]{0:T(128)}, u32[]{:S(2)}) copy-start(s32[96]{0:T(128)} %param.12) | copy-start | bytes 1156
  133.9 11.0 %copy-start.8 = (bf16[512,512]{1,0:T(8,128)(2,1)S(1)}, bf16[512,512]{1,0:T(8,128)(2,1)}, u32[]{:S(2)}) copy-start(bf16[512,512]{1,0:T(8,128)(2,1)} %param.13) | copy-start | bytes 1572868
  133.9 11.0 %copy-start.9 = (bf16[96,512]{1,0:T(8,128)(2,1)S(1)}, bf16[96,512]{1,0:T(8,128)(2,1)}, u32[]{:S(2)}) copy-start(bf16[96,512]{1,0:T(8,128)(2,1)} %param.11) | copy-start | bytes 294916
  133.9 11.1 %copy-start.11 = (f32[512]{0:T(512)S(1)}, f32[512]{0:T(512)}, u32[]{:S(2)}) copy-start(f32[512]{0:T(512)} %param.15) | copy-start | bytes 6148
  133.9 11.5 %copy-start.10 = (bf16[96,512]{1,0:T(8,128)(2,1)S(1)}, bf16[96,512]{1,0:T(8,128)(2,1)}, u32[]{:S(2)}) copy-start(bf16[96,512]{1,0:T(8,128)(2,1)} %param.18) | copy-start | bytes 294916
  133.9 37.7 %all-to-all-start = ((bf16[16,96,512]{2,1,0:T(8,128)(2,1)}), bf16[16,96,512]{2,1,0:T(8,128)(2,1)}, u32[]{:S(2)}, u32[]{:S(2)}) async-start(bf16[16,96,512]{2,1,0:T(8,128)(2,1)} %bitcast.21), calls=%async_computation | async-start | bytes 3145728 | tf_op jit(solution)/shard_map/all_to_all | solution.py:190
Sparse Core Ops, SparseCore 0:
  13.9 78.2 all-gather.3

commit v2 on v0

v2 whole, which is shorter than its diff:
```python
import jax
import jax.numpy as jnp
from jax import lax
from jax.experimental import pallas as pl
from jax.experimental.pallas import tpu as pltpu
from jax.sharding import Mesh
from jax.sharding import PartitionSpec as P

TILE = 128
HALF = TILE // 2
UNROLL = 12
EXACT = 256
MIB = 1024 * 1024
PARTS = ("z", "xl", "core", "y", "xh")
PLANE = ("xl", "y", "xh")
SHIFTS = (64, 32, 16, 8, 4, 2)


def column_of(row):
    count = row.shape[1]
    across = lax.broadcasted_iota(jnp.int32, (count, count), 0)
    down = lax.broadcasted_iota(jnp.int32, (count, count), 1)
    return jnp.sum(jnp.where(across == down, row, 0.0), axis=1, keepdims=True)


def scaled(values):
    top = jnp.max(jnp.max(jnp.abs(values), axis=1, keepdims=True), axis=0, keepdims=True)
    scale = jnp.ones_like(top)
    flags = []
    for shift in SHIFTS:
        fits = top * 2.0**shift <= 2.0**15
        factor = jnp.where(fits, 2.0**shift, 1.0)
        top, scale = top * factor, scale * factor
        flags.append(jnp.where(fits, 1.0, 0.0))
    return values * scale, flags


def prepare_kernel(
    features_ref,
    grad_ref,
    weight_ref,
    degree_ref,
    index_ref,
    edges_ref,
    old_index_ref,
    old_edges_ref,
    sent_ref,
    slots_ref,
):
    nodes, width = grad_ref.shape
    for at, (index, edges) in enumerate(
        ((index_ref, edges_ref), (old_index_ref, old_edges_ref))
    ):
        slots, fields = index.shape
        numbers = index[...].astype(jnp.float32)
        lanes = lax.broadcasted_iota(jnp.int32, (slots, TILE), 1)
        row = jnp.zeros((slots, TILE), jnp.float32)
        for field in range(fields):
            row = jnp.where(lanes == HALF + field, numbers[:, field : field + 1], row)
        slots_ref[at, :slots, :] = row.astype(jnp.int32)
        slots_ref[at, :slots, :HALF] = edges[...]
        wide = jnp.concatenate([row, jnp.zeros((TILE - slots, TILE), jnp.float32)], axis=0)
        slots_ref[at, slots:, :] = wide.T[HALF : HALF + 8, :].astype(jnp.int32)

    product = lax.dot_general(
        grad_ref[...],
        weight_ref[...],
        (((1,), (1,)), ((), ())),
        preferred_element_type=jnp.float32,
    )
    degree = column_of(degree_ref[...].astype(jnp.float32))
    mean_grad = (product / degree).astype(jnp.bfloat16).astype(jnp.float32)
    values, flags = scaled(mean_grad)
    sent_ref[:nodes, :] = values
    values, more = scaled(features_ref[...].astype(jnp.float32))
    sent_ref[nodes : 2 * nodes, :] = values
    lanes = lax.broadcasted_iota(jnp.int32, (8, width), 1)
    tail = jnp.zeros((8, width), jnp.float32)
    for at, flag in enumerate(flags + more):
        tail = jnp.where(lanes == at, flag, tail)
    sent_ref[2 * nodes :, :] = tail


def prepare(features, old_grad, w_neigh, old_degree, tables):
    nodes, width = features.shape
    slots = tables[0].shape[0]
    return pl.pallas_call(
        prepare_kernel,
        out_shape=(
            jax.ShapeDtypeStruct((2 * nodes + 8, width), jnp.float32),
            jax.ShapeDtypeStruct((2, slots + 8, TILE), jnp.int32),
        ),
        compiler_params=pltpu.CompilerParams(vmem_limit_bytes=8 * MIB),
    )(features, old_grad, w_neigh, old_degree, *tables)


def sums_kernel(
    lane_ref,
    own_info,
    other_info,
    own_ref,
    other_ref,
    sources_ref,
    out_ref,
    edges,
    dst_rows,
    src_rows,
    counts,
    held,
    total,
    sems,
):
    step = pl.program_id(0)
    lane = lane_ref[0]
    planes = sources_ref.shape[0]
    pairs = dst_rows.shape[0]

    def fetch(plane):
        whole = pltpu.make_async_copy(
            sources_ref.at[plane, pl.ds(pl.multiple_of(lane * HALF, HALF), TILE)],
            held.at[pl.ds(plane * TILE, TILE)],
            sems.at[plane],
        )
        part = pltpu.make_async_copy(
            sources_ref.at[plane, pl.ds(pl.multiple_of((1 - lane) * TILE, HALF), HALF)],
            held.at[pl.ds(planes * TILE + plane * HALF, HALF)],
            sems.at[planes + plane],
        )
        return whole, part

    @pl.when(step == 0)
    def _():
        for plane in range(planes):
            for copy in fetch(plane):
                copy.start()
        edges[...] = own_ref[...]

    @pl.when(step == 1)
    def _():
        edges[...] = other_ref[...]

    lanes = lax.broadcasted_iota(jnp.int32, (pairs, TILE), 1)
    left = lanes < HALF
    even, odd = edges[pl.ds(0, pairs, 2), :], edges[pl.ds(1, pairs, 2), :]

    def field(at):
        return jnp.where(left, even[:, at : at + 1], odd[:, at : at + 1])

    values = jnp.where(left, even, pltpu.roll(odd, HALF, 1))
    column, count = field(HALF + 1), field(HALF + 2)
    plane = (column * 43) >> 7
    part = column - 3 * plane
    source = values & (TILE - 1)
    whole = part == 2 * lane
    own = whole | ((part == 1) & ((source >> 6) == lane))
    own &= (lanes & (HALF - 1)) < count
    place = jnp.where(whole, source, (source & (HALF - 1)) + (plane & 1) * HALF)
    place += jnp.where(left, 0, TILE)
    dst_rows[...] = jnp.where(own, values >> 7, -1).astype(jnp.float32)
    src_rows[...] = jnp.where(own, place, -1).astype(jnp.float32)
    live_pairs = jnp.sum((even[:, HALF + 2 : HALF + 3] > 0).astype(jnp.int32))

    dst_ids = lax.broadcasted_iota(jnp.int32, (TILE, TILE), 0).astype(jnp.bfloat16)
    src_ids = lax.broadcasted_iota(jnp.int32, (2 * TILE, TILE), 0).astype(jnp.bfloat16)
    zero, unit = jnp.bfloat16(0), jnp.bfloat16(1)

    def spot(slot):
        row, column = [
            jnp.where(step == 0, own_info[at, slot], other_info[at, slot]) for at in (0, 1)
        ]
        plane = (column * 43) >> 7
        block = jnp.where(column - 3 * plane == 2 * lane, plane, planes + (plane >> 1))
        return block, pl.ds(pl.multiple_of(row * TILE, TILE), TILE)

    def pair_counts(pair):
        dst = dst_rows[pl.ds(pair, 1), :].astype(jnp.bfloat16)
        src = src_rows[pl.ds(pair, 1), :].astype(jnp.bfloat16)
        dst_hot = jnp.where(dst_ids == dst, unit, zero)
        src_hot = jnp.where(src_ids == src, unit, zero)
        return lax.dot_general(
            dst_hot, src_hot, (((1,), (1,)), ((), ())), preferred_element_type=jnp.float32
        ).astype(jnp.bfloat16)

    def build(first, last, unroll):
        counts[...] = jnp.zeros_like(counts)

        def add(turn, peak):
            found = [first + turn * unroll + at for at in range(unroll)]
            added = [pair_counts(pair) for pair in found]
            for pair, both in zip(found, added):
                for side in range(2):
                    block, rows = spot(2 * pair + side)
                    sums = counts[block, rows, :] + both[:, side * TILE : (side + 1) * TILE]
                    counts[block, rows, :] = sums
                    peak = jnp.maximum(peak, sums)
            return peak

        start = jnp.zeros((TILE, TILE), jnp.bfloat16)
        return lax.fori_loop(0, pl.cdiv(last - first, unroll), add, start)

    def product():
        left_side = jnp.concatenate([counts[at] for at in range(counts.shape[0])], axis=1)
        return jnp.dot(left_side, held[...], preferred_element_type=jnp.float32)

    peak = jnp.max(build(0, live_pairs, UNROLL).astype(jnp.float32))

    @pl.when(step == 0)
    def _():
        for plane in range(planes):
            for copy in fetch(plane):
                copy.wait()

    @pl.when(peak < EXACT)
    def _():
        out_ref[...] = product().astype(jnp.bfloat16)

    @pl.when(peak >= EXACT)
    def _():
        total[...] = jnp.zeros_like(total)

        def some(turn, carry):
            build(2 * turn, 2 * turn + 2, 2)
            total[...] += product()
            return carry

        lax.fori_loop(0, pairs // 2, some, 0)
        out_ref[...] = total[...].astype(jnp.bfloat16)


def edge_sums(lane, own, other, which, sources, rows):
    slots = own.shape[1] - 8
    planes, height, width = sources.shape
    depth = planes * height
    table = pl.BlockSpec((None, slots, TILE), lambda step, _: (which, 0, 0))
    info = pl.BlockSpec(
        (None, 8, TILE), lambda step, _: (which, slots // 8, 0), memory_space=pltpu.SMEM
    )
    return pl.pallas_call(
        sums_kernel,
        out_shape=jax.ShapeDtypeStruct((2 * rows, width), jnp.bfloat16),
        grid_spec=pltpu.PrefetchScalarGridSpec(
            num_scalar_prefetch=1,
            grid=(2,),
            in_specs=[info, info, table, table, pl.BlockSpec(memory_space=pltpu.HBM)],
            out_specs=pl.BlockSpec(
                (rows, width), lambda step, lane: (step + lane[0] - 2 * step * lane[0], 0)
            ),
            scratch_shapes=[
                pltpu.VMEM((slots, TILE), jnp.int32),
                pltpu.VMEM((slots // 2, TILE), jnp.float32),
                pltpu.VMEM((slots // 2, TILE), jnp.float32),
                pltpu.VMEM((depth // TILE, rows, TILE), jnp.bfloat16),
                pltpu.VMEM((depth, width), jnp.bfloat16),
                pltpu.VMEM((rows, width), jnp.float32),
                pltpu.SemaphoreType.DMA((2 * planes,)),
            ],
        ),
        compiler_params=pltpu.CompilerParams(vmem_limit_bytes=28 * MIB),
        cost_estimate=pl.CostEstimate(
            flops=8 * 10**9, bytes_accessed=10 * 10**6, transcendentals=0
        ),
    )(lane, own, other, own, other, sources)


def shards(
    features,
    degree,
    w_self,
    w_neigh,
    bias_term,
    tile_index,
    tile_edges,
    old_grad,
    old_degree,
    old_index,
    old_edges,
):
    nodes, width = features.shape
    rows = lax.axis_size("y") * lax.axis_size("xh") * nodes
    lane = lax.axis_index("xl")

    tables = [table[0, 0] for table in (tile_index, tile_edges, old_index, old_edges)]
    sent, own = prepare(features, old_grad, w_neigh, old_degree[None], tables)
    other = lax.ppermute(own, "xl", [(0, 1), (1, 0)])

    got = lax.all_gather(sent.astype(jnp.float16), ("z", "core"), axis=0, tiled=False)
    flags = got[:, 2 * nodes, : 2 * len(SHIFTS)].reshape(-1, 2, len(SHIFTS))
    factors = jnp.array([2.0**-shift for shift in SHIFTS], jnp.float32)
    undo = jnp.prod(jnp.where(flags > 0, factors, 1.0), axis=-1)

    def sums(at, which):
        values = got[:, at * nodes : (at + 1) * nodes].astype(jnp.float32)
        values = (values * undo[:, at, None, None]).astype(jnp.bfloat16)
        values = values.reshape(-1, 2 * nodes, width)
        partial = edge_sums(lane.reshape(1), own, other, which, values, rows)
        return lax.all_to_all(partial.reshape(-1, nodes, width), PLANE, 0, 0)

    old_parts = sums(0, 1)
    new_parts = sums(1, 0)

    old_summed = jnp.sum(old_parts.astype(jnp.float32), axis=0)
    self_grad = lax.dot_general(
        old_grad, w_self, (((1,), (1,)), ((), ())), preferred_element_type=jnp.float32
    )
    grad_input = (self_grad + old_summed).astype(jnp.bfloat16)

    summed = jnp.sum(new_parts.astype(jnp.float32), axis=0)
    neighbour_mean = (summed / degree[:, None].astype(jnp.float32)).astype(jnp.bfloat16)
    preact = jnp.dot(features, w_self, preferred_element_type=jnp.float32) + bias_term
    preact = preact + jnp.dot(neighbour_mean, w_neigh, preferred_element_type=jnp.float32)
    output = jax.nn.relu(preact).astype(jnp.bfloat16)
    return (output, grad_input)


def solution(mesh):
    parts = Mesh(mesh.devices.reshape(16, 2, 2, 4, 2), PARTS)
    block = ("z", "xl", "core")
    side = ("y", "xh")
    in_specs = (
        P(PARTS, None),
        P(PARTS),
        P(),
        P(),
        P(),
        P(block, side, None, None),
        P(block, side, None, None),
        P(PARTS, None),
        P(PARTS),
        P(block, side, None, None),
        P(block, side, None, None),
    )
    out_specs = (P(PARTS, None), P(PARTS, None))
    return jax.shard_map(
        shards, mesh=parts, in_specs=in_specs, out_specs=out_specs, check_vma=False
    )
```

time: 470 us -> 162 us (0.34)
  waiting for transfers between devices: 226 us -> 29.9 us
  matrix products: 135 us -> 2.08 us
  local copies, waits for them, and re-layouts: 88.3 us -> 13.4 us
  blocking collectives: 0 us -> 58.5 us
  Pallas kernels: 0 us -> 28.8 us
  starting transfers between devices: 0.16 us -> 17.5 us
  between operations: 13.9 us -> 0.82 us
    all_gather x2 -> x0, waiting for transfers between devices: 145 us -> none  [the longest x1 128 us: shards(): source_grads = lax.all_gather(mean_grad, 'row', axis=0, tiled=True)]
    dot_general x38 -> x1, matrix products: 131 us -> 0.22 us  [shards(): jnp.dot(features, w_self, preferred_element_type=jnp.float32) + bias_term]
    reduce_scatter x2 -> x0, waiting for transfers between devices: 80.1 us -> none  [the longest x1 80 us: shards(): lax.psum_scatter(forward_terms.astype(jnp.bfloat16), 'col', scatter_dimen...]
    gather x18 -> x0, local copies, waits for them, and re-layouts: 79.2 us -> none  [add_group(): picked = jnp.take(col_blocks, part_tiles[:, 1], axis=0)]
    all_gather x0 -> x1, blocking collectives: none -> 58.5 us  [shards(): lax.all_gather(sent.astype(jnp.float16), ('z', 'core'), axis=0, tiled=False)]
    all_to_all x0 -> x2, waiting for transfers between devices: none -> 29.9 us  [sums(): return lax.all_to_all(partial.reshape(-1, nodes, width), PLANE, 0, 0)]
    pallas_call x0 -> x3, Pallas kernels: none -> 28.8 us  [the longest x2 28.3 us: edge_sums(): pl.pallas_call(sums_kernel, out_shape=jax.ShapeDtypeStruct((2 * rows, wid...]
    all_to_all x0 -> x2, starting transfers between devices: none -> 14.7 us  [sums(): return lax.all_to_all(partial.reshape(-1, nodes, width), PLANE, 0, 0)]
  transfers between devices with their start and end apart: 4 -> 3, of which waited for: 3 -> 2; matrix products, arithmetic and copies ran while one was open for 48% -> 5% of each run, Pallas kernels for 0% -> 9%
where the time goes in v2:
time: 162 us; the launch traced here: 159 us
  blocking collectives  58.5 us (36%)
  waiting for transfers between devices  29.9 us (18%)
  Pallas kernels  28.8 us (18%)
  starting transfers between devices  17.5 us (11%)
  local copies, waits for them, and re-layouts  13.4 us (8%)
  other arithmetic  7.86 us (5%)
  matrix products  2.08 us (1%)
    all_gather x1, blocking collectives, shards(): lax.all_gather(sent.astype(jnp.float16), ('z', 'core'), axis=0, tiled=False)  58.5 us
    all_to_all x2, waiting for transfers between devices, sums(): return lax.all_to_all(partial.reshape(-1, nodes, width), PLANE, 0, 0)  29.9 us
    pallas_call x2, Pallas kernels, edge_sums(): pl.pallas_call(sums_kernel, out_shape=jax.ShapeDtypeStruct((2 * rows, wid...  28.3 us
    all_to_all x2, starting transfers between devices, sums(): return lax.all_to_all(partial.reshape(-1, nodes, width), PLANE, 0, 0)  14.7 us
    unnamed x33, local copies, waits for them, and re-layouts  13.4 us
    convert_element_type x1, other arithmetic, sums(): values = (values * undo[:, at, None, None]).astype(jnp.bfloat16)  5.86 us
  transfers between devices with their start and end apart: 3, of which 2 were waited for; matrix products, arithmetic and copies ran while one was open for 5% of the time, Pallas kernels for 9%

profile of v2, /device:TPU:6, one launch (start us, length us, event | category | flops | bytes accessed | tf_op | source)
XLA Modules:
  0.0 158.8 jit_solution(9269715872448682144)
XLA Ops:
  0.6 0.0 copy-start
  0.6 0.8 copy.18
  1.5 0.8 copy.19
  2.3 0.8 copy.20
  3.1 0.8 copy.21
  3.9 0.0 copy-start.3
  3.9 1.0 copy-done.3
  5.0 0.0 copy-start.5
  5.0 0.9 copy-done.5
  5.9 0.0 copy-start.7
  5.9 0.9 copy-done.7
  6.8 0.0 copy-start.9
  6.8 0.7 copy-done.9
  7.4 0.5 shard_map.131
  7.9 2.7 %collective-permute-start = (s32[2,80,128]{2,1,0:T(8,128)S(1)}, s32[2,80,128]{2,1,0:T(8,128)S(1)}, u32[]{:S(2)}, u32[]{:S(2)}) collective-permute-start(s32[2,80,128]{2,1,0:T(8,128)S(1)} %get-tuple-element.4.own_info.own_ref), channel_id=1, source_target_pairs={{0,16},{16,0},{1,17},{17,1},{2,18},{18,2},{3,19},{19,3},{4,20},{20... | collective-permute-start | bytes 245768 | tf_op jit(solution)/shard_map/ppermute | solution.py:284
  10.7 0.0 copy-start.12
  10.7 58.5 %all-gather.2 = f16[6400,512]{1,0:T(8,128)(2,1)S(1)} all-gather(f16[200,512]{1,0:T(8,128)(2,1)S(1)} %convert_element_type.34), channel_id=2, replica_groups=mesh['z'=16,'xl'=2,'core'=2,'y'=4,'xh'=2] {'z','core'}, dimensions={0}, use_global_device_ids=true | all-gather | bytes 6758400 | tf_op jit(solution)/shard_map/all_gather | solution.py:286
  69.1 0.0 copy-start.10
  69.2 2.7 %copy-done.10 = f16[6400,512]{1,0:T(8,128)(2,1)} copy-done((f16[6400,512]{1,0:T(8,128)(2,1)}, f16[6400,512]{1,0:T(8,128)(2,1)S(1)}, u32[]{:S(2)}) %copy-start.10) | copy-done | bytes 6553624
  71.9 0.1 copy.23
  72.0 0.0 copy-done.12
  72.0 0.1 select_reduce_fusion
  72.1 5.9 %multiply_convert_fusion = (bf16[32,96,512]{2,1,0:T(8,128)(2,1)}, bf16[32,96,512]{2,1,0:T(8,128)(2,1)}) fusion(f16[32,200,512]{2,1,0:T(8,128)(2,1)} %bitcast.30, f32[32]{0:T(128)S(1)} %get-tuple-element.8, f32[32]{0:T(128)S(1)} %get-tuple-element.9), kind=kLoop, calls=%fused_computation | loop fusion | flops 9437184 | bytes 12583168 | tf_op jit(solution)/shard_map/convert_element_type | solution.py:293
  78.0 0.0 collective-permute-done.other_info.other_ref
  78.0 0.0 copy-start.2
  78.0 1.9 %copy-done.2 = bf16[32,96,512]{2,1,0:T(8,128)(2,1)S(1)} copy-done((bf16[32,96,512]{2,1,0:T(8,128)(2,1)S(1)}, bf16[32,96,512]{2,1,0:T(8,128)(2,1)}, u32[]{:S(2)}) %copy-start.2) | copy-done | bytes 3145752
  79.9 14.4 %shard_map.133 = bf16[1536,512]{1,0:T(8,128)(2,1)} custom-call(s32[1]{0:T(128)} %bitcast.lane_ref, s32[2,80,128]{2,1,0:T(8,128)S(1)} %get-tuple-element.4.own_info.own_ref, s32[2,80,128]{2,1,0:T(8,128)S(1)} %collective-permute-done.other_info.other_ref, s32[2,80,128]{2,1,0:T(8,128)S(1)} %get-tuple-element.4.own_info.own_ref, ...), custom_call_target="tpu_custom_call" | custom-call | flops 8000000000 | bytes 10000000 | tf_op jit(solution)/shard_map/pallas_call | solution.py:238
  94.3 7.9 %all-to-all-start.1 = ((bf16[16,96,512]{2,1,0:T(8,128)(2,1)}), bf16[16,96,512]{2,1,0:T(8,128)(2,1)S(1)}, u32[]{:S(2)}, u32[]{:S(2)}) async-start(bf16[16,96,512]{2,1,0:T(8,128)(2,1)} %bitcast.12), calls=%async_computation.1 | async-start | bytes 3145728 | tf_op jit(solution)/shard_map/all_to_all | solution.py:296
  102.1 0.0 copy-start.1
  102.1 1.9 %copy-done.1 = bf16[32,96,512]{2,1,0:T(8,128)(2,1)S(1)} copy-done((bf16[32,96,512]{2,1,0:T(8,128)(2,1)S(1)}, bf16[32,96,512]{2,1,0:T(8,128)(2,1)}, u32[]{:S(2)}) %copy-start.1) | copy-done | bytes 3145752
  104.0 13.9 %shard_map.132 = bf16[1536,512]{1,0:T(8,128)(2,1)} custom-call(s32[1]{0:T(128)} %bitcast.lane_ref, s32[2,80,128]{2,1,0:T(8,128)S(1)} %get-tuple-element.4.own_info.own_ref, s32[2,80,128]{2,1,0:T(8,128)S(1)} %collective-permute-done.other_info.other_ref, s32[2,80,128]{2,1,0:T(8,128)S(1)} %get-tuple-element.4.own_info.own_ref, ...), custom_call_target="tpu_custom_call" | custom-call | flops 8000000000 | bytes 10000000 | tf_op jit(solution)/shard_map/pallas_call | solution.py:238
  117.9 0.0 copy-start.13
  117.9 0.0 copy-start.6
  117.9 0.0 copy-start.11
  118.0 0.0 copy-start.8
  118.0 7.8 %all-to-all-done.1 = bf16[16,96,512]{2,1,0:T(8,128)(2,1)S(1)} async-done(((bf16[16,96,512]{2,1,0:T(8,128)(2,1)}), bf16[16,96,512]{2,1,0:T(8,128)(2,1)S(1)}, u32[]{:S(2)}, u32[]{:S(2)}) %all-to-all-start.1) | async-done | bytes 1572896 | tf_op jit(solution)/shard_map/all_to_all | solution.py:296
  125.8 6.9 %all-to-all-start = ((bf16[16,96,512]{2,1,0:T(8,128)(2,1)}), bf16[16,96,512]{2,1,0:T(8,128)(2,1)}, u32[]{:S(2)}, u32[]{:S(2)}) async-start(bf16[16,96,512]{2,1,0:T(8,128)(2,1)} %bitcast.9), calls=%async_computation | async-start | bytes 3145728 | tf_op jit(solution)/shard_map/all_to_all | solution.py:296
  132.7 0.0 copy-done.13
  132.7 0.0 copy-start.4
  132.7 0.0 copy-done
  132.7 0.0 copy-done.6
  132.7 0.0 copy-done.11
  132.7 0.2 convolution_add_fusion.2
  133.0 0.2 convert_reduce_fusion
  133.2 0.0 copy-done.8
  133.2 0.9 fusion.2
  134.1 22.1 %all-to-all-done = bf16[16,96,512]{2,1,0:T(8,128)(2,1)} async-done(((bf16[16,96,512]{2,1,0:T(8,128)(2,1)}), bf16[16,96,512]{2,1,0:T(8,128)(2,1)}, u32[]{:S(2)}, u32[]{:S(2)}) %all-to-all-start) | async-done | bytes 1572896 | tf_op jit(solution)/shard_map/all_to_all | solution.py:296
  156.2 1.6 %convert_reduce_fusion.1 = f32[96,512]{1,0:T(8,128)S(1)} fusion(bf16[16,96,512]{2,1,0:T(8,128)(2,1)} %all-to-all-done), kind=kLoop, calls=%fused_computation.3 | loop fusion | flops 1523712 | bytes 1769472 | tf_op jit(solution)/shard_map/reduce_sum | solution.py:307
  157.9 0.0 copy-done.4
  157.9 0.9 fusion.1
  (6 shorter events, 0.1 us)
Async XLA Ops:
  0.6 132.1 %copy-start = (bf16[512,512]{1,0:T(8,128)(2,1)S(1)}, bf16[512,512]{1,0:T(8,128)(2,1)}, u32[]{:S(2)}) copy-start(bf16[512,512]{1,0:T(8,128)(2,1)} %param.14) | copy-start | bytes 1572868
  3.9 1.0 copy-start.3
  5.0 0.9 copy-start.5
  5.9 0.9 copy-start.7
  6.8 0.7 copy-start.9
  7.9 70.1 %collective-permute-start = (s32[2,80,128]{2,1,0:T(8,128)S(1)}, s32[2,80,128]{2,1,0:T(8,128)S(1)}, u32[]{:S(2)}, u32[]{:S(2)}) collective-permute-start(s32[2,80,128]{2,1,0:T(8,128)S(1)} %get-tuple-element.4.own_info.own_ref), channel_id=1, source_target_pairs={{0,16},{16,0},{1,17},{17,1},{2,18},{18,2},{3,19},{19,3},{4,20},{20... | collective-permute-start | bytes 245768 | tf_op jit(solution)/shard_map/ppermute | solution.py:284
  10.7 61.3 %copy-start.12 = (f32[6]{0:T(128)S(1)}, f32[6]{0:T(128)}, u32[]{:S(2)}) copy-start(f32[6]{0:T(128)} %constant.16.clone) | copy-start | bytes 76
  69.1 2.7 %copy-start.10 = (f16[6400,512]{1,0:T(8,128)(2,1)}, f16[6400,512]{1,0:T(8,128)(2,1)S(1)}, u32[]{:S(2)}) copy-start(f16[6400,512]{1,0:T(8,128)(2,1)S(1)} %all-gather.2) | copy-start | bytes 19660804
  78.0 1.9 %copy-start.2 = (bf16[32,96,512]{2,1,0:T(8,128)(2,1)S(1)}, bf16[32,96,512]{2,1,0:T(8,128)(2,1)}, u32[]{:S(2)}) copy-start(bf16[32,96,512]{2,1,0:T(8,128)(2,1)} %get-tuple-element.6) | copy-start | bytes 9437188
  94.3 31.5 %all-to-all-start.1 = ((bf16[16,96,512]{2,1,0:T(8,128)(2,1)}), bf16[16,96,512]{2,1,0:T(8,128)(2,1)S(1)}, u32[]{:S(2)}, u32[]{:S(2)}) async-start(bf16[16,96,512]{2,1,0:T(8,128)(2,1)} %bitcast.12), calls=%async_computation.1 | async-start | bytes 3145728 | tf_op jit(solution)/shard_map/all_to_all | solution.py:296
  102.1 1.9 %copy-start.1 = (bf16[32,96,512]{2,1,0:T(8,128)(2,1)S(1)}, bf16[32,96,512]{2,1,0:T(8,128)(2,1)}, u32[]{:S(2)}) copy-start(bf16[32,96,512]{2,1,0:T(8,128)(2,1)} %get-tuple-element.7) | copy-start | bytes 9437188
  117.9 14.8 %copy-start.13 = (s32[96]{0:T(128)S(1)}, s32[96]{0:T(128)}, u32[]{:S(2)}) copy-start(s32[96]{0:T(128)} %param.13) | copy-start | bytes 1156
  117.9 14.8 %copy-start.6 = (bf16[96,512]{1,0:T(8,128)(2,1)S(1)}, bf16[96,512]{1,0:T(8,128)(2,1)}, u32[]{:S(2)}) copy-start(bf16[96,512]{1,0:T(8,128)(2,1)} %features_ref.1) | copy-start | bytes 294916
  117.9 14.8 %copy-start.11 = (f32[512]{0:T(512)S(1)}, f32[512]{0:T(512)}, u32[]{:S(2)}) copy-start(f32[512]{0:T(512)} %param.16) | copy-start | bytes 6148
  118.0 15.2 %copy-start.8 = (bf16[96,512]{1,0:T(8,128)(2,1)S(1)}, bf16[96,512]{1,0:T(8,128)(2,1)}, u32[]{:S(2)}) copy-start(bf16[96,512]{1,0:T(8,128)(2,1)} %grad_ref.1) | copy-start | bytes 294916
  125.8 30.4 %all-to-all-start = ((bf16[16,96,512]{2,1,0:T(8,128)(2,1)}), bf16[16,96,512]{2,1,0:T(8,128)(2,1)}, u32[]{:S(2)}, u32[]{:S(2)}) async-start(bf16[16,96,512]{2,1,0:T(8,128)(2,1)} %bitcast.9), calls=%async_computation | async-start | bytes 3145728 | tf_op jit(solution)/shard_map/all_to_all | solution.py:296
  132.7 25.2 %copy-start.4 = (bf16[512,512]{1,0:T(8,128)(2,1)S(1)}, bf16[512,512]{1,0:T(8,128)(2,1)}, u32[]{:S(2)}) copy-start(bf16[512,512]{1,0:T(8,128)(2,1)} %weight_ref.1) | copy-start | bytes 1572868

commit v3 on v2

--- a/solution.py
+++ b/solution.py
@@ -10,7 +10,7 @@
 HALF = TILE // 2
 UNROLL = 12
 EXACT = 256
-MIB = 1024 * 1024
+VMEM = 58 * 1024 * 1024
 PARTS = ("z", "xl", "core", "y", "xh")
 PLANE = ("xl", "y", "xh")
 SHIFTS = (64, 32, 16, 8, 4, 2)
@@ -51,16 +51,16 @@
     for at, (index, edges) in enumerate(
         ((index_ref, edges_ref), (old_index_ref, old_edges_ref))
     ):
-        slots, fields = index.shape
-        numbers = index[...].astype(jnp.float32)
-        lanes = lax.broadcasted_iota(jnp.int32, (slots, TILE), 1)
-        row = jnp.zeros((slots, TILE), jnp.float32)
-        for field in range(fields):
-            row = jnp.where(lanes == HALF + field, numbers[:, field : field + 1], row)
-        slots_ref[at, :slots, :] = row.astype(jnp.int32)
-        slots_ref[at, :slots, :HALF] = edges[...]
-        wide = jnp.concatenate([row, jnp.zeros((TILE - slots, TILE), jnp.float32)], axis=0)
-        slots_ref[at, slots:, :] = wide.T[HALF : HALF + 8, :].astype(jnp.int32)
+        fields, _, slots = index.shape
+        numbers = jnp.concatenate([edges[...]] + [index[field] for field in range(fields)], axis=0)
+        numbers = jnp.concatenate(
+            [numbers, jnp.zeros((TILE - HALF - fields, slots), jnp.int32)], axis=0
+        )
+        numbers = jnp.concatenate(
+            [numbers, jnp.zeros((TILE, TILE - slots), jnp.int32)], axis=1
+        )
+        slots_ref[at, :slots, :] = numbers.astype(jnp.float32).T[:slots].astype(jnp.int32)
+        slots_ref[at, slots:, :] = numbers[HALF : HALF + 8, :]
 
     product = lax.dot_general(
         grad_ref[...],
@@ -83,15 +83,24 @@
 
 def prepare(features, old_grad, w_neigh, old_degree, tables):
     nodes, width = features.shape
-    slots = tables[0].shape[0]
+    slots = tables[0].shape[-1]
+    args = (features, old_grad, w_neigh, old_degree, *tables)
+    outs = (
+        jax.ShapeDtypeStruct((2 * nodes + 8, width), jnp.float32),
+        jax.ShapeDtypeStruct((2, slots + 8, TILE), jnp.int32),
+    )
+
+    def whole(arg):
+        return pl.BlockSpec(arg.shape, lambda _: (0,) * len(arg.shape))
+
     return pl.pallas_call(
         prepare_kernel,
-        out_shape=(
-            jax.ShapeDtypeStruct((2 * nodes + 8, width), jnp.float32),
-            jax.ShapeDtypeStruct((2, slots + 8, TILE), jnp.int32),
-        ),
-        compiler_params=pltpu.CompilerParams(vmem_limit_bytes=8 * MIB),
-    )(features, old_grad, w_neigh, old_degree, *tables)
+        out_shape=outs,
+        grid=(1,),
+        in_specs=[whole(arg) for arg in args],
+        out_specs=tuple(whole(out) for out in outs),
+        compiler_params=pltpu.CompilerParams(vmem_limit_bytes=VMEM),
+    )(*args)
 
 
 def sums_kernel(
@@ -100,7 +109,8 @@
     other_info,
     own_ref,
     other_ref,
-    sources_ref,
+    grads_ref,
+    features_ref,
     out_ref,
     edges,
     dst_rows,
@@ -110,32 +120,36 @@
     total,
     sems,
 ):
-    step = pl.program_id(0)
+    array, half = pl.program_id(0), pl.program_id(1)
     lane = lane_ref[0]
-    planes = sources_ref.shape[0]
+    planes = grads_ref.shape[0]
     pairs = dst_rows.shape[0]
 
-    def fetch(plane):
-        whole = pltpu.make_async_copy(
-            sources_ref.at[plane, pl.ds(pl.multiple_of(lane * HALF, HALF), TILE)],
-            held.at[pl.ds(plane * TILE, TILE)],
-            sems.at[plane],
-        )
-        part = pltpu.make_async_copy(
-            sources_ref.at[plane, pl.ds(pl.multiple_of((1 - lane) * TILE, HALF), HALF)],
-            held.at[pl.ds(planes * TILE + plane * HALF, HALF)],
-            sems.at[planes + plane],
-        )
-        return whole, part
-
-    @pl.when(step == 0)
-    def _():
+    def fetches(sources_ref, into):
         for plane in range(planes):
-            for copy in fetch(plane):
-                copy.start()
+            yield pltpu.make_async_copy(
+                sources_ref.at[plane, pl.ds(pl.multiple_of(lane * HALF, HALF), TILE)],
+                held.at[into, pl.ds(plane * TILE, TILE)],
+                sems.at[into, plane],
+            )
+            yield pltpu.make_async_copy(
+                sources_ref.at[plane, pl.ds(pl.multiple_of((1 - lane) * TILE, HALF), HALF)],
+                held.at[into, pl.ds(planes * TILE + plane * HALF, HALF)],
+                sems.at[into, planes + plane],
+            )
+
+    @pl.when((array == 0) & (half == 0))
+    def _():
+        for copy in fetches(grads_ref, 0):
+            copy.start()
+        for copy in fetches(features_ref, 1):
+            copy.start()
+
+    @pl.when(half == 0)
+    def _():
         edges[...] = own_ref[...]
 
-    @pl.when(step == 1)
+    @pl.when(half == 1)
     def _():
         edges[...] = other_ref[...]
 
@@ -166,7 +180,7 @@
 
     def spot(slot):
         row, column = [
-            jnp.where(step == 0, own_info[at, slot], other_info[at, slot]) for at in (0, 1)
+            jnp.where(half == 0, own_info[at, slot], other_info[at, slot]) for at in (0, 1)
         ]
         plane = (column * 43) >> 7
         block = jnp.where(column - 3 * plane == 2 * lane, plane, planes + (plane >> 1))
@@ -200,19 +214,28 @@
 
     def product():
         left_side = jnp.concatenate([counts[at] for at in range(counts.shape[0])], axis=1)
-        return jnp.dot(left_side, held[...], preferred_element_type=jnp.float32)
+        return jnp.dot(left_side, held[array], preferred_element_type=jnp.float32)
 
     peak = jnp.max(build(0, live_pairs, UNROLL).astype(jnp.float32))
 
-    @pl.when(step == 0)
-    def _():
-        for plane in range(planes):
-            for copy in fetch(plane):
-                copy.wait()
+    @pl.when((array == 0) & (half == 0))
+    def _():
+        for copy in fetches(grads_ref, 0):
+            copy.wait()
+
+    @pl.when((array == 1) & (half == 0))
+    def _():
+        for copy in fetches(features_ref, 1):
+            copy.wait()
+
+    def put(sums):
+        nodes = out_ref.shape[1]
+        for at in range(out_ref.shape[0]):
+            out_ref[at] = sums[at * nodes : (at + 1) * nodes].astype(jnp.bfloat16)
 
     @pl.when(peak < EXACT)
     def _():
-        out_ref[...] = product().astype(jnp.bfloat16)
+        put(product())
 
     @pl.when(peak >= EXACT)
     def _():
@@ -224,42 +247,46 @@
             return carry
 
         lax.fori_loop(0, pairs // 2, some, 0)
-        out_ref[...] = total[...].astype(jnp.bfloat16)
-
-
-def edge_sums(lane, own, other, which, sources, rows):
+        put(total[...])
+
+
+def edge_sums(lane, own, other, grads, features, devices, nodes):
     slots = own.shape[1] - 8
-    planes, height, width = sources.shape
-    depth = planes * height
-    table = pl.BlockSpec((None, slots, TILE), lambda step, _: (which, 0, 0))
+    planes, height, width = grads.shape
+    depth, rows = planes * height, devices * nodes
+    table = pl.BlockSpec((None, slots, TILE), lambda array, half, _: (1 - array, 0, 0))
     info = pl.BlockSpec(
-        (None, 8, TILE), lambda step, _: (which, slots // 8, 0), memory_space=pltpu.SMEM
-    )
+        (None, 8, TILE),
+        lambda array, half, _: (1 - array, slots // 8, 0),
+        memory_space=pltpu.SMEM,
+    )
+    far = pl.BlockSpec(memory_space=pl.ANY)
     return pl.pallas_call(
         sums_kernel,
-        out_shape=jax.ShapeDtypeStruct((2 * rows, width), jnp.bfloat16),
+        out_shape=jax.ShapeDtypeStruct((2 * devices, 2, nodes, width), jnp.bfloat16),
         grid_spec=pltpu.PrefetchScalarGridSpec(
             num_scalar_prefetch=1,
-            grid=(2,),
-            in_specs=[info, info, table, table, pl.BlockSpec(memory_space=pltpu.HBM)],
+            grid=(2, 2),
+            in_specs=[info, info, table, table, far, far],
             out_specs=pl.BlockSpec(
-                (rows, width), lambda step, lane: (step + lane[0] - 2 * step * lane[0], 0)
+                (devices, None, nodes, width),
+                lambda array, half, lane: (half + lane[0] - 2 * half * lane[0], array, 0, 0),
             ),
             scratch_shapes=[
                 pltpu.VMEM((slots, TILE), jnp.int32),
                 pltpu.VMEM((slots // 2, TILE), jnp.float32),
                 pltpu.VMEM((slots // 2, TILE), jnp.float32),
                 pltpu.VMEM((depth // TILE, rows, TILE), jnp.bfloat16),
-                pltpu.VMEM((depth, width), jnp.bfloat16),
+                pltpu.VMEM((2, depth, width), jnp.bfloat16),
                 pltpu.VMEM((rows, width), jnp.float32),
-                pltpu.SemaphoreType.DMA((2 * planes,)),
+                pltpu.SemaphoreType.DMA((2, 2 * planes)),
             ],
         ),
-        compiler_params=pltpu.CompilerParams(vmem_limit_bytes=28 * MIB),
+        compiler_params=pltpu.CompilerParams(vmem_limit_bytes=VMEM),
         cost_estimate=pl.CostEstimate(
-            flops=8 * 10**9, bytes_accessed=10 * 10**6, transcendentals=0
+            flops=16 * 10**9, bytes_accessed=20 * 10**6, transcendentals=0
         ),
-    )(lane, own, other, own, other, sources)
+    )(lane, own, other, own, other, grads, features)
 
 
 def shards(
@@ -276,10 +303,13 @@
     old_edges,
 ):
     nodes, width = features.shape
-    rows = lax.axis_size("y") * lax.axis_size("xh") * nodes
+    devices = lax.axis_size("y") * lax.axis_size("xh")
     lane = lax.axis_index("xl")
 
-    tables = [table[0, 0] for table in (tile_index, tile_edges, old_index, old_edges)]
+    tables = []
+    for index, edges in ((tile_index, tile_edges), (old_index, old_edges)):
+        tables.append(jnp.transpose(index[0], (2, 0, 1)))
+        tables.append(edges[0, 0].T)
     sent, own = prepare(features, old_grad, w_neigh, old_degree[None], tables)
     other = lax.ppermute(own, "xl", [(0, 1), (1, 0)])
 
@@ -288,23 +318,20 @@
     factors = jnp.array([2.0**-shift for shift in SHIFTS], jnp.float32)
     undo = jnp.prod(jnp.where(flags > 0, factors, 1.0), axis=-1)
 
-    def sums(at, which):
+    def sources(at):
         values = got[:, at * nodes : (at + 1) * nodes].astype(jnp.float32)
         values = (values * undo[:, at, None, None]).astype(jnp.bfloat16)
-        values = values.reshape(-1, 2 * nodes, width)
-        partial = edge_sums(lane.reshape(1), own, other, which, values, rows)
-        return lax.all_to_all(partial.reshape(-1, nodes, width), PLANE, 0, 0)
-
-    old_parts = sums(0, 1)
-    new_parts = sums(1, 0)
-
-    old_summed = jnp.sum(old_parts.astype(jnp.float32), axis=0)
+        return values.reshape(-1, 2 * nodes, width)
+
+    partial = edge_sums(lane.reshape(1), own, other, sources(0), sources(1), devices, nodes)
+    parts = lax.all_to_all(partial, PLANE, 0, 0)
+    old_summed = jnp.sum(parts[:, 0].astype(jnp.float32), axis=0)
     self_grad = lax.dot_general(
         old_grad, w_self, (((1,), (1,)), ((), ())), preferred_element_type=jnp.float32
     )
     grad_input = (self_grad + old_summed).astype(jnp.bfloat16)
 
-    summed = jnp.sum(new_parts.astype(jnp.float32), axis=0)
+    summed = jnp.sum(parts[:, 1].astype(jnp.float32), axis=0)
     neighbour_mean = (summed / degree[:, None].astype(jnp.float32)).astype(jnp.bfloat16)
     preact = jnp.dot(features, w_self, preferred_element_type=jnp.float32) + bias_term
     preact = preact + jnp.dot(neighbour_mean, w_neigh, preferred_element_type=jnp.float32)

time: 162 us -> 163 us (level)
  the two profiles are of different devices: /device:TPU:6 before, /device:TPU:66 now
where the time goes in v3:
time: 163 us
  waiting for transfers between devices  57.2 us (35%)
  blocking collectives  56.5 us (35%)
  Pallas kernels  22 us (13%)
  starting transfers between devices  11.2 us (7%)
  other arithmetic  9.25 us (6%)
  local copies, waits for them, and re-layouts  3.55 us (2%)
  matrix products  2.06 us (1%)
    all_to_all x1, waiting for transfers between devices, shards(): parts = lax.all_to_all(partial, PLANE, 0, 0)  57.2 us
    all_gather x1, blocking collectives, shards(): lax.all_gather(sent.astype(jnp.float16), ('z', 'core'), axis=0, tiled=False)  56.5 us
    pallas_call x1, Pallas kernels, edge_sums(): pl.pallas_call(sums_kernel, out_shape=jax.ShapeDtypeStruct((2 * devices,...  19.6 us
    all_to_all x1, starting transfers between devices, shards(): parts = lax.all_to_all(partial, PLANE, 0, 0)  8.79 us
    convert_element_type x1, other arithmetic, sources(): values = (values * undo[:, at, None, None]).astype(jnp.bfloat16)  5.77 us
    unnamed x19, local copies, waits for them, and re-layouts  3.51 us
  transfers between devices with their start and end apart: 2, of which 1 were waited for; matrix products, arithmetic and copies ran while one was open for 4% of the time, Pallas kernels for 0%

profile of v3, /device:TPU:66, one launch (start us, length us, event | category | flops | bytes accessed | tf_op | source)
XLA Modules:
  0.0 162.6 jit_solution(7696376960357239720)
XLA Ops:
  0.6 0.0 copy-start
  0.6 2.4 %shard_map.131 = (f32[200,512]{1,0:T(8,128)}, s32[2,80,128]{2,1,0:T(8,128)}) custom-call(bf16[96,512]{1,0:T(8,128)(2,1)} %features_ref.1, bf16[96,512]{1,0:T(8,128)(2,1)} %grad_ref.1, bf16[512,512]{1,0:T(8,128)(2,1)} %weight_ref.1, s32[1,96]{1,0:T(1,128)} %bitcast.36, s32[3,1,72]{2,1,0:T(1,128)} %bitcast.34, s32[64,72]{1,0:T(8,128)} %bitcast.32, ...), custom_call_target="tpu_custom_call" | custom-call | tf_op jit(solution)/shard_map/pallas_call | solution.py:96
  3.1 2.4 %collective-permute-start = (s32[2,80,128]{2,1,0:T(8,128)}, s32[2,80,128]{2,1,0:T(8,128)S(1)}, u32[]{:S(2)}, u32[]{:S(2)}) collective-permute-start(s32[2,80,128]{2,1,0:T(8,128)} %get-tuple-element.4.own_info.own_ref), channel_id=1, source_target_pairs={{0,16},{16,0},{1,17},{17,1},{2,18},{18,2},{3,19},{19,3},{4,20},{20... | collective-permute-start | bytes 245768 | tf_op jit(solution)/shard_map/ppermute | solution.py:314
  5.5 1.0 convert_element_type.36
  6.6 0.0 copy-start.6
  6.6 56.5 %all-gather.2 = f16[6400,512]{1,0:T(8,128)(2,1)S(1)} all-gather(f16[200,512]{1,0:T(8,128)(2,1)S(1)} %convert_element_type.36), channel_id=2, replica_groups=mesh['z'=16,'xl'=2,'core'=2,'y'=4,'xh'=2] {'z','core'}, dimensions={0}, use_global_device_ids=true | all-gather | bytes 6758400 | tf_op jit(solution)/shard_map/all_gather | solution.py:316
  63.1 0.0 copy-start.1
  63.1 2.7 %copy-done.1 = f16[6400,512]{1,0:T(8,128)(2,1)} copy-done((f16[6400,512]{1,0:T(8,128)(2,1)}, f16[6400,512]{1,0:T(8,128)(2,1)S(1)}, u32[]{:S(2)}) %copy-start.1) | copy-done | bytes 6553624
  65.9 0.1 copy.15
  66.0 0.0 copy-done.6
  66.0 0.1 select_reduce_fusion
  66.1 5.8 %multiply_convert_fusion = (bf16[32,96,512]{2,1,0:T(8,128)(2,1)}, bf16[32,96,512]{2,1,0:T(8,128)(2,1)}) fusion(f16[32,200,512]{2,1,0:T(8,128)(2,1)} %bitcast.29, f32[32]{0:T(128)S(1)} %get-tuple-element.10, f32[32]{0:T(128)S(1)} %get-tuple-element.11), kind=kLoop, calls=%fused_computation | loop fusion | flops 9437184 | bytes 12583168 | tf_op jit(solution)/shard_map/convert_element_type | solution.py:323
  71.9 0.0 collective-permute-done.other_info.other_ref
  71.9 0.0 copy-start.7
  71.9 0.6 copy-done.7
  72.5 19.6 %shard_map.132 = bf16[16,2,96,512]{3,2,1,0:T(8,128)(2,1)} custom-call(s32[1]{0:T(128)} %bitcast.lane_ref, s32[2,80,128]{2,1,0:T(8,128)} %get-tuple-element.4.own_info.own_ref, s32[2,80,128]{2,1,0:T(8,128)} %copy-done.7, s32[2,80,128]{2,1,0:T(8,128)} %get-tuple-element.4.own_info.own_ref, s32[2,80,128]{2,1,0:T(8,128)} %copy-done.7, ...), custom_call_target="tpu_custom_call" | custom-call | flops 16000000000 | bytes 20000000 | tf_op jit(solution)/shard_map/pallas_call | solution.py:264
  92.1 0.0 copy-start.8
  92.1 0.0 copy-start.3
  92.1 0.0 copy-start.5
  92.2 8.8 %all-to-all-start = ((bf16[16,2,96,512]{3,2,1,0:T(8,128)(2,1)}), bf16[16,2,96,512]{3,2,1,0:T(8,128)(2,1)}, u32[]{:S(2)}, u32[]{:S(2)}) async-start(bf16[16,2,96,512]{3,2,1,0:T(8,128)(2,1)} %shard_map.132), calls=%async_computation | async-start | bytes 6291456 | tf_op jit(solution)/shard_map/all_to_all | solution.py:327
  100.9 0.0 copy-done.8
  100.9 0.0 copy-start.4
  101.0 0.0 copy-start.2
  101.0 0.0 copy-done
  101.0 0.0 copy-done.3
  101.0 0.0 copy-done.5
  101.0 0.2 convolution_add_fusion.2
  101.2 57.2 %all-to-all-done = bf16[16,2,96,512]{3,2,1,0:T(8,128)(2,1)} async-done(((bf16[16,2,96,512]{3,2,1,0:T(8,128)(2,1)}), bf16[16,2,96,512]{3,2,1,0:T(8,128)(2,1)}, u32[]{:S(2)}, u32[]{:S(2)}) %all-to-all-start) | async-done | bytes 3145760 | tf_op jit(solution)/shard_map/all_to_all | solution.py:327
  158.4 2.4 %convert_reduce_fusion = (f32[96,512]{1,0:T(8,128)S(1)}, f32[96,512]{1,0:T(8,128)S(1)}) fusion(bf16[16,2,96,512]{3,2,1,0:T(8,128)(2,1)} %all-to-all-done), kind=kLoop, calls=%fused_computation.2 | loop fusion | flops 3047424 | bytes 3538944 | tf_op jit(solution)/shard_map/reduce_sum | solution.py:328
  160.7 0.0 copy-done.4
  160.8 0.9 fusion.2
  161.7 0.0 copy-done.2
  161.7 0.9 fusion.1
  (5 shorter events, 0.1 us)
Async XLA Ops:
  0.6 100.3 %copy-start = (bf16[512,512]{1,0:T(8,128)(2,1)S(1)}, bf16[512,512]{1,0:T(8,128)(2,1)}, u32[]{:S(2)}) copy-start(bf16[512,512]{1,0:T(8,128)(2,1)} %param.14) | copy-start | bytes 1572868
  3.1 68.8 %collective-permute-start = (s32[2,80,128]{2,1,0:T(8,128)}, s32[2,80,128]{2,1,0:T(8,128)S(1)}, u32[]{:S(2)}, u32[]{:S(2)}) collective-permute-start(s32[2,80,128]{2,1,0:T(8,128)} %get-tuple-element.4.own_info.own_ref), channel_id=1, source_target_pairs={{0,16},{16,0},{1,17},{17,1},{2,18},{18,2},{3,19},{19,3},{4,20},{20... | collective-permute-start | bytes 245768 | tf_op jit(solution)/shard_map/ppermute | solution.py:314
  6.6 59.4 %copy-start.6 = (f32[6]{0:T(128)S(1)}, f32[6]{0:T(128)}, u32[]{:S(2)}) copy-start(f32[6]{0:T(128)} %constant.16.clone) | copy-start | bytes 76
  63.1 2.7 %copy-start.1 = (f16[6400,512]{1,0:T(8,128)(2,1)}, f16[6400,512]{1,0:T(8,128)(2,1)S(1)}, u32[]{:S(2)}) copy-start(f16[6400,512]{1,0:T(8,128)(2,1)S(1)} %all-gather.2) | copy-start | bytes 19660804
  71.9 0.6 copy-start.7
  92.1 8.8 %copy-start.8 = (s32[96]{0:T(128)S(1)}, s32[96]{0:T(128)}, u32[]{:S(2)}) copy-start(s32[96]{0:T(128)} %param.13) | copy-start | bytes 1156
  92.1 8.9 %copy-start.3 = (bf16[96,512]{1,0:T(8,128)(2,1)S(1)}, bf16[96,512]{1,0:T(8,128)(2,1)}, u32[]{:S(2)}) copy-start(bf16[96,512]{1,0:T(8,128)(2,1)} %features_ref.1) | copy-start | bytes 294916
  92.1 8.9 %copy-start.5 = (f32[512]{0:T(512)S(1)}, f32[512]{0:T(512)}, u32[]{:S(2)}) copy-start(f32[512]{0:T(512)} %param.16) | copy-start | bytes 6148
  92.2 66.2 %all-to-all-start = ((bf16[16,2,96,512]{3,2,1,0:T(8,128)(2,1)}), bf16[16,2,96,512]{3,2,1,0:T(8,128)(2,1)}, u32[]{:S(2)}, u32[]{:S(2)}) async-start(bf16[16,2,96,512]{3,2,1,0:T(8,128)(2,1)} %shard_map.132), calls=%async_computation | async-start | bytes 6291456 | tf_op jit(solution)/shard_map/all_to_all | solution.py:327
  100.9 59.8 %copy-start.4 = (bf16[96,512]{1,0:T(8,128)(2,1)S(1)}, bf16[96,512]{1,0:T(8,128)(2,1)}, u32[]{:S(2)}) copy-start(bf16[96,512]{1,0:T(8,128)(2,1)} %grad_ref.1) | copy-start | bytes 294916
  101.0 60.7 %copy-start.2 = (bf16[512,512]{1,0:T(8,128)(2,1)S(1)}, bf16[512,512]{1,0:T(8,128)(2,1)}, u32[]{:S(2)}) copy-start(bf16[512,512]{1,0:T(8,128)(2,1)} %weight_ref.1) | copy-start | bytes 1572868

commit v4 on v3

--- a/solution.py
+++ b/solution.py
@@ -1,3 +1,5 @@
+import functools
+
 import jax
 import jax.numpy as jnp
 from jax import lax
@@ -13,7 +15,9 @@
 VMEM = 58 * 1024 * 1024
 PARTS = ("z", "xl", "core", "y", "xh")
 PLANE = ("xl", "y", "xh")
-SHIFTS = (64, 32, 16, 8, 4, 2)
+SHIFTS = (63, 32, 16, 8, 4, 2, 1)
+LARGEST = 32767.0
+TAIL = 16
 
 
 def column_of(row):
@@ -23,16 +27,31 @@
     return jnp.sum(jnp.where(across == down, row, 0.0), axis=1, keepdims=True)
 
 
+def row_of(column):
+    count = column.shape[0]
+    across = lax.broadcasted_iota(jnp.int32, (count, count), 0)
+    down = lax.broadcasted_iota(jnp.int32, (count, count), 1)
+    return jnp.sum(jnp.where(across == down, column, 0.0), axis=0, keepdims=True)
+
+
 def scaled(values):
-    top = jnp.max(jnp.max(jnp.abs(values), axis=1, keepdims=True), axis=0, keepdims=True)
-    scale = jnp.ones_like(top)
-    flags = []
+    top = jnp.max(jnp.abs(values), axis=1, keepdims=True)
+    scale, power = jnp.ones_like(top), jnp.zeros_like(top)
     for shift in SHIFTS:
-        fits = top * 2.0**shift <= 2.0**15
+        fits = top * 2.0**shift <= LARGEST
         factor = jnp.where(fits, 2.0**shift, 1.0)
         top, scale = top * factor, scale * factor
-        flags.append(jnp.where(fits, 1.0, 0.0))
-    return values * scale, flags
+        power += jnp.where(fits, float(shift), 0.0)
+    return jnp.round(values * scale).astype(jnp.int32).astype(jnp.int16), power
+
+
+def undone(power):
+    factor = jnp.ones_like(power)
+    for shift in SHIFTS:
+        has = power >= shift
+        factor = factor * jnp.where(has, 2.0**-shift, 1.0)
+        power = power - jnp.where(has, float(shift), 0.0)
+    return factor
 
 
 def prepare_kernel(
@@ -70,15 +89,15 @@
     )
     degree = column_of(degree_ref[...].astype(jnp.float32))
     mean_grad = (product / degree).astype(jnp.bfloat16).astype(jnp.float32)
-    values, flags = scaled(mean_grad)
+    values, grad_power = scaled(mean_grad)
     sent_ref[:nodes, :] = values
-    values, more = scaled(features_ref[...].astype(jnp.float32))
+    values, feature_power = scaled(features_ref[...].astype(jnp.float32))
     sent_ref[nodes : 2 * nodes, :] = values
-    lanes = lax.broadcasted_iota(jnp.int32, (8, width), 1)
-    tail = jnp.zeros((8, width), jnp.float32)
-    for at, flag in enumerate(flags + more):
-        tail = jnp.where(lanes == at, flag, tail)
-    sent_ref[2 * nodes :, :] = tail
+    lines = lax.broadcasted_iota(jnp.int32, (TAIL, nodes), 0)
+    tail = jnp.where(lines == 0, row_of(grad_power), 0.0)
+    tail = jnp.where(lines == 1, row_of(feature_power), tail)
+    tail = jnp.concatenate([tail, jnp.zeros((TAIL, width - nodes), jnp.float32)], axis=1)
+    sent_ref[2 * nodes :, :] = tail.astype(jnp.int32).astype(jnp.int16)
 
 
 def prepare(features, old_grad, w_neigh, old_degree, tables):
@@ -86,7 +105,7 @@
     slots = tables[0].shape[-1]
     args = (features, old_grad, w_neigh, old_degree, *tables)
     outs = (
-        jax.ShapeDtypeStruct((2 * nodes + 8, width), jnp.float32),
+        jax.ShapeDtypeStruct((2 * nodes + TAIL, width), jnp.int16),
         jax.ShapeDtypeStruct((2, slots + 8, TILE), jnp.int32),
     )
 
@@ -104,54 +123,79 @@
 
 
 def sums_kernel(
+    array,
     lane_ref,
     own_info,
     other_info,
     own_ref,
     other_ref,
-    grads_ref,
-    features_ref,
+    sent_ref,
     out_ref,
     edges,
     dst_rows,
     src_rows,
     counts,
+    raw,
+    tails,
+    factors,
     held,
     total,
     sems,
 ):
-    array, half = pl.program_id(0), pl.program_id(1)
+    half = pl.program_id(0)
     lane = lane_ref[0]
-    planes = grads_ref.shape[0]
+    nodes = out_ref.shape[1]
+    senders = tails.shape[0]
+    planes = senders // 2
     pairs = dst_rows.shape[0]
 
-    def fetches(sources_ref, into):
-        for plane in range(planes):
-            yield pltpu.make_async_copy(
-                sources_ref.at[plane, pl.ds(pl.multiple_of(lane * HALF, HALF), TILE)],
-                held.at[into, pl.ds(plane * TILE, TILE)],
-                sems.at[into, plane],
+    fetches = [
+        pltpu.make_async_copy(
+            sent_ref.at[sender, pl.ds(array * nodes, nodes)],
+            raw.at[pl.ds(sender * nodes, nodes)],
+            sems.at[sender],
+        )
+        for sender in range(senders)
+    ]
+    fetches.append(
+        pltpu.make_async_copy(
+            sent_ref.at[:, pl.ds(2 * nodes, TAIL), pl.ds(0, TILE)], tails, sems.at[senders]
+        )
+    )
+
+    @pl.when(half == 0)
+    def _():
+        for copy in fetches:
+            copy.start()
+        edges[...] = own_ref[...]
+
+    @pl.when(half == 1)
+    def _():
+        edges[...] = other_ref[...]
+
+    def hold():
+        powers = jnp.concatenate([tails[sender, array : array + 1, :] for sender in range(senders)], axis=0)
+        factor = undone(powers.astype(jnp.int32).astype(jnp.float32))
+        factor = jnp.concatenate([factor, jnp.ones((TILE - senders, TILE), jnp.float32)], axis=0).T
+        for sender in range(senders):
+            factors[sender * nodes : (sender + 1) * nodes] = jnp.broadcast_to(
+                factor[:nodes, sender : sender + 1], (nodes, TILE)
             )
-            yield pltpu.make_async_copy(
-                sources_ref.at[plane, pl.ds(pl.multiple_of((1 - lane) * TILE, HALF), HALF)],
-                held.at[into, pl.ds(planes * TILE + plane * HALF, HALF)],
-                sems.at[into, planes + plane],
-            )
-
-    @pl.when((array == 0) & (half == 0))
-    def _():
-        for copy in fetches(grads_ref, 0):
-            copy.start()
-        for copy in fetches(features_ref, 1):
-            copy.start()
-
-    @pl.when(half == 0)
-    def _():
-        edges[...] = own_ref[...]
-
-    @pl.when(half == 1)
-    def _():
-        edges[...] = other_ref[...]
+
+        def move(begin, into, size):
+            rows = pl.ds(pl.multiple_of(begin, HALF), size)
+            values = raw[rows, :].astype(jnp.int32).astype(jnp.float32)
+            times = factors[rows, :]
+            times = jnp.concatenate([times] * (values.shape[1] // TILE), axis=1)
+            held[pl.ds(pl.multiple_of(into, HALF), size), :] = (values * times).astype(jnp.bfloat16)
+
+        def move_plane(plane, carry):
+            begin = plane * 2 * nodes
+            move(begin + lane * HALF, plane * TILE, TILE)
+            move(begin + (1 - lane) * TILE, planes * TILE + plane * HALF, HALF)
+            return carry
+
+        lax.fori_loop(0, planes, move_plane, 0)
 
     lanes = lax.broadcasted_iota(jnp.int32, (pairs, TILE), 1)
     left = lanes < HALF
@@ -214,22 +258,17 @@
 
     def product():
         left_side = jnp.concatenate([counts[at] for at in range(counts.shape[0])], axis=1)
-        return jnp.dot(left_side, held[array], preferred_element_type=jnp.float32)
+        return jnp.dot(left_side, held[...], preferred_element_type=jnp.float32)
 
     peak = jnp.max(build(0, live_pairs, UNROLL).astype(jnp.float32))
 
-    @pl.when((array == 0) & (half == 0))
-    def _():
-        for copy in fetches(grads_ref, 0):
+    @pl.when(half == 0)
+    def _():
+        for copy in fetches:
             copy.wait()
-
-    @pl.when((array == 1) & (half == 0))
-    def _():
-        for copy in fetches(features_ref, 1):
-            copy.wait()
+        hold()
 
     def put(sums):
-        nodes = out_ref.shape[1]
         for at in range(out_ref.shape[0]):
             out_ref[at] = sums[at * nodes : (at + 1) * nodes].astype(jnp.bfloat16)
 
@@ -250,43 +289,43 @@
         put(total[...])
 
 
-def edge_sums(lane, own, other, grads, features, devices, nodes):
+def edge_sums(array, lane, own, other, sent, devices, nodes):
     slots = own.shape[1] - 8
-    planes, height, width = grads.shape
-    depth, rows = planes * height, devices * nodes
-    table = pl.BlockSpec((None, slots, TILE), lambda array, half, _: (1 - array, 0, 0))
+    senders, _, width = sent.shape
+    depth, rows = senders * nodes, devices * nodes
+    table = pl.BlockSpec((None, slots, TILE), lambda half, _: (1 - array, 0, 0))
     info = pl.BlockSpec(
-        (None, 8, TILE),
-        lambda array, half, _: (1 - array, slots // 8, 0),
-        memory_space=pltpu.SMEM,
-    )
-    far = pl.BlockSpec(memory_space=pl.ANY)
+        (None, 8, TILE), lambda half, _: (1 - array, slots // 8, 0), memory_space=pltpu.SMEM
+    )
     return pl.pallas_call(
-        sums_kernel,
-        out_shape=jax.ShapeDtypeStruct((2 * devices, 2, nodes, width), jnp.bfloat16),
+        functools.partial(sums_kernel, array),
+        out_shape=jax.ShapeDtypeStruct((2 * devices, nodes, width), jnp.bfloat16),
         grid_spec=pltpu.PrefetchScalarGridSpec(
             num_scalar_prefetch=1,
-            grid=(2, 2),
-            in_specs=[info, info, table, table, far, far],
+            grid=(2,),
+            in_specs=[info, info, table, table, pl.BlockSpec(memory_space=pl.ANY)],
             out_specs=pl.BlockSpec(
-                (devices, None, nodes, width),
-                lambda array, half, lane: (half + lane[0] - 2 * half * lane[0], array, 0, 0),
+                (devices, nodes, width),
+                lambda half, lane: (half + lane[0] - 2 * half * lane[0], 0, 0),
             ),
             scratch_shapes=[
                 pltpu.VMEM((slots, TILE), jnp.int32),
                 pltpu.VMEM((slots // 2, TILE), jnp.float32),
                 pltpu.VMEM((slots // 2, TILE), jnp.float32),
                 pltpu.VMEM((depth // TILE, rows, TILE), jnp.bfloat16),
-                pltpu.VMEM((2, depth, width), jnp.bfloat16),
+                pltpu.VMEM((depth, width), jnp.int16),
+                pltpu.VMEM((senders, TAIL, TILE), jnp.int16),
+                pltpu.VMEM((depth, TILE), jnp.float32),
+                pltpu.VMEM((depth, width), jnp.bfloat16),
                 pltpu.VMEM((rows, width), jnp.float32),
-                pltpu.SemaphoreType.DMA((2, 2 * planes)),
+                pltpu.SemaphoreType.DMA((senders + 1,)),
             ],
         ),
         compiler_params=pltpu.CompilerParams(vmem_limit_bytes=VMEM),
         cost_estimate=pl.CostEstimate(
-            flops=16 * 10**9, bytes_accessed=20 * 10**6, transcendentals=0
+            flops=8 * 10**9, bytes_accessed=10 * 10**6, transcendentals=0
         ),
-    )(lane, own, other, own, other, grads, features)
+    )(lane, own, other, own, other, sent)
 
 
 def shards(
@@ -313,25 +352,21 @@
     sent, own = prepare(features, old_grad, w_neigh, old_degree[None], tables)
     other = lax.ppermute(own, "xl", [(0, 1), (1, 0)])
 
-    got = lax.all_gather(sent.astype(jnp.float16), ("z", "core"), axis=0, tiled=False)
-    flags = got[:, 2 * nodes, : 2 * len(SHIFTS)].reshape(-1, 2, len(SHIFTS))
-    factors = jnp.array([2.0**-shift for shift in SHIFTS], jnp.float32)
-    undo = jnp.prod(jnp.where(flags > 0, factors, 1.0), axis=-1)
-
-    def sources(at):
-        values = got[:, at * nodes : (at + 1) * nodes].astype(jnp.float32)
-        values = (values * undo[:, at, None, None]).astype(jnp.bfloat16)
-        return values.reshape(-1, 2 * nodes, width)
-
-    partial = edge_sums(lane.reshape(1), own, other, sources(0), sources(1), devices, nodes)
-    parts = lax.all_to_all(partial, PLANE, 0, 0)
-    old_summed = jnp.sum(parts[:, 0].astype(jnp.float32), axis=0)
+    got = lax.all_gather(sent, ("z", "core"), axis=0, tiled=False)
+
+    def sums(array):
+        partial = edge_sums(array, lane.reshape(1), own, other, got, devices, nodes)
+        parts = lax.all_to_all(partial, PLANE, 0, 0)
+        return jnp.sum(parts.astype(jnp.float32), axis=0)
+
+    old_summed = sums(0)
+    summed = sums(1)
+
     self_grad = lax.dot_general(
         old_grad, w_self, (((1,), (1,)), ((), ())), preferred_element_type=jnp.float32
     )
     grad_input = (self_grad + old_summed).astype(jnp.bfloat16)
 
-    summed = jnp.sum(parts[:, 1].astype(jnp.float32), axis=0)
     neighbour_mean = (summed / degree[:, None].astype(jnp.float32)).astype(jnp.bfloat16)
     preact = jnp.dot(features, w_self, preferred_element_type=jnp.float32) + bias_term
     preact = preact + jnp.dot(neighbour_mean, w_neigh, preferred_element_type=jnp.float32)

time: 163 us -> 148 us (0.908)
  the two profiles are of different devices: /device:TPU:66 before, /device:TPU:6 now
where the time goes in v4:
time: 148 us
  blocking collectives  61.1 us (41%)
  waiting for transfers between devices  33 us (22%)
  Pallas kernels  29.5 us (20%)
  starting transfers between devices  18.4 us (12%)
  matrix products  2.08 us (1%)
  other arithmetic  1.87 us (1%)
    all_gather x1, blocking collectives, shards(): got = lax.all_gather(sent, ('z', 'core'), axis=0, tiled=False)  61.1 us
    all_to_all x2, waiting for transfers between devices, sums(): parts = lax.all_to_all(partial, PLANE, 0, 0)  33 us
    pallas_call x2, Pallas kernels, edge_sums(): pl.pallas_call(functools.partial(sums_kernel, array), out_shape=jax.Shape...  27 us
    all_to_all x2, starting transfers between devices, sums(): parts = lax.all_to_all(partial, PLANE, 0, 0)  15.7 us
  transfers between devices with their start and end apart: 3, of which 2 were waited for; matrix products, arithmetic and copies ran while one was open for 1% of the time, Pallas kernels for 9%

profile of v4, /device:TPU:6, one launch (start us, length us, event | category | flops | bytes accessed | tf_op | source)
XLA Modules:
  0.0 147.9 jit_solution(17143264723928767952)
XLA Ops:
  0.6 0.0 copy-start
  0.6 2.5 %shard_map.122 = (s16[208,512]{1,0:T(8,128)(2,1)}, s32[2,80,128]{2,1,0:T(8,128)}) custom-call(bf16[96,512]{1,0:T(8,128)(2,1)} %features_ref.1, bf16[96,512]{1,0:T(8,128)(2,1)} %grad_ref.1, bf16[512,512]{1,0:T(8,128)(2,1)} %weight_ref.1, s32[1,96]{1,0:T(1,128)} %bitcast.26, s32[3,1,72]{2,1,0:T(1,128)} %bitcast.24, s32[64,72]{1,0:T(8,128)} %bitcast.22, ...), custom_call_target="tpu_custom_call" | custom-call | tf_op jit(solution)/shard_map/pallas_call | solution.py:115
  3.2 2.7 %collective-permute-start = (s32[2,80,128]{2,1,0:T(8,128)}, s32[2,80,128]{2,1,0:T(8,128)S(1)}, u32[]{:S(2)}, u32[]{:S(2)}) collective-permute-start(s32[2,80,128]{2,1,0:T(8,128)} %get-tuple-element.4.own_info.own_ref), channel_id=1, source_target_pairs={{0,16},{16,0},{1,17},{17,1},{2,18},{18,2},{3,19},{19,3},{4,20},{20... | collective-permute-start | bytes 245768 | tf_op jit(solution)/shard_map/ppermute | solution.py:353
  5.9 61.1 %all-gather.2 = s16[6656,512]{1,0:T(8,128)(2,1)} all-gather(s16[208,512]{1,0:T(8,128)(2,1)} %get-tuple-element.5), channel_id=2, replica_groups=mesh['z'=16,'xl'=2,'core'=2,'y'=4,'xh'=2] {'z','core'}, dimensions={0}, use_global_device_ids=true | all-gather | bytes 7028736 | tf_op jit(solution)/shard_map/all_gather | solution.py:355
  67.0 0.0 collective-permute-done.other_info.other_ref
  67.0 0.0 copy-start.5
  67.0 0.6 copy-done.5
  67.7 13.5 %shard_map.124 = bf16[16,96,512]{2,1,0:T(8,128)(2,1)} custom-call(s32[1]{0:T(128)} %bitcast.lane_ref, s32[2,80,128]{2,1,0:T(8,128)} %get-tuple-element.4.own_info.own_ref, s32[2,80,128]{2,1,0:T(8,128)} %copy-done.5, s32[2,80,128]{2,1,0:T(8,128)} %get-tuple-element.4.own_info.own_ref, s32[2,80,128]{2,1,0:T(8,128)} %copy-done.5, s16[32,208,512]{2,1,0:T(8,128)(2,1)} %bitcast.20), custom_call_target="tpu_custom_call" | custom-call | flops 8000000000 | bytes 10000000 | tf_op jit(solution)/shard_map/pallas_call | solution.py:300
  81.2 6.7 %all-to-all-start.1 = ((bf16[16,96,512]{2,1,0:T(8,128)(2,1)}), bf16[16,96,512]{2,1,0:T(8,128)(2,1)S(1)}, u32[]{:S(2)}, u32[]{:S(2)}) async-start(bf16[16,96,512]{2,1,0:T(8,128)(2,1)} %shard_map.124), calls=%async_computation.1 | async-start | bytes 3145728 | tf_op jit(solution)/shard_map/all_to_all | solution.py:359
  87.9 13.5 %shard_map.123 = bf16[16,96,512]{2,1,0:T(8,128)(2,1)} custom-call(s32[1]{0:T(128)} %bitcast.lane_ref, s32[2,80,128]{2,1,0:T(8,128)} %get-tuple-element.4.own_info.own_ref, s32[2,80,128]{2,1,0:T(8,128)} %copy-done.5, s32[2,80,128]{2,1,0:T(8,128)} %get-tuple-element.4.own_info.own_ref, s32[2,80,128]{2,1,0:T(8,128)} %copy-done.5, s16[32,208,512]{2,1,0:T(8,128)(2,1)} %bitcast.21), custom_call_target="tpu_custom_call" | custom-call | flops 8000000000 | bytes 10000000 | tf_op jit(solution)/shard_map/pallas_call | solution.py:300
  101.3 0.0 copy-start.6
  101.3 0.0 copy-start.2
  101.4 0.0 copy-start.4
  101.4 11.1 %all-to-all-done.1 = bf16[16,96,512]{2,1,0:T(8,128)(2,1)S(1)} async-done(((bf16[16,96,512]{2,1,0:T(8,128)(2,1)}), bf16[16,96,512]{2,1,0:T(8,128)(2,1)S(1)}, u32[]{:S(2)}, u32[]{:S(2)}) %all-to-all-start.1) | async-done | bytes 1572896 | tf_op jit(solution)/shard_map/all_to_all | solution.py:359
  112.4 9.0 %all-to-all-start = ((bf16[16,96,512]{2,1,0:T(8,128)(2,1)}), bf16[16,96,512]{2,1,0:T(8,128)(2,1)}, u32[]{:S(2)}, u32[]{:S(2)}) async-start(bf16[16,96,512]{2,1,0:T(8,128)(2,1)} %shard_map.123), calls=%async_computation | async-start | bytes 3145728 | tf_op jit(solution)/shard_map/all_to_all | solution.py:359
  121.5 0.0 copy-done.6
  121.5 0.0 copy-start.3
  121.5 0.0 copy-done
  121.5 0.0 copy-done.2
  121.5 0.0 copy-done.4
  121.5 0.2 convolution_add_fusion.2
  121.7 0.2 convert_reduce_fusion
  122.0 0.4 copy-done.3
  122.4 0.0 copy-start.1
  122.4 0.9 fusion.2
  123.3 22.0 %all-to-all-done = bf16[16,96,512]{2,1,0:T(8,128)(2,1)} async-done(((bf16[16,96,512]{2,1,0:T(8,128)(2,1)}), bf16[16,96,512]{2,1,0:T(8,128)(2,1)}, u32[]{:S(2)}, u32[]{:S(2)}) %all-to-all-start) | async-done | bytes 1572896 | tf_op jit(solution)/shard_map/all_to_all | solution.py:359
  145.3 1.6 %convert_reduce_fusion.1 = f32[96,512]{1,0:T(8,128)S(1)} fusion(bf16[16,96,512]{2,1,0:T(8,128)(2,1)} %all-to-all-done), kind=kLoop, calls=%fused_computation.1 | loop fusion | flops 1523712 | bytes 1769472 | tf_op jit(solution)/shard_map/reduce_sum | solution.py:360
  146.9 0.0 copy-done.1
  146.9 0.9 fusion.1
  (1 shorter events, 0.0 us)
Async XLA Ops:
  0.6 120.9 %copy-start = (bf16[512,512]{1,0:T(8,128)(2,1)S(1)}, bf16[512,512]{1,0:T(8,128)(2,1)}, u32[]{:S(2)}) copy-start(bf16[512,512]{1,0:T(8,128)(2,1)} %param.13) | copy-start | bytes 1572868
  3.2 63.9 %collective-permute-start = (s32[2,80,128]{2,1,0:T(8,128)}, s32[2,80,128]{2,1,0:T(8,128)S(1)}, u32[]{:S(2)}, u32[]{:S(2)}) collective-permute-start(s32[2,80,128]{2,1,0:T(8,128)} %get-tuple-element.4.own_info.own_ref), channel_id=1, source_target_pairs={{0,16},{16,0},{1,17},{17,1},{2,18},{18,2},{3,19},{19,3},{4,20},{20... | collective-permute-start | bytes 245768 | tf_op jit(solution)/shard_map/ppermute | solution.py:353
  67.0 0.6 copy-start.5
  81.2 31.3 %all-to-all-start.1 = ((bf16[16,96,512]{2,1,0:T(8,128)(2,1)}), bf16[16,96,512]{2,1,0:T(8,128)(2,1)S(1)}, u32[]{:S(2)}, u32[]{:S(2)}) async-start(bf16[16,96,512]{2,1,0:T(8,128)(2,1)} %shard_map.124), calls=%async_computation.1 | async-start | bytes 3145728 | tf_op jit(solution)/shard_map/all_to_all | solution.py:359
  101.3 20.1 %copy-start.6 = (s32[96]{0:T(128)S(1)}, s32[96]{0:T(128)}, u32[]{:S(2)}) copy-start(s32[96]{0:T(128)} %param.12) | copy-start | bytes 1156
  101.3 20.2 %copy-start.2 = (bf16[96,512]{1,0:T(8,128)(2,1)S(1)}, bf16[96,512]{1,0:T(8,128)(2,1)}, u32[]{:S(2)}) copy-start(bf16[96,512]{1,0:T(8,128)(2,1)} %features_ref.1) | copy-start | bytes 294916
  101.4 20.2 %copy-start.4 = (f32[512]{0:T(512)S(1)}, f32[512]{0:T(512)}, u32[]{:S(2)}) copy-start(f32[512]{0:T(512)} %param.15) | copy-start | bytes 6148
  112.4 32.8 %all-to-all-start = ((bf16[16,96,512]{2,1,0:T(8,128)(2,1)}), bf16[16,96,512]{2,1,0:T(8,128)(2,1)}, u32[]{:S(2)}, u32[]{:S(2)}) async-start(bf16[16,96,512]{2,1,0:T(8,128)(2,1)} %shard_map.123), calls=%async_computation | async-start | bytes 3145728 | tf_op jit(solution)/shard_map/all_to_all | solution.py:359
  121.5 0.9 copy-start.3
  122.4 24.6 %copy-start.1 = (bf16[512,512]{1,0:T(8,128)(2,1)S(1)}, bf16[512,512]{1,0:T(8,128)(2,1)}, u32[]{:S(2)}) copy-start(bf16[512,512]{1,0:T(8,128)(2,1)} %weight_ref.1) | copy-start | bytes 1572868

commit v5 on v4

v5 whole, which is shorter than its diff:
```python
import jax
import jax.numpy as jnp
from jax import lax
from jax.experimental import pallas as pl
from jax.experimental.pallas import tpu as pltpu
from jax.sharding import Mesh
from jax.sharding import PartitionSpec as P

TILE = 128
HALF = TILE // 2
UNROLL = 12
EXACT = 256
VMEM = 58 * 1024 * 1024
PARTS = ("z", "xl", "core", "y", "xh")
PLANE = ("xl", "y", "xh")
SHIFTS = (63, 32, 16, 8, 4, 2, 1)
LARGEST = 32767.0
TAIL = 16


def column_of(row):
    count = row.shape[1]
    across = lax.broadcasted_iota(jnp.int32, (count, count), 0)
    down = lax.broadcasted_iota(jnp.int32, (count, count), 1)
    return jnp.sum(jnp.where(across == down, row, 0.0), axis=1, keepdims=True)


def row_of(column):
    count = column.shape[0]
    across = lax.broadcasted_iota(jnp.int32, (count, count), 0)
    down = lax.broadcasted_iota(jnp.int32, (count, count), 1)
    return jnp.sum(jnp.where(across == down, column, 0.0), axis=0, keepdims=True)


def scaled(values):
    top = jnp.max(jnp.abs(values), axis=1, keepdims=True)
    scale, power = jnp.ones_like(top), jnp.zeros_like(top)
    for shift in SHIFTS:
        fits = top * 2.0**shift <= LARGEST
        factor = jnp.where(fits, 2.0**shift, 1.0)
        top, scale = top * factor, scale * factor
        power += jnp.where(fits, float(shift), 0.0)
    return jnp.round(values * scale).astype(jnp.int32).astype(jnp.int16), power


def undone(power):
    factor = jnp.ones_like(power)
    for shift in SHIFTS:
        has = power >= shift
        factor = factor * jnp.where(has, 2.0**-shift, 1.0)
        power = power - jnp.where(has, float(shift), 0.0)
    return factor


def prepare_kernel(
    features_ref,
    grad_ref,
    weight_ref,
    degree_ref,
    index_ref,
    edges_ref,
    old_index_ref,
    old_edges_ref,
    sent_ref,
    slots_ref,
):
    nodes, width = grad_ref.shape
    for at, (index, edges) in enumerate(
        ((index_ref, edges_ref), (old_index_ref, old_edges_ref))
    ):
        fields, _, slots = index.shape
        numbers = jnp.concatenate([edges[...]] + [index[field] for field in range(fields)], axis=0)
        numbers = jnp.concatenate(
            [numbers, jnp.zeros((TILE - HALF - fields, slots), jnp.int32)], axis=0
        )
        numbers = jnp.concatenate(
            [numbers, jnp.zeros((TILE, TILE - slots), jnp.int32)], axis=1
        )
        slots_ref[at, :slots, :] = numbers.astype(jnp.float32).T[:slots].astype(jnp.int32)
        slots_ref[at, slots:, :] = numbers[HALF : HALF + 8, :]

    product = lax.dot_general(
        grad_ref[...],
        weight_ref[...],
        (((1,), (1,)), ((), ())),
        preferred_element_type=jnp.float32,
    )
    degree = column_of(degree_ref[...].astype(jnp.float32))
    mean_grad = (product / degree).astype(jnp.bfloat16).astype(jnp.float32)
    values, grad_power = scaled(mean_grad)
    sent_ref[:nodes, :] = values
    values, feature_power = scaled(features_ref[...].astype(jnp.float32))
    sent_ref[nodes : 2 * nodes, :] = values
    lines = lax.broadcasted_iota(jnp.int32, (TAIL, nodes), 0)
    tail = jnp.where(lines == 0, row_of(grad_power), 0.0)
    tail = jnp.where(lines == 1, row_of(feature_power), tail)
    tail = jnp.concatenate([tail, jnp.zeros((TAIL, width - nodes), jnp.float32)], axis=1)
    sent_ref[2 * nodes :, :] = tail.astype(jnp.int32).astype(jnp.int16)


def prepare(features, old_grad, w_neigh, old_degree, tables):
    nodes, width = features.shape
    slots = tables[0].shape[-1]
    args = (features, old_grad, w_neigh, old_degree, *tables)
    outs = (
        jax.ShapeDtypeStruct((2 * nodes + TAIL, width), jnp.int16),
        jax.ShapeDtypeStruct((2, slots + 8, TILE), jnp.int32),
    )

    def whole(arg):
        return pl.BlockSpec(arg.shape, lambda _: (0,) * len(arg.shape))

    return pl.pallas_call(
        prepare_kernel,
        out_shape=outs,
        grid=(1,),
        in_specs=[whole(arg) for arg in args],
        out_specs=tuple(whole(out) for out in outs),
        compiler_params=pltpu.CompilerParams(vmem_limit_bytes=VMEM),
    )(*args)


def sums_kernel(
    lane_ref,
    new_own_info,
    new_other_info,
    old_own_info,
    old_other_info,
    own_ref,
    other_ref,
    sent_ref,
    out_ref,
    dst_rows,
    src_rows,
    counts,
    raw,
    tails,
    factors,
    held,
    total,
    wide,
    sems,
):
    lane = lane_ref[0]
    devices, nodes = out_ref.shape[0] // 2, out_ref.shape[2]
    senders = tails.shape[0]
    planes = senders // 2
    slots = own_ref.shape[1] - 8
    pairs = slots // 2
    infos = ((old_own_info, old_other_info), (new_own_info, new_other_info))

    tail_fetch = pltpu.make_async_copy(
        sent_ref.at[:, pl.ds(2 * nodes, TAIL), pl.ds(0, TILE)], tails, sems.at[2 * senders]
    )
    fetches = [
        [
            pltpu.make_async_copy(
                sent_ref.at[sender, pl.ds(array * nodes, nodes)],
                raw.at[array, pl.ds(sender * nodes, nodes)],
                sems.at[array * senders + sender],
            )
            for sender in range(senders)
        ]
        for array in range(2)
    ]
    tail_fetch.start()
    for copy in fetches[0] + fetches[1]:
        copy.start()

    def hold(array):
        powers = [tails[sender, array : array + 1, :] for sender in range(senders)]
        powers = jnp.concatenate(powers, axis=0).astype(jnp.int32).astype(jnp.float32)
        rest = jnp.ones((TILE - senders, TILE), jnp.float32)
        factor = jnp.concatenate([undone(powers), rest], axis=0).T
        for sender in range(senders):
            factors[sender * nodes : (sender + 1) * nodes] = jnp.broadcast_to(
                factor[:nodes, sender : sender + 1], (nodes, TILE)
            )

        def move(begin, into, size):
            rows = pl.ds(pl.multiple_of(begin, HALF), size)
            values = raw[array, rows, :].astype(jnp.int32).astype(jnp.float32)
            times = factors[rows, :]
            times = jnp.concatenate([times] * (values.shape[1] // TILE), axis=1)
            rows = pl.ds(pl.multiple_of(into, HALF), size)
            held[rows, :] = (values * times).astype(jnp.bfloat16)

        def move_plane(plane, carry):
            begin = plane * 2 * nodes
            move(begin + lane * HALF, plane * TILE, TILE)
            move(begin + (1 - lane) * TILE, planes * TILE + plane * HALF, HALF)
            return carry

        lax.fori_loop(0, planes, move_plane, 0)

    lanes = lax.broadcasted_iota(jnp.int32, (pairs, TILE), 1)
    left = lanes < HALF

    def plan(at, edges):
        even, odd = edges[pl.ds(0, pairs, 2), :], edges[pl.ds(1, pairs, 2), :]

        def field(at):
            return jnp.where(left, even[:, at : at + 1], odd[:, at : at + 1])

        values = jnp.where(left, even, pltpu.roll(odd, HALF, 1))
        column, count = field(HALF + 1), field(HALF + 2)
        plane = (column * 43) >> 7
        part = column - 3 * plane
        source = values & (TILE - 1)
        whole = part == 2 * lane
        own = whole | ((part == 1) & ((source >> 6) == lane))
        own &= (lanes & (HALF - 1)) < count
        place = jnp.where(whole, source, (source & (HALF - 1)) + (plane & 1) * HALF)
        place += jnp.where(left, 0, TILE)
        dst_rows[at] = jnp.where(own, values >> 7, -1).astype(jnp.float32)
        src_rows[at] = jnp.where(own, place, -1).astype(jnp.float32)
        return jnp.sum((even[:, HALF + 2 : HALF + 3] > 0).astype(jnp.int32))

    dst_ids = lax.broadcasted_iota(jnp.int32, (TILE, TILE), 0).astype(jnp.bfloat16)
    src_ids = lax.broadcasted_iota(jnp.int32, (2 * TILE, TILE), 0).astype(jnp.bfloat16)
    zero, unit = jnp.bfloat16(0), jnp.bfloat16(1)

    def spot(info, slot):
        row, column = info[0, slot], info[1, slot]
        plane = (column * 43) >> 7
        block = jnp.where(column - 3 * plane == 2 * lane, plane, planes + (plane >> 1))
        return block, pl.ds(pl.multiple_of(row * TILE, TILE), TILE)

    def pair_counts(at, pair):
        dst = dst_rows[at, pl.ds(pair, 1), :].astype(jnp.bfloat16)
        src = src_rows[at, pl.ds(pair, 1), :].astype(jnp.bfloat16)
        dst_hot = jnp.where(dst_ids == dst, unit, zero)
        src_hot = jnp.where(src_ids == src, unit, zero)
        return lax.dot_general(
            dst_hot, src_hot, (((1,), (1,)), ((), ())), preferred_element_type=jnp.float32
        ).astype(jnp.bfloat16)

    def build(at, info, first, last, unroll):
        counts[at] = jnp.zeros(counts.shape[1:], jnp.bfloat16)

        def add(turn, peak):
            found = [first + turn * unroll + pair for pair in range(unroll)]
            added = [pair_counts(at, pair) for pair in found]
            for pair, both in zip(found, added):
                for side in range(2):
                    block, rows = spot(info, 2 * pair + side)
                    sums = counts[at, block, rows, :]
                    sums = sums + both[:, side * TILE : (side + 1) * TILE]
                    counts[at, block, rows, :] = sums
                    peak = jnp.maximum(peak, sums)
            return peak

        start = jnp.zeros((TILE, TILE), jnp.bfloat16)
        return lax.fori_loop(0, pl.cdiv(last - first, unroll), add, start)

    def product(at):
        left_side = jnp.concatenate([counts[at, block] for block in range(counts.shape[1])], axis=1)
        return jnp.dot(left_side, held[...], preferred_element_type=jnp.float32)

    def put(array, half):
        where = half + lane - 2 * half * lane
        at = 2 * array + half
        return [
            pltpu.make_async_copy(
                total.at[at, pl.ds(device * nodes, nodes)],
                out_ref.at[where * devices + device, array],
                sems.at[2 * senders + 1 + at * devices + device],
            )
            for device in range(devices)
        ]

    peaks = []
    for array in range(2):
        for half, edges in enumerate((own_ref, other_ref)):
            at = 2 * array + half
            live_pairs = plan(at, edges.at[1 - array])
            peaks.append(build(at, infos[array][half], 0, live_pairs, UNROLL))
    tail_fetch.wait()
    for array in range(2):
        for copy in fetches[array]:
            copy.wait()
        hold(array)
        for half in range(2):
            at = 2 * array + half
            peak = jnp.max(peaks[at].astype(jnp.float32))

            @pl.when(peak < EXACT)
            def _(at=at):
                total[at] = product(at).astype(jnp.bfloat16)

            @pl.when(peak >= EXACT)
            def _(at=at, info=infos[array][half]):
                wide[...] = jnp.zeros_like(wide)

                def some(turn, carry):
                    build(at, info, 2 * turn, 2 * turn + 2, 2)
                    wide[...] += product(at)
                    return carry

                lax.fori_loop(0, pairs // 2, some, 0)
                total[at] = wide[...].astype(jnp.bfloat16)

            for copy in put(array, half):
                copy.start()
    for array in range(2):
        for half in range(2):
            for copy in put(array, half):
                copy.wait()


def edge_sums(lane, own, other, sent, devices, nodes):
    slots = own.shape[1] - 8
    senders, _, width = sent.shape
    depth, rows = senders * nodes, devices * nodes
    table = pl.BlockSpec(own.shape, lambda _, lane: (0, 0, 0))

    def info(graph):
        return pl.BlockSpec(
            (None, 8, TILE), lambda _, lane: (graph, slots // 8, 0), memory_space=pltpu.SMEM
        )

    far = pl.BlockSpec(memory_space=pl.ANY)
    return pl.pallas_call(
        sums_kernel,
        out_shape=jax.ShapeDtypeStruct((2 * devices, 2, nodes, width), jnp.bfloat16),
        grid_spec=pltpu.PrefetchScalarGridSpec(
            num_scalar_prefetch=1,
            grid=(1,),
            in_specs=[info(0), info(0), info(1), info(1), table, table, far],
            out_specs=far,
            scratch_shapes=[
                pltpu.VMEM((4, slots // 2, TILE), jnp.float32),
                pltpu.VMEM((4, slots // 2, TILE), jnp.float32),
                pltpu.VMEM((4, depth // TILE, rows, TILE), jnp.bfloat16),
                pltpu.VMEM((2, depth, width), jnp.int16),
                pltpu.VMEM((senders, TAIL, TILE), jnp.int16),
                pltpu.VMEM((depth, TILE), jnp.float32),
                pltpu.VMEM((depth, width), jnp.bfloat16),
                pltpu.VMEM((4, rows, width), jnp.bfloat16),
                pltpu.VMEM((rows, width), jnp.float32),
                pltpu.SemaphoreType.DMA((2 * senders + 1 + 4 * devices,)),
            ],
        ),
        compiler_params=pltpu.CompilerParams(vmem_limit_bytes=VMEM),
        cost_estimate=pl.CostEstimate(
            flops=16 * 10**9, bytes_accessed=20 * 10**6, transcendentals=0
        ),
    )(lane, own, other, own, other, own, other, sent)


def finish_kernel(
    parts_ref,
    features_ref,
    grad_ref,
    self_ref,
    neigh_ref,
    bias_ref,
    degree_ref,
    out_ref,
    grad_out_ref,
    parts,
    sems,
):
    senders = parts.shape[0]
    fetches = [
        pltpu.make_async_copy(parts_ref.at[sender], parts.at[sender], sems.at[sender])
        for sender in range(senders)
    ]
    for copy in fetches:
        copy.start()
    own_grad = lax.dot_general(
        grad_ref[...], self_ref[...], (((1,), (1,)), ((), ())), preferred_element_type=jnp.float32
    )
    own_out = jnp.dot(features_ref[...], self_ref[...], preferred_element_type=jnp.float32)
    degree = column_of(degree_ref[...].astype(jnp.float32))
    for copy in fetches:
        copy.wait()

    def summed(array):
        sums = parts[0, array].astype(jnp.float32)
        for sender in range(1, senders):
            sums += parts[sender, array].astype(jnp.float32)
        return sums

    mean = (summed(1) / degree).astype(jnp.bfloat16)
    grad_out_ref[...] = (own_grad + summed(0)).astype(jnp.bfloat16)
    preact = jnp.dot(mean, neigh_ref[...], preferred_element_type=jnp.float32)
    preact = own_out + preact + bias_ref[...]
    out_ref[...] = jnp.maximum(preact, 0.0).astype(jnp.bfloat16)


def finish(parts, features, old_grad, w_self, w_neigh, bias_term, degree):
    args = (features, old_grad, w_self, w_neigh, bias_term, degree)
    out = jax.ShapeDtypeStruct(features.shape, jnp.bfloat16)

    def whole(arg):
        return pl.BlockSpec(arg.shape, lambda _: (0,) * len(arg.shape))

    return pl.pallas_call(
        finish_kernel,
        out_shape=(out, out),
        grid=(1,),
        in_specs=[pl.BlockSpec(memory_space=pl.ANY)] + [whole(arg) for arg in args],
        out_specs=(whole(out), whole(out)),
        scratch_shapes=[
            pltpu.VMEM(parts.shape, jnp.bfloat16),
            pltpu.SemaphoreType.DMA((parts.shape[0],)),
        ],
        compiler_params=pltpu.CompilerParams(vmem_limit_bytes=VMEM),
    )(parts, *args)


def shards(
    features,
    degree,
    w_self,
    w_neigh,
    bias_term,
    tile_index,
    tile_edges,
    old_grad,
    old_degree,
    old_index,
    old_edges,
):
    nodes, width = features.shape
    devices = lax.axis_size("y") * lax.axis_size("xh")
    lane = lax.axis_index("xl")

    tables = []
    for index, edges in ((tile_index, tile_edges), (old_index, old_edges)):
        tables.append(jnp.transpose(index[0], (2, 0, 1)))
        tables.append(edges[0, 0].T)
    sent, own = prepare(features, old_grad, w_neigh, old_degree[None], tables)
    other = lax.ppermute(own, "xl", [(0, 1), (1, 0)])

    got = lax.all_gather(sent, ("z", "core"), axis=0, tiled=False)

    partial = edge_sums(lane.reshape(1), own, other, got, devices, nodes)
    parts = lax.all_to_all(partial, PLANE, 0, 0)
    return finish(parts, features, old_grad, w_self, w_neigh, bias_term[None], degree[None])


def solution(mesh):
    parts = Mesh(mesh.devices.reshape(16, 2, 2, 4, 2), PARTS)
    block = ("z", "xl", "core")
    side = ("y", "xh")
    in_specs = (
        P(PARTS, None),
        P(PARTS),
        P(),
        P(),
        P(),
        P(block, side, None, None),
        P(block, side, None, None),
        P(PARTS, None),
        P(PARTS),
        P(block, side, None, None),
        P(block, side, None, None),
    )
    out_specs = (P(PARTS, None), P(PARTS, None))
    return jax.shard_map(
        shards, mesh=parts, in_specs=in_specs, out_specs=out_specs, check_vma=False
    )
```

time: 148 us -> 143 us (0.966)
  blocking collectives: 61.1 us -> 108 us
  waiting for transfers between devices: 33 us -> 0.01 us
  starting transfers between devices: 18.4 us -> 2.72 us
  matrix products: 2.08 us -> 0 us
  other arithmetic: 1.87 us -> 0 us
    all_to_all x0 -> x1, blocking collectives: none -> 46.5 us  [shards(): parts = lax.all_to_all(partial, PLANE, 0, 0)]
    all_to_all x2 -> x0, waiting for transfers between devices: 33 us -> none  [sums(): parts = lax.all_to_all(partial, PLANE, 0, 0)]
    all_to_all x2 -> x0, starting transfers between devices: 15.7 us -> none  [sums(): parts = lax.all_to_all(partial, PLANE, 0, 0)]
    dot_general x3 -> x0, matrix products: 2.08 us -> none  [the longest x1 0.94 us: shards(): lax.dot_general(old_grad, w_self, (((1,), (1,)), ((), ())), preferred_ele...]
    reduce_sum x2 -> x0, other arithmetic: 1.87 us -> none  [sums(): return jnp.sum(parts.astype(jnp.float32), axis=0)]
  transfers between devices with their start and end apart: 3 -> 1, of which waited for: 2 -> 0; matrix products, arithmetic and copies ran while one was open for 1% -> 0% of each run, Pallas kernels for 9% -> 0%
where the time goes in v5:
time: 143 us; the launch traced here: 142 us
  blocking collectives  108 us (76%)
  Pallas kernels  30.4 us (21%)
  starting transfers between devices  2.72 us (2%)
    all_gather x1, blocking collectives, shards(): got = lax.all_gather(sent, ('z', 'core'), axis=0, tiled=False)  61.1 us
    all_to_all x1, blocking collectives, shards(): parts = lax.all_to_all(partial, PLANE, 0, 0)  46.5 us
    pallas_call x1, Pallas kernels, edge_sums(): pl.pallas_call(sums_kernel, out_shape=jax.ShapeDtypeStruct((2 * devices,...  23.2 us
    pallas_call x1, Pallas kernels, finish(): pl.pallas_call(finish_kernel, out_shape=(out, out), grid=(1,), in_specs=[...  4.7 us
  transfers between devices with their start and end apart: 1, of which 0 were waited for; matrix products, arithmetic and copies ran while one was open for 0% of the time, Pallas kernels for 0%

profile of v5, /device:TPU:6, one launch (start us, length us, event | category | flops | bytes accessed | tf_op | source)
XLA Modules:
  0.0 142.2 jit_solution(13377390309180960874)
XLA Ops:
  0.6 2.5 %shard_map.122 = (s16[208,512]{1,0:T(8,128)(2,1)}, s32[2,80,128]{2,1,0:T(8,128)}) custom-call(bf16[96,512]{1,0:T(8,128)(2,1)} %features_ref.3, bf16[96,512]{1,0:T(8,128)(2,1)} %grad_ref.3, bf16[512,512]{1,0:T(8,128)(2,1)} %neigh_ref.1, s32[1,96]{1,0:T(1,128)} %bitcast.24, s32[3,1,72]{2,1,0:T(1,128)} %bitcast.21, s32[64,72]{1,0:T(8,128)} %bitcast.18, ...), custom_call_target="tpu_custom_call" | custom-call | tf_op jit(solution)/shard_map/pallas_call | solution.py:113
  3.1 2.7 %collective-permute-start = (s32[2,80,128]{2,1,0:T(8,128)}, s32[2,80,128]{2,1,0:T(8,128)S(1)}, u32[]{:S(2)}, u32[]{:S(2)}) collective-permute-start(s32[2,80,128]{2,1,0:T(8,128)} %get-tuple-element.4.new_own_info.old_own_info.own_ref), channel_id=1, source_target_pairs={{0,16},{16,0},{1,17},{17,1},{2,18},{18,2},{3,19},{19,3},{4,20},{20... | collective-permute-start | bytes 245768 | tf_op jit(solution)/shard_map/ppermute | solution.py:435
  5.8 61.1 %all-gather.2 = s16[6656,512]{1,0:T(8,128)(2,1)} all-gather(s16[208,512]{1,0:T(8,128)(2,1)} %get-tuple-element.5), channel_id=2, replica_groups=mesh['z'=16,'xl'=2,'core'=2,'y'=4,'xh'=2] {'z','core'}, dimensions={0}, use_global_device_ids=true | all-gather | bytes 7028736 | tf_op jit(solution)/shard_map/all_gather | solution.py:437
  67.0 0.0 collective-permute-done.new_other_info.old_other_info.other_ref
  67.0 0.0 copy-start
  67.0 0.6 copy-done
  67.6 23.2 %shard_map.123 = bf16[16,2,96,512]{3,2,1,0:T(8,128)(2,1)} custom-call(s32[1]{0:T(128)} %bitcast.lane_ref, s32[2,80,128]{2,1,0:T(8,128)} %get-tuple-element.4.new_own_info.old_own_info.own_ref, s32[2,80,128]{2,1,0:T(8,128)} %copy-done, s32[2,80,128]{2,1,0:T(8,128)} %get-tuple-element.4.new_own_info.old_own_info.own_ref, s32[2,80,128]{2,1,0:T(8,128)} %copy-done, ...), custom_call_target="tpu_custom_call" | custom-call | flops 16000000000 | bytes 20000000 | tf_op jit(solution)/shard_map/pallas_call | solution.py:323
  90.8 46.5 %all_to_all.5.parts_ref = bf16[16,2,96,512]{3,2,1,0:T(8,128)(2,1)} all-to-all(bf16[16,2,96,512]{3,2,1,0:T(8,128)(2,1)} %shard_map.123), channel_id=1, replica_groups=mesh['z'=16,'xl'=2,'core'=2,'y'=4,'xh'=2] {'xl','y','xh'}, dimensions={0} | all-to-all | bytes 6291456 | tf_op jit(solution)/shard_map/all_to_all | solution.py:440
  137.3 4.7 %shard_map.124 = (bf16[96,512]{1,0:T(8,128)(2,1)}, bf16[96,512]{1,0:T(8,128)(2,1)}) custom-call(bf16[16,2,96,512]{3,2,1,0:T(8,128)(2,1)} %all_to_all.5.parts_ref, bf16[96,512]{1,0:T(8,128)(2,1)} %features_ref.3, bf16[96,512]{1,0:T(8,128)(2,1)} %grad_ref.3, bf16[512,512]{1,0:T(8,128)(2,1)} %self_ref.1, bf16[512,512]{1,0:T(8,128)(2,1)} %neigh_ref.1, ...), custom_call_target="tpu_custom_call" | custom-call | tf_op jit(solution)/shard_map/pallas_call | solution.py:399
Async XLA Ops:
  3.1 63.9 %collective-permute-start = (s32[2,80,128]{2,1,0:T(8,128)}, s32[2,80,128]{2,1,0:T(8,128)S(1)}, u32[]{:S(2)}, u32[]{:S(2)}) collective-permute-start(s32[2,80,128]{2,1,0:T(8,128)} %get-tuple-element.4.new_own_info.old_own_info.own_ref), channel_id=1, source_target_pairs={{0,16},{16,0},{1,17},{17,1},{2,18},{18,2},{3,19},{19,3},{4,20},{20... | collective-permute-start | bytes 245768 | tf_op jit(solution)/shard_map/ppermute | solution.py:435
  67.0 0.6 copy-start

commit v6 on v5

--- a/solution.py
+++ b/solution.py
@@ -15,7 +15,7 @@
 PLANE = ("xl", "y", "xh")
 SHIFTS = (63, 32, 16, 8, 4, 2, 1)
 LARGEST = 32767.0
-TAIL = 16
+TAIL = 8
 
 
 def column_of(row):
@@ -134,7 +134,6 @@
     src_rows,
     counts,
     raw,
-    tails,
     factors,
     held,
     total,
@@ -143,52 +142,54 @@
 ):
     lane = lane_ref[0]
     devices, nodes = out_ref.shape[0] // 2, out_ref.shape[2]
-    senders = tails.shape[0]
+    senders = raw.shape[0]
     planes = senders // 2
     slots = own_ref.shape[1] - 8
     pairs = slots // 2
     infos = ((old_own_info, old_other_info), (new_own_info, new_other_info))
 
-    tail_fetch = pltpu.make_async_copy(
-        sent_ref.at[:, pl.ds(2 * nodes, TAIL), pl.ds(0, TILE)], tails, sems.at[2 * senders]
-    )
     fetches = [
-        [
-            pltpu.make_async_copy(
-                sent_ref.at[sender, pl.ds(array * nodes, nodes)],
-                raw.at[array, pl.ds(sender * nodes, nodes)],
-                sems.at[array * senders + sender],
-            )
-            for sender in range(senders)
-        ]
-        for array in range(2)
+        pltpu.make_async_copy(sent_ref.at[sender], raw.at[sender], sems.at[sender])
+        for sender in range(senders)
     ]
-    tail_fetch.start()
-    for copy in fetches[0] + fetches[1]:
+    for copy in fetches:
         copy.start()
 
     def hold(array):
-        powers = [tails[sender, array : array + 1, :] for sender in range(senders)]
-        powers = jnp.concatenate(powers, axis=0).astype(jnp.int32).astype(jnp.float32)
+        first = array * nodes
+        powers = [raw[sender, 2 * nodes :, :TILE][array : array + 1] for sender in range(senders)]
+        powers = [power.astype(jnp.int32).astype(jnp.float32) for power in powers]
         rest = jnp.ones((TILE - senders, TILE), jnp.float32)
-        factor = jnp.concatenate([undone(powers), rest], axis=0).T
+        factor = jnp.concatenate([undone(jnp.concatenate(powers, axis=0)), rest], axis=0).T
         for sender in range(senders):
-            factors[sender * nodes : (sender + 1) * nodes] = jnp.broadcast_to(
+            factors[sender] = jnp.broadcast_to(
                 factor[:nodes, sender : sender + 1], (nodes, TILE)
             )
 
-        def move(begin, into, size):
-            rows = pl.ds(pl.multiple_of(begin, HALF), size)
-            values = raw[array, rows, :].astype(jnp.int32).astype(jnp.float32)
-            times = factors[rows, :]
+        def move(sender, begin, into, size):
+            values = raw[sender, first + begin : first + begin + size, :]
+            values = values.astype(jnp.int32).astype(jnp.float32)
+            times = factors[sender, begin : begin + size, :]
             times = jnp.concatenate([times] * (values.shape[1] // TILE), axis=1)
-            rows = pl.ds(pl.multiple_of(into, HALF), size)
+            rows = pl.ds(pl.multiple_of(into, 16), size)
             held[rows, :] = (values * times).astype(jnp.bfloat16)
 
         def move_plane(plane, carry):
-            begin = plane * 2 * nodes
-            move(begin + lane * HALF, plane * TILE, TILE)
-            move(begin + (1 - lane) * TILE, planes * TILE + plane * HALF, HALF)
+            whole, part = plane * TILE, planes * TILE + plane * HALF
+            one, two = 2 * plane, 2 * plane + 1
+
+            @pl.when(lane == 0)
+            def _():
+                move(one, 0, whole, nodes)
+                move(two, 0, whole + nodes, TILE - nodes)
+                move(two, TILE - nodes, part, HALF)
+
+            @pl.when(lane == 1)
+            def _():
+                move(one, 0, part, HALF)
+                move(one, HALF, whole, nodes - HALF)
+                move(two, 0, whole + nodes - HALF, nodes)
+
             return carry
 
         lax.fori_loop(0, planes, move_plane, 0)
@@ -235,9 +236,10 @@
             dst_hot, src_hot, (((1,), (1,)), ((), ())), preferred_element_type=jnp.float32
         ).astype(jnp.bfloat16)
 
+    def clear(at):
+        counts[at] = jnp.zeros(counts.shape[1:], jnp.bfloat16)
+
     def build(at, info, first, last, unroll):
-        counts[at] = jnp.zeros(counts.shape[1:], jnp.bfloat16)
-
         def add(turn, peak):
             found = [first + turn * unroll + pair for pair in range(unroll)]
             added = [pair_counts(at, pair) for pair in found]
@@ -264,44 +266,54 @@
             pltpu.make_async_copy(
                 total.at[at, pl.ds(device * nodes, nodes)],
                 out_ref.at[where * devices + device, array],
-                sems.at[2 * senders + 1 + at * devices + device],
+                sems.at[senders + at * devices + device],
             )
             for device in range(devices)
         ]
 
-    peaks = []
+    for half in range(2):
+        clear(half)
     for array in range(2):
+        top = jnp.zeros((TILE, TILE), jnp.bfloat16)
         for half, edges in enumerate((own_ref, other_ref)):
             at = 2 * array + half
             live_pairs = plan(at, edges.at[1 - array])
-            peaks.append(build(at, infos[array][half], 0, live_pairs, UNROLL))
-    tail_fetch.wait()
-    for array in range(2):
-        for copy in fetches[array]:
-            copy.wait()
+            top = jnp.maximum(top, build(at, infos[array][half], 0, live_pairs, UNROLL))
+        top = jnp.max(top.astype(jnp.float32))
+        if array == 0:
+            for copy in fetches:
+                copy.wait()
         hold(array)
-        for half in range(2):
-            at = 2 * array + half
-            peak = jnp.max(peaks[at].astype(jnp.float32))
-
-            @pl.when(peak < EXACT)
-            def _(at=at):
+
+        @pl.when(top < EXACT)
+        def _(array=array):
+            for half in range(2):
+                at = 2 * array + half
                 total[at] = product(at).astype(jnp.bfloat16)
-
-            @pl.when(peak >= EXACT)
-            def _(at=at, info=infos[array][half]):
+                if array == 0:
+                    clear(2 + half)
+                for copy in put(array, half):
+                    copy.start()
+
+        @pl.when(top >= EXACT)
+        def _(array=array):
+            for half in range(2):
+                at, info = 2 * array + half, infos[array][half]
                 wide[...] = jnp.zeros_like(wide)
 
-                def some(turn, carry):
+                def some(turn, carry, at=at, info=info):
+                    clear(at)
                     build(at, info, 2 * turn, 2 * turn + 2, 2)
                     wide[...] += product(at)
                     return carry
 
                 lax.fori_loop(0, pairs // 2, some, 0)
                 total[at] = wide[...].astype(jnp.bfloat16)
-
-            for copy in put(array, half):
-                copy.start()
+                if array == 0:
+                    clear(2 + half)
+                for copy in put(array, half):
+                    copy.start()
+
     for array in range(2):
         for half in range(2):
             for copy in put(array, half):
@@ -332,13 +344,12 @@
                 pltpu.VMEM((4, slots // 2, TILE), jnp.float32),
                 pltpu.VMEM((4, slots // 2, TILE), jnp.float32),
                 pltpu.VMEM((4, depth // TILE, rows, TILE), jnp.bfloat16),
-                pltpu.VMEM((2, depth, width), jnp.int16),
-                pltpu.VMEM((senders, TAIL, TILE), jnp.int16),
-                pltpu.VMEM((depth, TILE), jnp.float32),
+                pltpu.VMEM(sent.shape, jnp.int16),
+                pltpu.VMEM((senders, nodes, TILE), jnp.float32),
                 pltpu.VMEM((depth, width), jnp.bfloat16),
                 pltpu.VMEM((4, rows, width), jnp.bfloat16),
                 pltpu.VMEM((rows, width), jnp.float32),
-                pltpu.SemaphoreType.DMA((2 * senders + 1 + 4 * devices,)),
+                pltpu.SemaphoreType.DMA((senders + 4 * devices,)),
             ],
         ),
         compiler_params=pltpu.CompilerParams(vmem_limit_bytes=VMEM),
@@ -359,55 +370,72 @@
     out_ref,
     grad_out_ref,
     parts,
+    features,
+    grad,
+    w_self,
+    w_neigh,
+    own_out,
+    own_grad,
+    mean,
     sems,
 ):
     senders = parts.shape[0]
+    sources = (features_ref, grad_ref, self_ref, neigh_ref)
+    ends = (features, grad, w_self, w_neigh)
     fetches = [
-        pltpu.make_async_copy(parts_ref.at[sender], parts.at[sender], sems.at[sender])
-        for sender in range(senders)
+        pltpu.make_async_copy(source, end, sems.at[at])
+        for at, (source, end) in enumerate(zip(sources, ends))
     ]
-    for copy in fetches:
+    part_fetches = [
+        pltpu.make_async_copy(parts_ref.at[at], parts.at[at], sems.at[len(ends) + at])
+        for at in range(senders)
+    ]
+    for copy in fetches + part_fetches:
         copy.start()
-    own_grad = lax.dot_general(
-        grad_ref[...], self_ref[...], (((1,), (1,)), ((), ())), preferred_element_type=jnp.float32
-    )
-    own_out = jnp.dot(features_ref[...], self_ref[...], preferred_element_type=jnp.float32)
     degree = column_of(degree_ref[...].astype(jnp.float32))
     for copy in fetches:
         copy.wait()
-
-    def summed(array):
-        sums = parts[0, array].astype(jnp.float32)
-        for sender in range(1, senders):
-            sums += parts[sender, array].astype(jnp.float32)
-        return sums
-
-    mean = (summed(1) / degree).astype(jnp.bfloat16)
-    grad_out_ref[...] = (own_grad + summed(0)).astype(jnp.bfloat16)
-    preact = jnp.dot(mean, neigh_ref[...], preferred_element_type=jnp.float32)
-    preact = own_out + preact + bias_ref[...]
+    own_grad[...] = lax.dot_general(
+        grad[...], w_self[...], (((1,), (1,)), ((), ())), preferred_element_type=jnp.float32
+    )
+    own_out[...] = jnp.dot(features[...], w_self[...], preferred_element_type=jnp.float32)
+    for copy in part_fetches:
+        copy.wait()
+    for begin in range(0, features.shape[0], 16):
+        rows = pl.ds(begin, 16)
+
+        def summed(array):
+            return sum(parts[at, array, rows, :].astype(jnp.float32) for at in range(senders))
+
+        mean[rows, :] = (summed(1) / degree[begin : begin + 16]).astype(jnp.bfloat16)
+        grad_out_ref[rows, :] = (own_grad[rows, :] + summed(0)).astype(jnp.bfloat16)
+    preact = jnp.dot(mean[...], w_neigh[...], preferred_element_type=jnp.float32)
+    preact = own_out[...] + preact + bias_ref[...]
     out_ref[...] = jnp.maximum(preact, 0.0).astype(jnp.bfloat16)
 
 
 def finish(parts, features, old_grad, w_self, w_neigh, bias_term, degree):
-    args = (features, old_grad, w_self, w_neigh, bias_term, degree)
     out = jax.ShapeDtypeStruct(features.shape, jnp.bfloat16)
+    far = pl.BlockSpec(memory_space=pl.ANY)
 
     def whole(arg):
         return pl.BlockSpec(arg.shape, lambda _: (0,) * len(arg.shape))
 
+    held = (parts, features, old_grad, w_self, w_neigh)
     return pl.pallas_call(
         finish_kernel,
         out_shape=(out, out),
         grid=(1,),
-        in_specs=[pl.BlockSpec(memory_space=pl.ANY)] + [whole(arg) for arg in args],
+        in_specs=[far] * 5 + [whole(bias_term), whole(degree)],
         out_specs=(whole(out), whole(out)),
-        scratch_shapes=[
-            pltpu.VMEM(parts.shape, jnp.bfloat16),
-            pltpu.SemaphoreType.DMA((parts.shape[0],)),
+        scratch_shapes=[pltpu.VMEM(arg.shape, jnp.bfloat16) for arg in held]
+        + [pltpu.VMEM(features.shape, jnp.float32)] * 2
+        + [
+            pltpu.VMEM(features.shape, jnp.bfloat16),
+            pltpu.SemaphoreType.DMA((4 + parts.shape[0],)),
         ],
         compiler_params=pltpu.CompilerParams(vmem_limit_bytes=VMEM),
-    )(parts, *args)
+    )(parts, features, old_grad, w_self, w_neigh, bias_term, degree)
 
 
 def shards(

time: 143 us -> 141 us (0.986)
  blocking collectives: 108 us -> 105 us
where the time goes in v6:
time: 141 us; the launch traced here: 139 us
  blocking collectives  105 us (74%)
  Pallas kernels  29.4 us (21%)
  starting transfers between devices  2.72 us (2%)
    all_gather x1, blocking collectives, shards(): got = lax.all_gather(sent, ('z', 'core'), axis=0, tiled=False)  60.1 us
    all_to_all x1, blocking collectives, shards(): parts = lax.all_to_all(partial, PLANE, 0, 0)  45.4 us
    pallas_call x1, Pallas kernels, edge_sums(): pl.pallas_call(sums_kernel, out_shape=jax.ShapeDtypeStruct((2 * devices,...  22.7 us
    pallas_call x1, Pallas kernels, finish(): pl.pallas_call(finish_kernel, out_shape=(out, out), grid=(1,), in_specs=[...  4.22 us
  transfers between devices with their start and end apart: 1, of which 0 were waited for; matrix products, arithmetic and copies ran while one was open for 0% of the time, Pallas kernels for 0%

profile of v6, /device:TPU:6, one launch (start us, length us, event | category | flops | bytes accessed | tf_op | source)
XLA Modules:
  0.0 139.0 jit_solution(7965465547706751545)
XLA Ops:
  0.6 2.5 %shard_map.122 = (s16[200,512]{1,0:T(8,128)(2,1)}, s32[2,80,128]{2,1,0:T(8,128)}) custom-call(bf16[96,512]{1,0:T(8,128)(2,1)} %features_ref.3, bf16[96,512]{1,0:T(8,128)(2,1)} %grad_ref.3, bf16[512,512]{1,0:T(8,128)(2,1)} %neigh_ref.1, s32[1,96]{1,0:T(1,128)} %bitcast.24, s32[3,1,72]{2,1,0:T(1,128)} %bitcast.21, s32[64,72]{1,0:T(8,128)} %bitcast.18, ...), custom_call_target="tpu_custom_call" | custom-call | tf_op jit(solution)/shard_map/pallas_call | solution.py:113
  3.1 2.7 %collective-permute-start = (s32[2,80,128]{2,1,0:T(8,128)}, s32[2,80,128]{2,1,0:T(8,128)S(1)}, u32[]{:S(2)}, u32[]{:S(2)}) collective-permute-start(s32[2,80,128]{2,1,0:T(8,128)} %get-tuple-element.4.new_own_info.old_own_info.own_ref), channel_id=1, source_target_pairs={{0,16},{16,0},{1,17},{17,1},{2,18},{18,2},{3,19},{19,3},{4,20},{20... | collective-permute-start | bytes 245768 | tf_op jit(solution)/shard_map/ppermute | solution.py:463
  5.8 60.1 %all-gather.2 = s16[6400,512]{1,0:T(8,128)(2,1)} all-gather(s16[200,512]{1,0:T(8,128)(2,1)} %get-tuple-element.5), channel_id=2, replica_groups=mesh['z'=16,'xl'=2,'core'=2,'y'=4,'xh'=2] {'z','core'}, dimensions={0}, use_global_device_ids=true | all-gather | bytes 6758400 | tf_op jit(solution)/shard_map/all_gather | solution.py:465
  65.9 0.0 collective-permute-done.new_other_info.old_other_info.other_ref
  65.9 0.0 copy-start
  65.9 0.6 copy-done
  66.6 22.7 %shard_map.123 = bf16[16,2,96,512]{3,2,1,0:T(8,128)(2,1)} custom-call(s32[1]{0:T(128)} %bitcast.lane_ref, s32[2,80,128]{2,1,0:T(8,128)} %get-tuple-element.4.new_own_info.old_own_info.own_ref, s32[2,80,128]{2,1,0:T(8,128)} %copy-done, s32[2,80,128]{2,1,0:T(8,128)} %get-tuple-element.4.new_own_info.old_own_info.own_ref, s32[2,80,128]{2,1,0:T(8,128)} %copy-done, ...), custom_call_target="tpu_custom_call" | custom-call | flops 16000000000 | bytes 20000000 | tf_op jit(solution)/shard_map/pallas_call | solution.py:335
  89.3 45.4 %all_to_all.5.parts_ref = bf16[16,2,96,512]{3,2,1,0:T(8,128)(2,1)} all-to-all(bf16[16,2,96,512]{3,2,1,0:T(8,128)(2,1)} %shard_map.123), channel_id=1, replica_groups=mesh['z'=16,'xl'=2,'core'=2,'y'=4,'xh'=2] {'xl','y','xh'}, dimensions={0} | all-to-all | bytes 6291456 | tf_op jit(solution)/shard_map/all_to_all | solution.py:468
  134.6 4.2 %shard_map.124 = (bf16[96,512]{1,0:T(8,128)(2,1)}, bf16[96,512]{1,0:T(8,128)(2,1)}) custom-call(bf16[16,2,96,512]{3,2,1,0:T(8,128)(2,1)} %all_to_all.5.parts_ref, bf16[96,512]{1,0:T(8,128)(2,1)} %features_ref.3, bf16[96,512]{1,0:T(8,128)(2,1)} %grad_ref.3, bf16[512,512]{1,0:T(8,128)(2,1)} %self_ref.1, bf16[512,512]{1,0:T(8,128)(2,1)} %neigh_ref.1, ...), custom_call_target="tpu_custom_call" | custom-call | tf_op jit(solution)/shard_map/pallas_call | solution.py:425
Async XLA Ops:
  3.1 62.8 %collective-permute-start = (s32[2,80,128]{2,1,0:T(8,128)}, s32[2,80,128]{2,1,0:T(8,128)S(1)}, u32[]{:S(2)}, u32[]{:S(2)}) collective-permute-start(s32[2,80,128]{2,1,0:T(8,128)} %get-tuple-element.4.new_own_info.old_own_info.own_ref), channel_id=1, source_target_pairs={{0,16},{16,0},{1,17},{17,1},{2,18},{18,2},{3,19},{19,3},{4,20},{20... | collective-permute-start | bytes 245768 | tf_op jit(solution)/shard_map/ppermute | solution.py:463
  65.9 0.6 copy-start

commit v7 on v6

--- a/solution.py
+++ b/solution.py
@@ -11,6 +11,7 @@
 UNROLL = 12
 EXACT = 256
 VMEM = 58 * 1024 * 1024
+NEAR = 56 * 1024 * 1024
 PARTS = ("z", "xl", "core", "y", "xh")
 PLANE = ("xl", "y", "xh")
 SHIFTS = (63, 32, 16, 8, 4, 2, 1)
@@ -122,21 +123,17 @@
 
 def sums_kernel(
     lane_ref,
-    new_own_info,
-    new_other_info,
-    old_own_info,
-    old_other_info,
     own_ref,
     other_ref,
     sent_ref,
     out_ref,
+    infos,
     dst_rows,
     src_rows,
     counts,
     raw,
     factors,
     held,
-    total,
     wide,
     sems,
 ):
@@ -146,13 +143,18 @@
     planes = senders // 2
     slots = own_ref.shape[1] - 8
     pairs = slots // 2
-    infos = ((old_own_info, old_other_info), (new_own_info, new_other_info))
-
-    fetches = [
-        pltpu.make_async_copy(sent_ref.at[sender], raw.at[sender], sems.at[sender])
-        for sender in range(senders)
+    info_fetches = [
+        pltpu.make_async_copy(
+            table.at[1 - array, pl.ds(slots, 8)],
+            infos.at[2 * array + half],
+            sems.at[2 * array + half],
+        )
+        for array in range(2)
+        for half, table in enumerate((own_ref, other_ref))
     ]
-    for copy in fetches:
+    fetch = pltpu.make_async_copy(sent_ref, raw, sems.at[4])
+    fetch.start()
+    for copy in info_fetches:
         copy.start()
 
     def hold(array):
@@ -221,8 +223,8 @@
     src_ids = lax.broadcasted_iota(jnp.int32, (2 * TILE, TILE), 0).astype(jnp.bfloat16)
     zero, unit = jnp.bfloat16(0), jnp.bfloat16(1)
 
-    def spot(info, slot):
-        row, column = info[0, slot], info[1, slot]
+    def spot(at, slot):
+        row, column = infos[at, 0, slot], infos[at, 1, slot]
         plane = (column * 43) >> 7
         block = jnp.where(column - 3 * plane == 2 * lane, plane, planes + (plane >> 1))
         return block, pl.ds(pl.multiple_of(row * TILE, TILE), TILE)
@@ -239,13 +241,13 @@
     def clear(at):
         counts[at] = jnp.zeros(counts.shape[1:], jnp.bfloat16)
 
-    def build(at, info, first, last, unroll):
+    def build(at, first, last, unroll):
         def add(turn, peak):
             found = [first + turn * unroll + pair for pair in range(unroll)]
             added = [pair_counts(at, pair) for pair in found]
             for pair, both in zip(found, added):
                 for side in range(2):
-                    block, rows = spot(info, 2 * pair + side)
+                    block, rows = spot(at, 2 * pair + side)
                     sums = counts[at, block, rows, :]
                     sums = sums + both[:, side * TILE : (side + 1) * TILE]
                     counts[at, block, rows, :] = sums
@@ -259,148 +261,98 @@
         left_side = jnp.concatenate([counts[at, block] for block in range(counts.shape[1])], axis=1)
         return jnp.dot(left_side, held[...], preferred_element_type=jnp.float32)
 
-    def put(array, half):
+    def put(array, half, sums):
         where = half + lane - 2 * half * lane
-        at = 2 * array + half
-        return [
-            pltpu.make_async_copy(
-                total.at[at, pl.ds(device * nodes, nodes)],
-                out_ref.at[where * devices + device, array],
-                sems.at[senders + at * devices + device],
-            )
-            for device in range(devices)
-        ]
+        for device in range(devices):
+            rows = sums[device * nodes : (device + 1) * nodes]
+            out_ref[where * devices + device, array] = rows.astype(jnp.bfloat16)
 
     for half in range(2):
         clear(half)
+    for copy in info_fetches:
+        copy.wait()
     for array in range(2):
         top = jnp.zeros((TILE, TILE), jnp.bfloat16)
         for half, edges in enumerate((own_ref, other_ref)):
             at = 2 * array + half
             live_pairs = plan(at, edges.at[1 - array])
-            top = jnp.maximum(top, build(at, infos[array][half], 0, live_pairs, UNROLL))
+            top = jnp.maximum(top, build(at, 0, live_pairs, UNROLL))
         top = jnp.max(top.astype(jnp.float32))
         if array == 0:
-            for copy in fetches:
-                copy.wait()
+            fetch.wait()
         hold(array)
 
         @pl.when(top < EXACT)
         def _(array=array):
             for half in range(2):
-                at = 2 * array + half
-                total[at] = product(at).astype(jnp.bfloat16)
+                put(array, half, product(2 * array + half))
                 if array == 0:
                     clear(2 + half)
-                for copy in put(array, half):
-                    copy.start()
 
         @pl.when(top >= EXACT)
         def _(array=array):
             for half in range(2):
-                at, info = 2 * array + half, infos[array][half]
+                at = 2 * array + half
                 wide[...] = jnp.zeros_like(wide)
 
-                def some(turn, carry, at=at, info=info):
+                def some(turn, carry, at=at):
                     clear(at)
-                    build(at, info, 2 * turn, 2 * turn + 2, 2)
+                    build(at, 2 * turn, 2 * turn + 2, 2)
                     wide[...] += product(at)
                     return carry
 
                 lax.fori_loop(0, pairs // 2, some, 0)
-                total[at] = wide[...].astype(jnp.bfloat16)
+                put(array, half, wide[...])
                 if array == 0:
                     clear(2 + half)
-                for copy in put(array, half):
-                    copy.start()
-
-    for array in range(2):
-        for half in range(2):
-            for copy in put(array, half):
-                copy.wait()
 
 
 def edge_sums(lane, own, other, sent, devices, nodes):
     slots = own.shape[1] - 8
     senders, _, width = sent.shape
     depth, rows = senders * nodes, devices * nodes
-    table = pl.BlockSpec(own.shape, lambda _, lane: (0, 0, 0))
-
-    def info(graph):
-        return pl.BlockSpec(
-            (None, 8, TILE), lambda _, lane: (graph, slots // 8, 0), memory_space=pltpu.SMEM
-        )
-
-    far = pl.BlockSpec(memory_space=pl.ANY)
+    near = pl.BlockSpec(memory_space=pltpu.VMEM)
     return pl.pallas_call(
         sums_kernel,
         out_shape=jax.ShapeDtypeStruct((2 * devices, 2, nodes, width), jnp.bfloat16),
-        grid_spec=pltpu.PrefetchScalarGridSpec(
-            num_scalar_prefetch=1,
-            grid=(1,),
-            in_specs=[info(0), info(0), info(1), info(1), table, table, far],
-            out_specs=far,
-            scratch_shapes=[
-                pltpu.VMEM((4, slots // 2, TILE), jnp.float32),
-                pltpu.VMEM((4, slots // 2, TILE), jnp.float32),
-                pltpu.VMEM((4, depth // TILE, rows, TILE), jnp.bfloat16),
-                pltpu.VMEM(sent.shape, jnp.int16),
-                pltpu.VMEM((senders, nodes, TILE), jnp.float32),
-                pltpu.VMEM((depth, width), jnp.bfloat16),
-                pltpu.VMEM((4, rows, width), jnp.bfloat16),
-                pltpu.VMEM((rows, width), jnp.float32),
-                pltpu.SemaphoreType.DMA((senders + 4 * devices,)),
-            ],
-        ),
-        compiler_params=pltpu.CompilerParams(vmem_limit_bytes=VMEM),
+        in_specs=[pl.BlockSpec(memory_space=pltpu.SMEM), near, near, pl.BlockSpec(memory_space=pl.ANY)],
+        out_specs=near,
+        scratch_shapes=[
+            pltpu.SMEM((4, 8, TILE), jnp.int32),
+            pltpu.VMEM((4, slots // 2, TILE), jnp.float32),
+            pltpu.VMEM((4, slots // 2, TILE), jnp.float32),
+            pltpu.VMEM((4, depth // TILE, rows, TILE), jnp.bfloat16),
+            pltpu.VMEM(sent.shape, jnp.int16),
+            pltpu.VMEM((senders, nodes, TILE), jnp.float32),
+            pltpu.VMEM((depth, width), jnp.bfloat16),
+            pltpu.VMEM((rows, width), jnp.float32),
+            pltpu.SemaphoreType.DMA((5,)),
+        ],
+        compiler_params=pltpu.CompilerParams(vmem_limit_bytes=NEAR),
         cost_estimate=pl.CostEstimate(
             flops=16 * 10**9, bytes_accessed=20 * 10**6, transcendentals=0
         ),
-    )(lane, own, other, own, other, own, other, sent)
+    )(lane, own, other, sent)
 
 
 def finish_kernel(
-    parts_ref,
-    features_ref,
-    grad_ref,
-    self_ref,
-    neigh_ref,
-    bias_ref,
-    degree_ref,
-    out_ref,
-    grad_out_ref,
     parts,
     features,
     grad,
     w_self,
     w_neigh,
-    own_out,
+    bias_ref,
+    degree_ref,
+    out_ref,
+    grad_out_ref,
     own_grad,
     mean,
-    sems,
 ):
     senders = parts.shape[0]
-    sources = (features_ref, grad_ref, self_ref, neigh_ref)
-    ends = (features, grad, w_self, w_neigh)
-    fetches = [
-        pltpu.make_async_copy(source, end, sems.at[at])
-        for at, (source, end) in enumerate(zip(sources, ends))
-    ]
-    part_fetches = [
-        pltpu.make_async_copy(parts_ref.at[at], parts.at[at], sems.at[len(ends) + at])
-        for at in range(senders)
-    ]
-    for copy in fetches + part_fetches:
-        copy.start()
     degree = column_of(degree_ref[...].astype(jnp.float32))
-    for copy in fetches:
-        copy.wait()
     own_grad[...] = lax.dot_general(
         grad[...], w_self[...], (((1,), (1,)), ((), ())), preferred_element_type=jnp.float32
     )
-    own_out[...] = jnp.dot(features[...], w_self[...], preferred_element_type=jnp.float32)
-    for copy in part_fetches:
-        copy.wait()
     for begin in range(0, features.shape[0], 16):
         rows = pl.ds(begin, 16)
 
@@ -409,32 +361,21 @@
 
         mean[rows, :] = (summed(1) / degree[begin : begin + 16]).astype(jnp.bfloat16)
         grad_out_ref[rows, :] = (own_grad[rows, :] + summed(0)).astype(jnp.bfloat16)
-    preact = jnp.dot(mean[...], w_neigh[...], preferred_element_type=jnp.float32)
-    preact = own_out[...] + preact + bias_ref[...]
-    out_ref[...] = jnp.maximum(preact, 0.0).astype(jnp.bfloat16)
+    preact = jnp.dot(features[...], w_self[...], preferred_element_type=jnp.float32)
+    preact = preact + jnp.dot(mean[...], w_neigh[...], preferred_element_type=jnp.float32)
+    out_ref[...] = jnp.maximum(preact + bias_ref[...], 0.0).astype(jnp.bfloat16)
 
 
 def finish(parts, features, old_grad, w_self, w_neigh, bias_term, degree):
     out = jax.ShapeDtypeStruct(features.shape, jnp.bfloat16)
-    far = pl.BlockSpec(memory_space=pl.ANY)
-
-    def whole(arg):
-        return pl.BlockSpec(arg.shape, lambda _: (0,) * len(arg.shape))
-
-    held = (parts, features, old_grad, w_self, w_neigh)
     return pl.pallas_call(
         finish_kernel,
         out_shape=(out, out),
-        grid=(1,),
-        in_specs=[far] * 5 + [whole(bias_term), whole(degree)],
-        out_specs=(whole(out), whole(out)),
-        scratch_shapes=[pltpu.VMEM(arg.shape, jnp.bfloat16) for arg in held]
-        + [pltpu.VMEM(features.shape, jnp.float32)] * 2
-        + [
+        scratch_shapes=[
+            pltpu.VMEM(features.shape, jnp.float32),
             pltpu.VMEM(features.shape, jnp.bfloat16),
-            pltpu.SemaphoreType.DMA((4 + parts.shape[0],)),
         ],
-        compiler_params=pltpu.CompilerParams(vmem_limit_bytes=VMEM),
+        compiler_params=pltpu.CompilerParams(vmem_limit_bytes=16 * 1024 * 1024),
     )(parts, features, old_grad, w_self, w_neigh, bias_term, degree)
 
 

time: 141 us -> 138 us (0.979)
  Pallas kernels: 29.4 us -> 27.5 us
    pallas_call x1, Pallas kernels: 4.22 us -> 1.28 us  [finish(): pl.pallas_call(finish_kernel, out_shape=(out, out), scratch_shapes=[pltpu...]
where the time goes in v7:
time: 138 us; the launch traced here: 137 us
  blocking collectives  105 us (76%)
  Pallas kernels  27.5 us (20%)
  starting transfers between devices  2.72 us (2%)
    all_gather x1, blocking collectives, shards(): got = lax.all_gather(sent, ('z', 'core'), axis=0, tiled=False)  60.1 us
    all_to_all x1, blocking collectives, shards(): parts = lax.all_to_all(partial, PLANE, 0, 0)  45.3 us
    pallas_call x1, Pallas kernels, edge_sums(): pl.pallas_call(sums_kernel, out_shape=jax.ShapeDtypeStruct((2 * devices,...  23.8 us
  transfers between devices with their start and end apart: 1, of which 0 were waited for; matrix products, arithmetic and copies ran while one was open for 0% of the time, Pallas kernels for 0%

profile of v7, /device:TPU:6, one launch (start us, length us, event | category | flops | bytes accessed | tf_op | source)
XLA Modules:
  0.0 137.1 jit_solution(5131979337823000559)
XLA Ops:
  0.6 2.5 %shard_map.122 = (s16[200,512]{1,0:T(8,128)(2,1)}, s32[2,80,128]{2,1,0:T(8,128)}) custom-call(bf16[96,512]{1,0:T(8,128)(2,1)} %features.1, bf16[96,512]{1,0:T(8,128)(2,1)} %grad.1, bf16[512,512]{1,0:T(8,128)(2,1)} %w_neigh.1, s32[1,96]{1,0:T(1,128)} %bitcast.24, s32[3,1,72]{2,1,0:T(1,128)} %bitcast.22, s32[64,72]{1,0:T(8,128)} %bitcast.20, ...), custom_call_target="tpu_custom_call" | custom-call | tf_op jit(solution)/shard_map/pallas_call | solution.py:114
  3.1 2.7 %collective-permute-start = (s32[2,80,128]{2,1,0:T(8,128)}, s32[2,80,128]{2,1,0:T(8,128)S(1)}, u32[]{:S(2)}, u32[]{:S(2)}) collective-permute-start(s32[2,80,128]{2,1,0:T(8,128)} %get-tuple-element.4.own_ref), channel_id=1, source_target_pairs={{0,16},{16,0},{1,17},{17,1},{2,18},{18,2},{3,19},{19,3},{4,20},{20... | collective-permute-start | bytes 245768 | tf_op jit(solution)/shard_map/ppermute | solution.py:404
  5.8 60.1 %all-gather.2 = s16[6400,512]{1,0:T(8,128)(2,1)} all-gather(s16[200,512]{1,0:T(8,128)(2,1)} %get-tuple-element.5), channel_id=2, replica_groups=mesh['z'=16,'xl'=2,'core'=2,'y'=4,'xh'=2] {'z','core'}, dimensions={0}, use_global_device_ids=true | all-gather | bytes 6758400 | tf_op jit(solution)/shard_map/all_gather | solution.py:406
  65.9 0.0 collective-permute-done.other_ref
  65.9 0.0 copy-start.6
  65.9 0.6 copy-done.6
  66.6 23.8 %shard_map.123 = bf16[16,2,96,512]{3,2,1,0:T(8,128)(2,1)} custom-call(s32[1]{0:T(128)} %bitcast.lane_ref, s32[2,80,128]{2,1,0:T(8,128)} %get-tuple-element.4.own_ref, s32[2,80,128]{2,1,0:T(8,128)} %copy-done.6, s16[32,200,512]{2,1,0:T(8,128)(2,1)} %bitcast.19), custom_call_target="tpu_custom_call" | custom-call | flops 16000000000 | bytes 20000000 | tf_op jit(solution)/shard_map/pallas_call | solution.py:315
  90.3 0.0 copy-start
  90.4 0.0 copy-start.1
  90.4 0.0 copy-start.2
  90.4 0.0 copy-start.3
  90.4 0.0 copy-start.4
  90.4 0.0 copy-start.5
  90.4 45.3 %all_to_all.5.parts = bf16[16,2,96,512]{3,2,1,0:T(8,128)(2,1)S(1)} all-to-all(bf16[16,2,96,512]{3,2,1,0:T(8,128)(2,1)} %shard_map.123), channel_id=1, replica_groups=mesh['z'=16,'xl'=2,'core'=2,'y'=4,'xh'=2] {'xl','y','xh'}, dimensions={0} | all-to-all | bytes 6291456 | tf_op jit(solution)/shard_map/all_to_all | solution.py:409
  135.7 0.0 copy-done
  135.7 0.0 copy-done.1
  135.7 0.0 copy-done.2
  135.7 0.0 copy-done.3
  135.7 0.0 copy-done.4
  135.8 0.0 copy-done.5
  135.8 1.3 shard_map.124
Async XLA Ops:
  3.1 62.8 %collective-permute-start = (s32[2,80,128]{2,1,0:T(8,128)}, s32[2,80,128]{2,1,0:T(8,128)S(1)}, u32[]{:S(2)}, u32[]{:S(2)}) collective-permute-start(s32[2,80,128]{2,1,0:T(8,128)} %get-tuple-element.4.own_ref), channel_id=1, source_target_pairs={{0,16},{16,0},{1,17},{17,1},{2,18},{18,2},{3,19},{19,3},{4,20},{20... | collective-permute-start | bytes 245768 | tf_op jit(solution)/shard_map/ppermute | solution.py:404
  65.9 0.6 copy-start.6
  90.3 45.4 %copy-start = (bf16[512,512]{1,0:T(8,128)(2,1)S(1)}, bf16[512,512]{1,0:T(8,128)(2,1)}, u32[]{:S(2)}) copy-start(bf16[512,512]{1,0:T(8,128)(2,1)} %w_neigh.1) | copy-start | bytes 1572868
  90.4 45.4 %copy-start.1 = (bf16[512,512]{1,0:T(8,128)(2,1)S(1)}, bf16[512,512]{1,0:T(8,128)(2,1)}, u32[]{:S(2)}) copy-start(bf16[512,512]{1,0:T(8,128)(2,1)} %w_self.1) | copy-start | bytes 1572868
  90.4 45.4 %copy-start.2 = (bf16[96,512]{1,0:T(8,128)(2,1)S(1)}, bf16[96,512]{1,0:T(8,128)(2,1)}, u32[]{:S(2)}) copy-start(bf16[96,512]{1,0:T(8,128)(2,1)} %features.1) | copy-start | bytes 294916
  90.4 45.4 %copy-start.3 = (bf16[96,512]{1,0:T(8,128)(2,1)S(1)}, bf16[96,512]{1,0:T(8,128)(2,1)}, u32[]{:S(2)}) copy-start(bf16[96,512]{1,0:T(8,128)(2,1)} %grad.1) | copy-start | bytes 294916
  90.4 45.4 %copy-start.4 = (f32[512]{0:T(512)S(1)}, f32[512]{0:T(512)}, u32[]{:S(2)}) copy-start(f32[512]{0:T(512)} %param.15) | copy-start | bytes 6148
  90.4 45.4 %copy-start.5 = (s32[96]{0:T(128)S(1)}, s32[96]{0:T(128)}, u32[]{:S(2)}) copy-start(s32[96]{0:T(128)} %param.12) | copy-start | bytes 1156

commit v8 on v7

--- a/solution.py
+++ b/solution.py
@@ -11,7 +11,7 @@
 UNROLL = 12
 EXACT = 256
 VMEM = 58 * 1024 * 1024
-NEAR = 56 * 1024 * 1024
+NEAR = 52 * 1024 * 1024
 PARTS = ("z", "xl", "core", "y", "xh")
 PLANE = ("xl", "y", "xh")
 SHIFTS = (63, 32, 16, 8, 4, 2, 1)
@@ -153,8 +153,7 @@
         for half, table in enumerate((own_ref, other_ref))
     ]
     fetch = pltpu.make_async_copy(sent_ref, raw, sems.at[4])
-    fetch.start()
-    for copy in info_fetches:
+    for copy in info_fetches + [fetch]:
         copy.start()
 
     def hold(array):

time: 138 us -> 137 us (level)
  the two profiles are of different devices: /device:TPU:6 before, /device:TPU:32 now
where the time goes in v8:
time: 137 us; the launch traced here: 138 us
  blocking collectives  107 us (78%)
  Pallas kernels  26.1 us (19%)
  starting transfers between devices  3.39 us (2%)
    all_gather x1, blocking collectives, shards(): got = lax.all_gather(sent, ('z', 'core'), axis=0, tiled=False)  59.2 us
    all_to_all x1, blocking collectives, shards(): parts = lax.all_to_all(partial, PLANE, 0, 0)  48.2 us
    pallas_call x1, Pallas kernels, edge_sums(): pl.pallas_call(sums_kernel, out_shape=jax.ShapeDtypeStruct((2 * devices,...  22.4 us
    ppermute x1, starting transfers between devices, shards(): other = lax.ppermute(own, 'xl', [(0, 1), (1, 0)])  3.39 us
  transfers between devices with their start and end apart: 1, of which 0 were waited for; matrix products, arithmetic and copies ran while one was open for 0% of the time, Pallas kernels for 0%

profile of v8, /device:TPU:32, one launch (start us, length us, event | category | flops | bytes accessed | tf_op | source)
XLA Modules:
  0.0 137.7 jit_solution(17477066059456863214)
XLA Ops:
  0.6 2.5 %shard_map.122 = (s16[200,512]{1,0:T(8,128)(2,1)}, s32[2,80,128]{2,1,0:T(8,128)}) custom-call(bf16[96,512]{1,0:T(8,128)(2,1)} %features.1, bf16[96,512]{1,0:T(8,128)(2,1)} %grad.1, bf16[512,512]{1,0:T(8,128)(2,1)} %w_neigh.1, s32[1,96]{1,0:T(1,128)} %bitcast.24, s32[3,1,72]{2,1,0:T(1,128)} %bitcast.22, s32[64,72]{1,0:T(8,128)} %bitcast.20, ...), custom_call_target="tpu_custom_call" | custom-call | tf_op jit(solution)/shard_map/pallas_call | solution.py:114
  3.1 3.4 %collective-permute-start = (s32[2,80,128]{2,1,0:T(8,128)}, s32[2,80,128]{2,1,0:T(8,128)S(1)}, u32[]{:S(2)}, u32[]{:S(2)}) collective-permute-start(s32[2,80,128]{2,1,0:T(8,128)} %get-tuple-element.4.own_ref), channel_id=1, source_target_pairs={{0,16},{16,0},{1,17},{17,1},{2,18},{18,2},{3,19},{19,3},{4,20},{20... | collective-permute-start | bytes 245768 | tf_op jit(solution)/shard_map/ppermute | solution.py:403
  6.5 0.0 copy-start.6
  6.5 59.2 %all-gather.2 = s16[6400,512]{1,0:T(8,128)(2,1)} all-gather(s16[200,512]{1,0:T(8,128)(2,1)} %get-tuple-element.5), channel_id=2, replica_groups=mesh['z'=16,'xl'=2,'core'=2,'y'=4,'xh'=2] {'z','core'}, dimensions={0}, use_global_device_ids=true | all-gather | bytes 6758400 | tf_op jit(solution)/shard_map/all_gather | solution.py:405
  65.7 0.0 collective-permute-done.other_ref
  65.7 0.0 copy-done.6
  65.7 22.4 %shard_map.123 = bf16[16,2,96,512]{3,2,1,0:T(8,128)(2,1)} custom-call(s32[1]{0:T(128)} %bitcast.lane_ref, s32[2,80,128]{2,1,0:T(8,128)S(1)} %copy-done.6, s32[2,80,128]{2,1,0:T(8,128)S(1)} %collective-permute-done.other_ref, s16[32,200,512]{2,1,0:T(8,128)(2,1)} %bitcast.19), custom_call_target="tpu_custom_call" | custom-call | flops 16000000000 | bytes 20000000 | tf_op jit(solution)/shard_map/pallas_call | solution.py:314
  88.1 0.0 copy-start
  88.1 0.0 copy-start.1
  88.1 0.0 copy-start.2
  88.1 0.0 copy-start.3
  88.1 0.0 copy-start.4
  88.1 0.0 copy-start.5
  88.2 48.2 %all_to_all.5.parts = bf16[16,2,96,512]{3,2,1,0:T(8,128)(2,1)S(1)} all-to-all(bf16[16,2,96,512]{3,2,1,0:T(8,128)(2,1)} %shard_map.123), channel_id=1, replica_groups=mesh['z'=16,'xl'=2,'core'=2,'y'=4,'xh'=2] {'xl','y','xh'}, dimensions={0} | all-to-all | bytes 6291456 | tf_op jit(solution)/shard_map/all_to_all | solution.py:408
  136.3 0.0 copy-done
  136.4 0.0 copy-done.1
  136.4 0.0 copy-done.2
  136.4 0.0 copy-done.3
  136.4 0.0 copy-done.4
  136.4 0.0 copy-done.5
  136.4 1.3 shard_map.124
Async XLA Ops:
  3.1 62.6 %collective-permute-start = (s32[2,80,128]{2,1,0:T(8,128)}, s32[2,80,128]{2,1,0:T(8,128)S(1)}, u32[]{:S(2)}, u32[]{:S(2)}) collective-permute-start(s32[2,80,128]{2,1,0:T(8,128)} %get-tuple-element.4.own_ref), channel_id=1, source_target_pairs={{0,16},{16,0},{1,17},{17,1},{2,18},{18,2},{3,19},{19,3},{4,20},{20... | collective-permute-start | bytes 245768 | tf_op jit(solution)/shard_map/ppermute | solution.py:403
  6.5 59.2 %copy-start.6 = (s32[2,80,128]{2,1,0:T(8,128)S(1)}, s32[2,80,128]{2,1,0:T(8,128)}, u32[]{:S(2)}) copy-start(s32[2,80,128]{2,1,0:T(8,128)} %get-tuple-element.4.own_ref) | copy-start | bytes 245764
  88.1 48.3 %copy-start = (bf16[512,512]{1,0:T(8,128)(2,1)S(1)}, bf16[512,512]{1,0:T(8,128)(2,1)}, u32[]{:S(2)}) copy-start(bf16[512,512]{1,0:T(8,128)(2,1)} %w_neigh.1) | copy-start | bytes 1572868
  88.1 48.3 %copy-start.1 = (bf16[512,512]{1,0:T(8,128)(2,1)S(1)}, bf16[512,512]{1,0:T(8,128)(2,1)}, u32[]{:S(2)}) copy-start(bf16[512,512]{1,0:T(8,128)(2,1)} %w_self.1) | copy-start | bytes 1572868
  88.1 48.2 %copy-start.2 = (bf16[96,512]{1,0:T(8,128)(2,1)S(1)}, bf16[96,512]{1,0:T(8,128)(2,1)}, u32[]{:S(2)}) copy-start(bf16[96,512]{1,0:T(8,128)(2,1)} %features.1) | copy-start | bytes 294916
  88.1 48.2 %copy-start.3 = (bf16[96,512]{1,0:T(8,128)(2,1)S(1)}, bf16[96,512]{1,0:T(8,128)(2,1)}, u32[]{:S(2)}) copy-start(bf16[96,512]{1,0:T(8,128)(2,1)} %grad.1) | copy-start | bytes 294916
  88.1 48.2 %copy-start.4 = (f32[512]{0:T(512)S(1)}, f32[512]{0:T(512)}, u32[]{:S(2)}) copy-start(f32[512]{0:T(512)} %param.15) | copy-start | bytes 6148
  88.1 48.2 %copy-start.5 = (s32[96]{0:T(128)S(1)}, s32[96]{0:T(128)}, u32[]{:S(2)}) copy-start(s32[96]{0:T(128)} %param.12) | copy-start | bytes 1156

commit v9 on v8

--- a/solution.py
+++ b/solution.py
@@ -16,7 +16,7 @@
 PLANE = ("xl", "y", "xh")
 SHIFTS = (63, 32, 16, 8, 4, 2, 1)
 LARGEST = 32767.0
-TAIL = 8
+TAIL = 16
 
 
 def column_of(row):

time: 137 us -> 137 us (level)
  the two profiles are of different devices: /device:TPU:32 before, /device:TPU:6 now
where the time goes in v9:
time: 137 us; the launch traced here: 136 us
  blocking collectives  108 us (79%)
  Pallas kernels  25.1 us (18%)
  starting transfers between devices  2.72 us (2%)
    all_gather x1, blocking collectives, shards(): got = lax.all_gather(sent, ('z', 'core'), axis=0, tiled=False)  61.1 us
    all_to_all x1, blocking collectives, shards(): parts = lax.all_to_all(partial, PLANE, 0, 0)  46.5 us
    pallas_call x1, Pallas kernels, edge_sums(): pl.pallas_call(sums_kernel, out_shape=jax.ShapeDtypeStruct((2 * devices,...  21.3 us
  transfers between devices with their start and end apart: 1, of which 0 were waited for; matrix products, arithmetic and copies ran while one was open for 0% of the time, Pallas kernels for 0%

profile of v9, /device:TPU:6, one launch (start us, length us, event | category | flops | bytes accessed | tf_op | source)
XLA Modules:
  0.0 136.2 jit_solution(12385673091520642471)
XLA Ops:
  0.6 2.5 %shard_map.122 = (s16[208,512]{1,0:T(8,128)(2,1)}, s32[2,80,128]{2,1,0:T(8,128)}) custom-call(bf16[96,512]{1,0:T(8,128)(2,1)} %features.1, bf16[96,512]{1,0:T(8,128)(2,1)} %grad.1, bf16[512,512]{1,0:T(8,128)(2,1)} %w_neigh.1, s32[1,96]{1,0:T(1,128)} %bitcast.24, s32[3,1,72]{2,1,0:T(1,128)} %bitcast.22, s32[64,72]{1,0:T(8,128)} %bitcast.20, ...), custom_call_target="tpu_custom_call" | custom-call | tf_op jit(solution)/shard_map/pallas_call | solution.py:114
  3.1 2.7 %collective-permute-start = (s32[2,80,128]{2,1,0:T(8,128)}, s32[2,80,128]{2,1,0:T(8,128)S(1)}, u32[]{:S(2)}, u32[]{:S(2)}) collective-permute-start(s32[2,80,128]{2,1,0:T(8,128)} %get-tuple-element.4.own_ref), channel_id=1, source_target_pairs={{0,16},{16,0},{1,17},{17,1},{2,18},{18,2},{3,19},{19,3},{4,20},{20... | collective-permute-start | bytes 245768 | tf_op jit(solution)/shard_map/ppermute | solution.py:403
  5.8 0.0 copy-start.6
  5.8 61.1 %all-gather.2 = s16[6656,512]{1,0:T(8,128)(2,1)} all-gather(s16[208,512]{1,0:T(8,128)(2,1)} %get-tuple-element.5), channel_id=2, replica_groups=mesh['z'=16,'xl'=2,'core'=2,'y'=4,'xh'=2] {'z','core'}, dimensions={0}, use_global_device_ids=true | all-gather | bytes 7028736 | tf_op jit(solution)/shard_map/all_gather | solution.py:405
  67.0 0.0 collective-permute-done.other_ref
  67.0 0.0 copy-done.6
  67.0 21.3 %shard_map.123 = bf16[16,2,96,512]{3,2,1,0:T(8,128)(2,1)} custom-call(s32[1]{0:T(128)} %bitcast.lane_ref, s32[2,80,128]{2,1,0:T(8,128)S(1)} %copy-done.6, s32[2,80,128]{2,1,0:T(8,128)S(1)} %collective-permute-done.other_ref, s16[32,208,512]{2,1,0:T(8,128)(2,1)} %bitcast.19), custom_call_target="tpu_custom_call" | custom-call | flops 16000000000 | bytes 20000000 | tf_op jit(solution)/shard_map/pallas_call | solution.py:314
  88.3 0.0 copy-start
  88.3 0.0 copy-start.1
  88.3 0.0 copy-start.2
  88.3 0.0 copy-start.3
  88.3 0.0 copy-start.4
  88.4 0.0 copy-start.5
  88.4 46.5 %all_to_all.5.parts = bf16[16,2,96,512]{3,2,1,0:T(8,128)(2,1)S(1)} all-to-all(bf16[16,2,96,512]{3,2,1,0:T(8,128)(2,1)} %shard_map.123), channel_id=1, replica_groups=mesh['z'=16,'xl'=2,'core'=2,'y'=4,'xh'=2] {'xl','y','xh'}, dimensions={0} | all-to-all | bytes 6291456 | tf_op jit(solution)/shard_map/all_to_all | solution.py:408
  134.9 0.0 copy-done
  134.9 0.0 copy-done.1
  134.9 0.0 copy-done.2
  134.9 0.0 copy-done.3
  134.9 0.0 copy-done.4
  134.9 0.0 copy-done.5
  134.9 1.3 shard_map.124
Async XLA Ops:
  3.1 63.9 %collective-permute-start = (s32[2,80,128]{2,1,0:T(8,128)}, s32[2,80,128]{2,1,0:T(8,128)S(1)}, u32[]{:S(2)}, u32[]{:S(2)}) collective-permute-start(s32[2,80,128]{2,1,0:T(8,128)} %get-tuple-element.4.own_ref), channel_id=1, source_target_pairs={{0,16},{16,0},{1,17},{17,1},{2,18},{18,2},{3,19},{19,3},{4,20},{20... | collective-permute-start | bytes 245768 | tf_op jit(solution)/shard_map/ppermute | solution.py:403
  5.8 61.2 %copy-start.6 = (s32[2,80,128]{2,1,0:T(8,128)S(1)}, s32[2,80,128]{2,1,0:T(8,128)}, u32[]{:S(2)}) copy-start(s32[2,80,128]{2,1,0:T(8,128)} %get-tuple-element.4.own_ref) | copy-start | bytes 245764
  88.3 46.6 %copy-start = (bf16[512,512]{1,0:T(8,128)(2,1)S(1)}, bf16[512,512]{1,0:T(8,128)(2,1)}, u32[]{:S(2)}) copy-start(bf16[512,512]{1,0:T(8,128)(2,1)} %w_neigh.1) | copy-start | bytes 1572868
  88.3 46.6 %copy-start.1 = (bf16[512,512]{1,0:T(8,128)(2,1)S(1)}, bf16[512,512]{1,0:T(8,128)(2,1)}, u32[]{:S(2)}) copy-start(bf16[512,512]{1,0:T(8,128)(2,1)} %w_self.1) | copy-start | bytes 1572868
  88.3 46.6 %copy-start.2 = (bf16[96,512]{1,0:T(8,128)(2,1)S(1)}, bf16[96,512]{1,0:T(8,128)(2,1)}, u32[]{:S(2)}) copy-start(bf16[96,512]{1,0:T(8,128)(2,1)} %features.1) | copy-start | bytes 294916
  88.3 46.6 %copy-start.3 = (bf16[96,512]{1,0:T(8,128)(2,1)S(1)}, bf16[96,512]{1,0:T(8,128)(2,1)}, u32[]{:S(2)}) copy-start(bf16[96,512]{1,0:T(8,128)(2,1)} %grad.1) | copy-start | bytes 294916
  88.3 46.5 %copy-start.4 = (f32[512]{0:T(512)S(1)}, f32[512]{0:T(512)}, u32[]{:S(2)}) copy-start(f32[512]{0:T(512)} %param.15) | copy-start | bytes 6148
  88.4 46.5 %copy-start.5 = (s32[96]{0:T(128)S(1)}, s32[96]{0:T(128)}, u32[]{:S(2)}) copy-start(s32[96]{0:T(128)} %param.12) | copy-start | bytes 1156
